TPU v7x, 128 devices: a whole 4x4x4 slice. The times are simulated.
128 devices in a mesh: freq: 4 (over y), blk: 32 (over x, z, core).
Axes of the slice: x: 4, y: 4, z: 4, core: 2. Of those that a mesh axis runs over, the one named last changes fastest.
Arguments:
- voltages: float32 [32, 32, 2, 128, 256], P('blk', None, None, 'freq'), may hold values from -6 to 6
- pair_table: int32 [544, 2], P('blk'), may hold values from 0 to 31, as said below
- bad_feeds: int32 [64], replicated, may hold values from 0 to 2047
Outputs:
- visibilities: float32 [544, 32, 2, 128, 128], P('blk', 'freq')
Inputs may be any that keep to these rules, and one draw needn't show every extreme that they name: `pair_table`: device k of blk holds blocks k * 1 to k + 1 - 1 and tiles k * 17 to k * 17 + 16. Of its tiles, the first 1 (2) / 2 name two of its own blocks; then for d = 1 to 15 in turn, 1 tiles each name one own block and one block of device k + d; the last (2) / 2 name one own block and one block of device k + 16; device numbers are taken modulo 32, and either block of a tile may come first. Every unordered pair of blocks is named at least once.
All inputs are finite; a program needn't handle non-finite values.
Results may differ from a plain program's by a relative error of at most 0.000098.
Values sent between devices are 32-bit elements; how exact they have to be, the bound alone decides.
No kernel may reach another device: no remote copies, remote signals or barrier semaphores. Data moves between devices by JAX's collectives and lax.ppermute only.
A program may use at most 128 MiB of HBM per device.

v0:
```python
import jax
import jax.numpy as jnp
from jax import lax
from jax.sharding import PartitionSpec as P


def passed_along(value, axis, steps):
    count = lax.axis_size(axis)
    pairs = [(source, (source + steps) % count) for source in range(count)]
    return lax.ppermute(value, axis, pairs)


def correlate(left, right):
    scale = 1.0 / left.shape[-1]
    prec = lax.Precision.HIGHEST
    left_re = left[:, :, 0]
    left_im = left[:, :, 1]
    stacked = jnp.stack([jnp.stack([left_re, left_im], 2), jnp.stack([left_im, -left_re], 2)], 2)
    return jnp.einsum("gcokps,gckqs->gcopq", stacked, right, precision=prec) * scale


def shards(voltages, pair_table, bad_feeds):
    blk_count = lax.axis_size("blk")
    moved = lax.all_to_all(voltages, "freq", split_axis=1, concat_axis=3, tiled=True)
    per_dev, chan_dev, _, width, samples = moved.shape
    here = lax.axis_index("blk")
    inputs = (here * per_dev + jnp.arange(per_dev, dtype=jnp.int32))[:, None] * width + jnp.arange(
        width, dtype=jnp.int32
    )[None, :]
    flagged = jnp.any((inputs // 2)[:, :, None] == bad_feeds[None, None, :], axis=-1)
    keep = jnp.where(flagged, 0.0, 1.0).astype(jnp.float32)
    own_blocks = moved * keep[:, None, None, :, None]
    tile_count = per_dev * per_dev
    own_count = per_dev * (per_dev + 1) // 2
    shared_count = (tile_count + 1) // 2
    half = blk_count // 2
    sign = jnp.array([1.0, -1.0], jnp.float32)[:, None, None]

    def correlate_group(pair_rows, far_blocks):
        swapped = pair_rows[:, 0] // per_dev != here
        own_local = jnp.where(swapped, pair_rows[:, 1], pair_rows[:, 0]) % per_dev
        far_local = jnp.where(swapped, pair_rows[:, 0], pair_rows[:, 1]) % per_dev
        tile = correlate(
            jnp.take(own_blocks, own_local, axis=0), jnp.take(far_blocks, far_local, axis=0)
        )
        flipped = jnp.swapaxes(tile, -1, -2) * sign
        return jnp.where(swapped[:, None, None, None, None], flipped, tile)

    def place_group(visibility, start, count, far_blocks):
        pair_rows = lax.dynamic_slice_in_dim(pair_table, start, count, 0)
        return lax.dynamic_update_slice_in_dim(
            visibility, correlate_group(pair_rows, far_blocks), start, 0
        )

    visibility = jnp.zeros((pair_table.shape[0], chan_dev, 2, width, width), jnp.float32)
    visibility = place_group(visibility, 0, own_count, own_blocks)

    def advance(buffer):
        return passed_along(buffer, "blk", -1)

    def forward_chain(step, carry):
        buffer, visibility = carry
        buffer = advance(buffer)
        return (
            buffer,
            place_group(visibility, own_count + (step - 1) * tile_count, tile_count, buffer),
        )

    buffer, visibility = lax.fori_loop(1, half, forward_chain, (own_blocks, visibility))
    buffer = advance(buffer)
    visibility = place_group(visibility, own_count + (half - 1) * tile_count, shared_count, buffer)
    return visibility


def solution(mesh):
    placed = (P("blk", None, None, "freq", None), P("blk", None), P())
    return jax.shard_map(
        shards,
        mesh=mesh,
        in_specs=placed,
        out_specs=P("blk", "freq", None, None, None),
        check_vma=False,
    )
```

profile of v0, /device:TPU:0, one launch (start us, length us, event | category | flops | bytes accessed | tf_op | source)
XLA Modules:
  0.0 688.2 jit_solution(14216579928049349435)
XLA Ops:
  6.1 25.0 %all-to-all-done = f32[1,32,2,32,256]{4,3,2,0,1:T(8,128)S(1)} async-done(((f32[1,32,2,32,256]{4,3,2,0,1:T(8,128)}), f32[1,32,2,32,256]{4,3,2,0,1:T(8,128)S(1)}, u32[]{:S(2)}, u32[]{:S(2)}) %all-to-all-start) | async-done | bytes 2097184 | tf_op jit(solution)/shard_map/all_to_all | solution.py:24
  49.0 8.8 %dynamic_update_slice.19 = f32[17,8,2,128,128]{4,3,2,1,0:T(8,128)} pad(f32[1,8,2,128,128]{4,3,2,1,0:T(8,128)S(1)} %bitcast_select_fusion.2, f32[]{:T(128)} %constant.321.clone.1), padding=0_16x0_0x0_0x0_0x0_0 | pad | bytes 18874372 | tf_op jit(solution)/shard_map/dynamic_update_slice | solution.py:51
  57.8 594.4 %while.21 = (s32[]{:T(128)}, f32[1,8,2,128,256]{4,3,2,1,0:T(8,128)}, f32[17,8,2,128,128]{4,3,2,1,0:T(8,128)}, s32[17,2]{0,1:T(2,128)S(1)}, s32[]{:T(128)}, /*ind...) while((s32[]{:T(128)}, ...), condition=%wide.wide.region_2.3_spmd.clone, body=%wide.wide.region_1.2_spmd.sunk.clone.sunk | while | flops 1611399168 | bytes 25166584 | solution.py:69
  63.5 22.6 %collective-permute-done = f32[1,8,2,128,256]{4,3,2,1,0:T(8,128)S(1)} collective-permute-done((f32[1,8,2,128,256]{4,3,2,1,0:T(8,128)}, f32[1,8,2,128,256]{4,3,2,1,0:T(8,128)S(1)}, u32[]{:S(2)}, u32[]{:S(2)}) %collective-permute-start) | collective-permute-done | bytes 2097184 | tf_op jit(solution)/shard_map/while/body/eval_jaxpr/ppermute | solution.py:10
  86.1 5.5 fusion.55
  103.1 22.6 %collective-permute-done = f32[1,8,2,128,256]{4,3,2,1,0:T(8,128)S(1)} collective-permute-done((f32[1,8,2,128,256]{4,3,2,1,0:T(8,128)}, f32[1,8,2,128,256]{4,3,2,1,0:T(8,128)S(1)}, u32[]{:S(2)}, u32[]{:S(2)}) %collective-permute-start) | collective-permute-done | bytes 2097184 | tf_op jit(solution)/shard_map/while/body/eval_jaxpr/ppermute | solution.py:10
  125.8 5.5 fusion.55
  142.8 22.6 %collective-permute-done = f32[1,8,2,128,256]{4,3,2,1,0:T(8,128)S(1)} collective-permute-done((f32[1,8,2,128,256]{4,3,2,1,0:T(8,128)}, f32[1,8,2,128,256]{4,3,2,1,0:T(8,128)S(1)}, u32[]{:S(2)}, u32[]{:S(2)}) %collective-permute-start) | collective-permute-done | bytes 2097184 | tf_op jit(solution)/shard_map/while/body/eval_jaxpr/ppermute | solution.py:10
  165.5 5.5 fusion.55
  182.5 22.6 %collective-permute-done = f32[1,8,2,128,256]{4,3,2,1,0:T(8,128)S(1)} collective-permute-done((f32[1,8,2,128,256]{4,3,2,1,0:T(8,128)}, f32[1,8,2,128,256]{4,3,2,1,0:T(8,128)S(1)}, u32[]{:S(2)}, u32[]{:S(2)}) %collective-permute-start) | collective-permute-done | bytes 2097184 | tf_op jit(solution)/shard_map/while/body/eval_jaxpr/ppermute | solution.py:10
  205.1 5.5 fusion.55
  222.2 22.6 %collective-permute-done = f32[1,8,2,128,256]{4,3,2,1,0:T(8,128)S(1)} collective-permute-done((f32[1,8,2,128,256]{4,3,2,1,0:T(8,128)}, f32[1,8,2,128,256]{4,3,2,1,0:T(8,128)S(1)}, u32[]{:S(2)}, u32[]{:S(2)}) %collective-permute-start) | collective-permute-done | bytes 2097184 | tf_op jit(solution)/shard_map/while/body/eval_jaxpr/ppermute | solution.py:10
  244.8 5.5 fusion.55
  261.8 22.6 %collective-permute-done = f32[1,8,2,128,256]{4,3,2,1,0:T(8,128)S(1)} collective-permute-done((f32[1,8,2,128,256]{4,3,2,1,0:T(8,128)}, f32[1,8,2,128,256]{4,3,2,1,0:T(8,128)S(1)}, u32[]{:S(2)}, u32[]{:S(2)}) %collective-permute-start) | collective-permute-done | bytes 2097184 | tf_op jit(solution)/shard_map/while/body/eval_jaxpr/ppermute | solution.py:10
  284.5 5.5 fusion.55
  301.5 22.6 %collective-permute-done = f32[1,8,2,128,256]{4,3,2,1,0:T(8,128)S(1)} collective-permute-done((f32[1,8,2,128,256]{4,3,2,1,0:T(8,128)}, f32[1,8,2,128,256]{4,3,2,1,0:T(8,128)S(1)}, u32[]{:S(2)}, u32[]{:S(2)}) %collective-permute-start) | collective-permute-done | bytes 2097184 | tf_op jit(solution)/shard_map/while/body/eval_jaxpr/ppermute | solution.py:10
  324.2 5.5 fusion.55
  341.2 22.6 %collective-permute-done = f32[1,8,2,128,256]{4,3,2,1,0:T(8,128)S(1)} collective-permute-done((f32[1,8,2,128,256]{4,3,2,1,0:T(8,128)}, f32[1,8,2,128,256]{4,3,2,1,0:T(8,128)S(1)}, u32[]{:S(2)}, u32[]{:S(2)}) %collective-permute-start) | collective-permute-done | bytes 2097184 | tf_op jit(solution)/shard_map/while/body/eval_jaxpr/ppermute | solution.py:10
  363.8 5.5 fusion.55
  380.9 22.6 %collective-permute-done = f32[1,8,2,128,256]{4,3,2,1,0:T(8,128)S(1)} collective-permute-done((f32[1,8,2,128,256]{4,3,2,1,0:T(8,128)}, f32[1,8,2,128,256]{4,3,2,1,0:T(8,128)S(1)}, u32[]{:S(2)}, u32[]{:S(2)}) %collective-permute-start) | collective-permute-done | bytes 2097184 | tf_op jit(solution)/shard_map/while/body/eval_jaxpr/ppermute | solution.py:10
  403.5 5.5 fusion.55
  420.5 22.6 %collective-permute-done = f32[1,8,2,128,256]{4,3,2,1,0:T(8,128)S(1)} collective-permute-done((f32[1,8,2,128,256]{4,3,2,1,0:T(8,128)}, f32[1,8,2,128,256]{4,3,2,1,0:T(8,128)S(1)}, u32[]{:S(2)}, u32[]{:S(2)}) %collective-permute-start) | collective-permute-done | bytes 2097184 | tf_op jit(solution)/shard_map/while/body/eval_jaxpr/ppermute | solution.py:10
  443.2 5.5 fusion.55
  460.2 22.6 %collective-permute-done = f32[1,8,2,128,256]{4,3,2,1,0:T(8,128)S(1)} collective-permute-done((f32[1,8,2,128,256]{4,3,2,1,0:T(8,128)}, f32[1,8,2,128,256]{4,3,2,1,0:T(8,128)S(1)}, u32[]{:S(2)}, u32[]{:S(2)}) %collective-permute-start) | collective-permute-done | bytes 2097184 | tf_op jit(solution)/shard_map/while/body/eval_jaxpr/ppermute | solution.py:10
  482.8 5.5 fusion.55
  499.9 22.6 %collective-permute-done = f32[1,8,2,128,256]{4,3,2,1,0:T(8,128)S(1)} collective-permute-done((f32[1,8,2,128,256]{4,3,2,1,0:T(8,128)}, f32[1,8,2,128,256]{4,3,2,1,0:T(8,128)S(1)}, u32[]{:S(2)}, u32[]{:S(2)}) %collective-permute-start) | collective-permute-done | bytes 2097184 | tf_op jit(solution)/shard_map/while/body/eval_jaxpr/ppermute | solution.py:10
  522.5 5.5 fusion.55
  539.5 22.6 %collective-permute-done = f32[1,8,2,128,256]{4,3,2,1,0:T(8,128)S(1)} collective-permute-done((f32[1,8,2,128,256]{4,3,2,1,0:T(8,128)}, f32[1,8,2,128,256]{4,3,2,1,0:T(8,128)S(1)}, u32[]{:S(2)}, u32[]{:S(2)}) %collective-permute-start) | collective-permute-done | bytes 2097184 | tf_op jit(solution)/shard_map/while/body/eval_jaxpr/ppermute | solution.py:10
  562.2 5.5 fusion.55
  579.2 22.6 %collective-permute-done = f32[1,8,2,128,256]{4,3,2,1,0:T(8,128)S(1)} collective-permute-done((f32[1,8,2,128,256]{4,3,2,1,0:T(8,128)}, f32[1,8,2,128,256]{4,3,2,1,0:T(8,128)S(1)}, u32[]{:S(2)}, u32[]{:S(2)}) %collective-permute-start) | collective-permute-done | bytes 2097184 | tf_op jit(solution)/shard_map/while/body/eval_jaxpr/ppermute | solution.py:10
  618.9 22.6 %collective-permute-done = f32[1,8,2,128,256]{4,3,2,1,0:T(8,128)S(1)} collective-permute-done((f32[1,8,2,128,256]{4,3,2,1,0:T(8,128)}, f32[1,8,2,128,256]{4,3,2,1,0:T(8,128)S(1)}, u32[]{:S(2)}, u32[]{:S(2)}) %collective-permute-start) | collective-permute-done | bytes 2097184 | tf_op jit(solution)/shard_map/while/body/eval_jaxpr/ppermute | solution.py:10
  657.9 23.3 %collective-permute-done.1 = f32[1,8,2,128,256]{4,3,2,1,0:T(8,128)S(1)} collective-permute-done((f32[1,8,2,128,256]{4,3,2,1,0:T(8,128)}, f32[1,8,2,128,256]{4,3,2,1,0:T(8,128)S(1)}, u32[]{:S(2)}, u32[]{:S(2)}) %collective-permute-start.1) | collective-permute-done | bytes 2097184 | tf_op jit(solution)/shard_map/ppermute | solution.py:10
  (124 shorter events, 208.8 us)
Async XLA Ops:
  0.0 4.7 copy-start.3
  0.0 5.9 copy-start.5
  0.0 31.0 %all-to-all-start = ((f32[1,32,2,32,256]{4,3,2,0,1:T(8,128)}), f32[1,32,2,32,256]{4,3,2,0,1:T(8,128)S(1)}, u32[]{:S(2)}, u32[]{:S(2)}) async-start(f32[1,32,2,32,256]{4,3,2,0,1:T(8,128)} %bitcast.141), calls=%async_computation | async-start | bytes 4194304 | tf_op jit(solution)/shard_map/all_to_all | solution.py:24
  32.7 11.9 %copy-start = (f32[1,8,2,128,256]{4,3,2,1,0:T(8,128)}, f32[1,8,2,128,256]{4,3,2,1,0:T(8,128)S(1)}, u32[]{:S(2)}) copy-start(f32[1,8,2,128,256]{4,3,2,1,0:T(8,128)S(1)} %get-tuple-element.400) | copy-start | bytes 6291460
  38.0 1.3 copy-start.1
  46.5 2.3 copy-start.2
  46.5 2.3 copy-start.4
  57.8 28.4 %collective-permute-start = (f32[1,8,2,128,256]{4,3,2,1,0:T(8,128)}, f32[1,8,2,128,256]{4,3,2,1,0:T(8,128)S(1)}, u32[]{:S(2)}, u32[]{:S(2)}) collective-permute-start(f32[1,8,2,128,256]{4,3,2,1,0:T(8,128)} %get-tuple-element.413), channel_id=1, source_target_pairs={{0,31},{1,0},{2,1},{3,2},{4,3},{5,4},{6,5},{7,6},{8,7},{9,8},{10,9... | collective-permute-start | bytes 6291464 | tf_op jit(solution)/shard_map/while/body/eval_jaxpr/ppermute | solution.py:10
  96.8 29.0 %collective-permute-start = (f32[1,8,2,128,256]{4,3,2,1,0:T(8,128)}, f32[1,8,2,128,256]{4,3,2,1,0:T(8,128)S(1)}, u32[]{:S(2)}, u32[]{:S(2)}) collective-permute-start(f32[1,8,2,128,256]{4,3,2,1,0:T(8,128)} %get-tuple-element.413), channel_id=1, source_target_pairs={{0,31},{1,0},{2,1},{3,2},{4,3},{5,4},{6,5},{7,6},{8,7},{9,8},{10,9... | collective-permute-start | bytes 6291464 | tf_op jit(solution)/shard_map/while/body/eval_jaxpr/ppermute | solution.py:10
  136.5 29.0 %collective-permute-start = (f32[1,8,2,128,256]{4,3,2,1,0:T(8,128)}, f32[1,8,2,128,256]{4,3,2,1,0:T(8,128)S(1)}, u32[]{:S(2)}, u32[]{:S(2)}) collective-permute-start(f32[1,8,2,128,256]{4,3,2,1,0:T(8,128)} %get-tuple-element.413), channel_id=1, source_target_pairs={{0,31},{1,0},{2,1},{3,2},{4,3},{5,4},{6,5},{7,6},{8,7},{9,8},{10,9... | collective-permute-start | bytes 6291464 | tf_op jit(solution)/shard_map/while/body/eval_jaxpr/ppermute | solution.py:10
  176.2 29.0 %collective-permute-start = (f32[1,8,2,128,256]{4,3,2,1,0:T(8,128)}, f32[1,8,2,128,256]{4,3,2,1,0:T(8,128)S(1)}, u32[]{:S(2)}, u32[]{:S(2)}) collective-permute-start(f32[1,8,2,128,256]{4,3,2,1,0:T(8,128)} %get-tuple-element.413), channel_id=1, source_target_pairs={{0,31},{1,0},{2,1},{3,2},{4,3},{5,4},{6,5},{7,6},{8,7},{9,8},{10,9... | collective-permute-start | bytes 6291464 | tf_op jit(solution)/shard_map/while/body/eval_jaxpr/ppermute | solution.py:10
  215.8 29.0 %collective-permute-start = (f32[1,8,2,128,256]{4,3,2,1,0:T(8,128)}, f32[1,8,2,128,256]{4,3,2,1,0:T(8,128)S(1)}, u32[]{:S(2)}, u32[]{:S(2)}) collective-permute-start(f32[1,8,2,128,256]{4,3,2,1,0:T(8,128)} %get-tuple-element.413), channel_id=1, source_target_pairs={{0,31},{1,0},{2,1},{3,2},{4,3},{5,4},{6,5},{7,6},{8,7},{9,8},{10,9... | collective-permute-start | bytes 6291464 | tf_op jit(solution)/shard_map/while/body/eval_jaxpr/ppermute | solution.py:10
  255.5 29.0 %collective-permute-start = (f32[1,8,2,128,256]{4,3,2,1,0:T(8,128)}, f32[1,8,2,128,256]{4,3,2,1,0:T(8,128)S(1)}, u32[]{:S(2)}, u32[]{:S(2)}) collective-permute-start(f32[1,8,2,128,256]{4,3,2,1,0:T(8,128)} %get-tuple-element.413), channel_id=1, source_target_pairs={{0,31},{1,0},{2,1},{3,2},{4,3},{5,4},{6,5},{7,6},{8,7},{9,8},{10,9... | collective-permute-start | bytes 6291464 | tf_op jit(solution)/shard_map/while/body/eval_jaxpr/ppermute | solution.py:10
  295.2 29.0 %collective-permute-start = (f32[1,8,2,128,256]{4,3,2,1,0:T(8,128)}, f32[1,8,2,128,256]{4,3,2,1,0:T(8,128)S(1)}, u32[]{:S(2)}, u32[]{:S(2)}) collective-permute-start(f32[1,8,2,128,256]{4,3,2,1,0:T(8,128)} %get-tuple-element.413), channel_id=1, source_target_pairs={{0,31},{1,0},{2,1},{3,2},{4,3},{5,4},{6,5},{7,6},{8,7},{9,8},{10,9... | collective-permute-start | bytes 6291464 | tf_op jit(solution)/shard_map/while/body/eval_jaxpr/ppermute | solution.py:10
  334.8 29.0 %collective-permute-start = (f32[1,8,2,128,256]{4,3,2,1,0:T(8,128)}, f32[1,8,2,128,256]{4,3,2,1,0:T(8,128)S(1)}, u32[]{:S(2)}, u32[]{:S(2)}) collective-permute-start(f32[1,8,2,128,256]{4,3,2,1,0:T(8,128)} %get-tuple-element.413), channel_id=1, source_target_pairs={{0,31},{1,0},{2,1},{3,2},{4,3},{5,4},{6,5},{7,6},{8,7},{9,8},{10,9... | collective-permute-start | bytes 6291464 | tf_op jit(solution)/shard_map/while/body/eval_jaxpr/ppermute | solution.py:10
  374.5 29.0 %collective-permute-start = (f32[1,8,2,128,256]{4,3,2,1,0:T(8,128)}, f32[1,8,2,128,256]{4,3,2,1,0:T(8,128)S(1)}, u32[]{:S(2)}, u32[]{:S(2)}) collective-permute-start(f32[1,8,2,128,256]{4,3,2,1,0:T(8,128)} %get-tuple-element.413), channel_id=1, source_target_pairs={{0,31},{1,0},{2,1},{3,2},{4,3},{5,4},{6,5},{7,6},{8,7},{9,8},{10,9... | collective-permute-start | bytes 6291464 | tf_op jit(solution)/shard_map/while/body/eval_jaxpr/ppermute | solution.py:10
  414.2 29.0 %collective-permute-start = (f32[1,8,2,128,256]{4,3,2,1,0:T(8,128)}, f32[1,8,2,128,256]{4,3,2,1,0:T(8,128)S(1)}, u32[]{:S(2)}, u32[]{:S(2)}) collective-permute-start(f32[1,8,2,128,256]{4,3,2,1,0:T(8,128)} %get-tuple-element.413), channel_id=1, source_target_pairs={{0,31},{1,0},{2,1},{3,2},{4,3},{5,4},{6,5},{7,6},{8,7},{9,8},{10,9... | collective-permute-start | bytes 6291464 | tf_op jit(solution)/shard_map/while/body/eval_jaxpr/ppermute | solution.py:10
  453.9 29.0 %collective-permute-start = (f32[1,8,2,128,256]{4,3,2,1,0:T(8,128)}, f32[1,8,2,128,256]{4,3,2,1,0:T(8,128)S(1)}, u32[]{:S(2)}, u32[]{:S(2)}) collective-permute-start(f32[1,8,2,128,256]{4,3,2,1,0:T(8,128)} %get-tuple-element.413), channel_id=1, source_target_pairs={{0,31},{1,0},{2,1},{3,2},{4,3},{5,4},{6,5},{7,6},{8,7},{9,8},{10,9... | collective-permute-start | bytes 6291464 | tf_op jit(solution)/shard_map/while/body/eval_jaxpr/ppermute | solution.py:10
  493.5 29.0 %collective-permute-start = (f32[1,8,2,128,256]{4,3,2,1,0:T(8,128)}, f32[1,8,2,128,256]{4,3,2,1,0:T(8,128)S(1)}, u32[]{:S(2)}, u32[]{:S(2)}) collective-permute-start(f32[1,8,2,128,256]{4,3,2,1,0:T(8,128)} %get-tuple-element.413), channel_id=1, source_target_pairs={{0,31},{1,0},{2,1},{3,2},{4,3},{5,4},{6,5},{7,6},{8,7},{9,8},{10,9... | collective-permute-start | bytes 6291464 | tf_op jit(solution)/shard_map/while/body/eval_jaxpr/ppermute | solution.py:10
  533.2 29.0 %collective-permute-start = (f32[1,8,2,128,256]{4,3,2,1,0:T(8,128)}, f32[1,8,2,128,256]{4,3,2,1,0:T(8,128)S(1)}, u32[]{:S(2)}, u32[]{:S(2)}) collective-permute-start(f32[1,8,2,128,256]{4,3,2,1,0:T(8,128)} %get-tuple-element.413), channel_id=1, source_target_pairs={{0,31},{1,0},{2,1},{3,2},{4,3},{5,4},{6,5},{7,6},{8,7},{9,8},{10,9... | collective-permute-start | bytes 6291464 | tf_op jit(solution)/shard_map/while/body/eval_jaxpr/ppermute | solution.py:10
  572.9 29.0 %collective-permute-start = (f32[1,8,2,128,256]{4,3,2,1,0:T(8,128)}, f32[1,8,2,128,256]{4,3,2,1,0:T(8,128)S(1)}, u32[]{:S(2)}, u32[]{:S(2)}) collective-permute-start(f32[1,8,2,128,256]{4,3,2,1,0:T(8,128)} %get-tuple-element.413), channel_id=1, source_target_pairs={{0,31},{1,0},{2,1},{3,2},{4,3},{5,4},{6,5},{7,6},{8,7},{9,8},{10,9... | collective-permute-start | bytes 6291464 | tf_op jit(solution)/shard_map/while/body/eval_jaxpr/ppermute | solution.py:10
  612.5 29.0 %collective-permute-start = (f32[1,8,2,128,256]{4,3,2,1,0:T(8,128)}, f32[1,8,2,128,256]{4,3,2,1,0:T(8,128)S(1)}, u32[]{:S(2)}, u32[]{:S(2)}) collective-permute-start(f32[1,8,2,128,256]{4,3,2,1,0:T(8,128)} %get-tuple-element.413), channel_id=1, source_target_pairs={{0,31},{1,0},{2,1},{3,2},{4,3},{5,4},{6,5},{7,6},{8,7},{9,8},{10,9... | collective-permute-start | bytes 6291464 | tf_op jit(solution)/shard_map/while/body/eval_jaxpr/ppermute | solution.py:10
  652.2 29.0 %collective-permute-start.1 = (f32[1,8,2,128,256]{4,3,2,1,0:T(8,128)}, f32[1,8,2,128,256]{4,3,2,1,0:T(8,128)S(1)}, u32[]{:S(2)}, u32[]{:S(2)}) collective-permute-start(f32[1,8,2,128,256]{4,3,2,1,0:T(8,128)} %get-tuple-element.245), channel_id=1, source_target_pairs={{0,31},{1,0},{2,1},{3,2},{4,3},{5,4},{6,5},{7,6},{8,7},{9,8},{10,9... | collective-permute-start | bytes 6291464 | tf_op jit(solution)/shard_map/ppermute | solution.py:10
where the time goes:
time: 689 us; the launch traced here: 688 us
  waiting for transfers between devices  388 us (56%)
  matrix products  92.1 us (13%)
  starting transfers between devices  86 us (12%)
  local copies, waits for them, and re-layouts  66.7 us (10%)
  other arithmetic  44.5 us (6%)
  loops' own time  9.53 us (1%)
    ppermute x16, waiting for transfers between devices, passed_along(): return lax.ppermute(value, axis, pairs)  363 us
    dot_general x17, matrix products, correlate(): jnp.einsum('gcokps,gckqs->gcopq', stacked, right, precision=prec) * scale  92.1 us
    ppermute x16, starting transfers between devices, passed_along(): return lax.ppermute(value, axis, pairs)  81.3 us
    dynamic_update_slice x16, other arithmetic, place_group(): lax.dynamic_update_slice_in_dim(visibility, correlate_group(pair_rows, fa...  36.9 us
    all_to_all x1, waiting for transfers between devices, shards(): lax.all_to_all(voltages, 'freq', split_axis=1, concat_axis=3, tiled=True)  25 us
    mul x17, local copies, waits for them, and re-layouts, correlate(): jnp.einsum('gcokps,gckqs->gcopq', stacked, right, precision=prec) * scale  22.7 us
    while x15, local copies, waits for them, and re-layouts  20.5 us
  transfers between devices with their start and end apart: 17, of which 17 were waited for; matrix products, arithmetic and copies ran while one was open for 1% of the time, Pallas kernels for 0%

commit v1 on v0

v1 whole, which is shorter than its diff:
```python
import functools

import jax
import jax.numpy as jnp
from jax import lax
from jax.experimental import pallas as pl
from jax.experimental.pallas import tpu as pltpu
from jax.sharding import PartitionSpec as P

CHUNKS = (4, 4)
SIDE = 4


def place(x, z, core):
    return ((x % SIDE) * SIDE + z % SIDE) * 2 + core


def fetch(value, source_of):
    pairs = []
    for x in range(SIDE):
        for z in range(SIDE):
            for core in range(2):
                source = source_of(x, z, core)
                if source is not None:
                    pairs.append((place(*source), place(x, z, core)))
    return lax.ppermute(value, "blk", pairs)


def side(core, flip):
    return 1 if (core == 0) != flip else -1


def after(value, *others):
    return lax.optimization_barrier((value, *others))[0]


def position(info):
    here = info[0]
    return lax.rem(lax.div(here, 2), SIDE), lax.rem(here, 2)


def tile_of(slot, info):
    kind, distance_0, distance_1, exchanged = slot
    z, core = position(info)
    if kind == "own":
        return jnp.int32(0)
    if kind == "mixed":
        return jnp.where(core == 0, 1, 15)
    mine = jnp.where(core == 0, distance_0, distance_1)
    other = jnp.where(core == 0, distance_1, distance_0)
    distance = other if exchanged else mine
    wraps = z + distance >= SIDE
    if kind == "ahead":
        chips = jnp.where(wraps, distance, distance + SIDE)
    else:
        chips = jnp.where(wraps, distance + SIDE, distance)
    if kind == "two":
        chips = jnp.int32(2 * SIDE)
    if exchanged:
        return jnp.where(core == 0, 2 * chips + 1, 2 * chips - 1)
    return 2 * chips


def split(value):
    high = value.astype(jnp.bfloat16)
    low = (value - high.astype(jnp.float32)).astype(jnp.bfloat16)
    return high, low


def tiles_kernel(slots, first, info, own_ref, *refs):
    count = len(slots)
    far_refs = refs[: count - sum(slot[0] == "own" for slot in slots)]
    out_ref, held, sems = refs[-3:]
    channels, _, width, samples = own_ref.shape
    tiles = [tile_of(slot, info) for slot in slots]
    swaps = [info[1 + tile] != info[0] for tile in tiles]

    def copy(index, channel):
        turn = lax.rem(channel, 2)
        return pltpu.make_async_copy(
            held.at[turn, index], out_ref.at[tiles[index], first + channel], sems.at[turn, index]
        )

    def one_channel(channel, _):
        turn = lax.rem(channel, 2)

        @pl.when(channel >= 2)
        def _():
            for index in range(count):
                copy(index, channel - 2).wait()

        own = [split(own_ref[channel, part]) for part in range(2)]
        for index in range(count):
            if slots[index][0] == "own":
                left = right = own
            else:
                far = [split(far_refs[index][channel, part]) for part in range(2)]
                swapped = swaps[index]
                left = [[jnp.where(swapped, f, o) for f, o in zip(a, b)] for a, b in zip(far, own)]
                right = [[jnp.where(swapped, o, f) for f, o in zip(a, b)] for a, b in zip(far, own)]
            rows_high = jnp.concatenate([left[0][0], left[1][0]], axis=1)
            rows_low = jnp.concatenate([left[0][1], left[1][1]], axis=1)
            columns = []
            for level in range(2):
                real = jnp.concatenate([right[0][level], right[1][level]], axis=1)
                imag = jnp.concatenate([-right[1][level], right[0][level]], axis=1)
                columns.append(jnp.concatenate([real, imag], axis=0))
            dims = (((1,), (1,)), ((), ()))
            both = lax.dot_general(
                jnp.concatenate([rows_high, rows_low], axis=0),
                columns[0],
                dims,
                preferred_element_type=jnp.float32,
            )
            cross = lax.dot_general(rows_high, columns[1], dims, preferred_element_type=jnp.float32)
            total = (both[:width] + (both[width:] + cross)) * (1.0 / samples)
            held[turn, index, 0] = total[:, :width]
            held[turn, index, 1] = total[:, width:]
            copy(index, channel).start()
        return 0

    lax.fori_loop(0, channels, one_channel, 0)
    for channel in range(max(0, channels - 2), channels):
        for index in range(count):
            copy(index, channel).wait()


def correlate(visibility, shape, info, own, fars, slots, first, name):
    count = len(slots)
    channels, parts, width, samples = own.shape
    inside = pl.BlockSpec(memory_space=pltpu.VMEM)
    anywhere = pl.BlockSpec(memory_space=pl.ANY)
    before = [] if visibility is None else [visibility]
    return pl.pallas_call(
        functools.partial(tiles_kernel, slots, first),
        in_specs=[pl.BlockSpec(memory_space=pltpu.SMEM)] + [inside] * (len(fars) + 1) + [anywhere] * len(before),
        out_specs=anywhere,
        scratch_shapes=[
            pltpu.VMEM((2, count, 2, width, width), jnp.float32),
            pltpu.SemaphoreType.DMA((2, count)),
        ],
        out_shape=jax.ShapeDtypeStruct(shape, jnp.float32),
        input_output_aliases={len(fars) + 2: 0} if before else {},
        compiler_params=pltpu.CompilerParams(vmem_limit_bytes=16 * 1024 * 1024),
        cost_estimate=pl.CostEstimate(
            flops=channels * count * 2 * 3 * width * 2 * width * samples * 2,
            bytes_accessed=4 * channels * parts * width * ((len(fars) + 1) * samples + count * width),
            transcendentals=0,
        ),
        name=name,
    )(info, own, *fars, *before)


def gather_kernel(info, *refs):
    pieces, out_ref = refs[:SIDE], refs[SIDE]
    rows = pieces[0].shape[2]
    for shift in range(SIDE):
        source = lax.rem(info[0] + SIDE - shift, SIDE)
        start = pl.multiple_of(source * rows, rows)
        out_ref[:, :, pl.ds(start, rows)] = pieces[shift][...]


def on_chip(kernel, info, values, shapes, name):
    inside = pl.BlockSpec(memory_space=pltpu.VMEM)
    return pl.pallas_call(
        kernel,
        in_specs=[pl.BlockSpec(memory_space=pltpu.SMEM)] + [inside] * len(values),
        out_specs=[inside] * len(shapes),
        out_shape=[jax.ShapeDtypeStruct(shape, jnp.float32) for shape in shapes],
        compiler_params=pltpu.CompilerParams(vmem_limit_bytes=16 * 1024 * 1024),
        name=name,
    )(info, *values)


def gather_rows(info, pieces):
    count, parts, rows, samples = pieces[0].shape
    return on_chip(gather_kernel, info, pieces, [(count, parts, rows * SIDE, samples)], "rows")[0]


def choose_kernel(rule, info, first_ref, second_ref, *outs):
    for out, wanted in zip(outs, rule(*position(info))):

        @pl.when(wanted)
        def _():
            out[...] = first_ref[...]

        @pl.when(jnp.logical_not(wanted))
        def _():
            out[...] = second_ref[...]


def choose(rule, count, info, first, second, name):
    return on_chip(functools.partial(choose_kernel, rule), info, [first, second], [first.shape] * count, name)


def far_column(z, core):
    return [z >= 2]


def row_sources(z, core):
    down = z >= 1
    up = z == SIDE - 1
    first = core == 0
    return [jnp.where(first, down, up), jnp.where(first, up, down), core == 1]


def shards(voltages, pair_table, bad_feeds):
    here = lax.axis_index("blk").astype(jnp.int32)
    freq = lax.axis_index("freq").astype(jnp.int32)
    freq_count = lax.axis_size("freq")
    _, channels, parts, rows, samples = voltages.shape
    group = channels // freq_count
    width = rows * freq_count

    inputs = here * width + freq * rows + jnp.arange(rows, dtype=jnp.int32)
    flagged = jnp.any((inputs // 2)[:, None] == bad_feeds[None, :], axis=-1)
    keep = jnp.where(flagged, 0.0, 1.0).astype(jnp.float32)[:, None]
    info = jnp.concatenate([here[None], pair_table[:, 0]])
    freq_info = freq[None]
    shape = (pair_table.shape[0], group, parts, width, width)
    firsts = [sum(CHUNKS[:number]) for number in range(len(CHUNKS))]

    def corner_turn(number, *earlier):
        count = CHUNKS[number]
        with jax.named_scope(f"turn_{number}"):

            def piece(shift):
                start = ((freq + shift) % freq_count) * group + firsts[number]
                return lax.dynamic_slice_in_dim(voltages[0], start, count, 0) * keep

            pieces = [piece(0)]
            for shift in (1, 2, 3):
                pairs = [(source, (source + shift) % freq_count) for source in range(freq_count)]
                pieces.append(lax.ppermute(after(piece(shift), *earlier), "freq", pairs))
            return gather_rows(freq_info, pieces)

    def scoped(name, number, value, source_of):
        with jax.named_scope(f"{name}_{number}"):
            return fetch(value, source_of)

    def exchange(name, number, value):
        return scoped(name + "_core", number, value, lambda x, z, c: (x, z, 1 - c))

    def get_q0(number, own, *earlier):
        own = after(own, *earlier)
        q0 = scoped("q0", number, own, lambda x, z, c: (x + 1, z, c))
        w = scoped("w", number, own, lambda x, z, c: (x - 1, z, c) if z >= 2 else None)
        return q0, w

    def get_row(number, q0, *earlier):
        q0 = after(q0, *earlier)
        qa = scoped("qa", number, q0, lambda x, z, c: (x, z + side(c, False), c))
        qb = scoped("qb", number, q0, lambda x, z, c: (x, z + side(c, True), c))
        return qa, qb

    def get_q2(number, qa, *earlier):
        return scoped("q2", number, after(qa, *earlier), lambda x, z, c: (x, z + side(c, False), c))

    def get_rc(number, q0, w, *earlier):
        source = choose(far_column, 1, info, after(w, *earlier), q0, f"pick_{number}")[0]
        return scoped(
            "rc", number, source, lambda x, z, c: (x - 1, z, c) if z >= 2 else (x + 1, z, c)
        )

    def get_s(number, own, rc, *earlier):
        to_a, to_b, to_mixed = choose(row_sources, 3, info, own, rc, f"pick3_{number}")
        sa = scoped("sa", number, to_a, lambda x, z, c: (x, z + side(c, False), c))
        sb = scoped("sb", number, after(to_b, *earlier), lambda x, z, c: (x, z + side(c, True), c))
        return sa, sb, exchange("rc", number, to_mixed)

    def get_x2(number, q2, *earlier):
        return scoped(
            "x2", number, after(q2, *earlier), lambda x, z, c: (x - 1, z, c) if z <= 1 else (x + 1, z, c)
        )

    def tiles(visibility, number, own, fars, slots, label):
        return correlate(
            visibility, shape, info, own, fars, slots, firsts[number], f"tiles_{label}_{number}"
        )

    near = ("ahead", 1, 3)
    away = ("ahead", 3, 1)
    same = ("ahead", 0, 0)
    twice = ("ahead", 2, 2)

    def with_other(slot):
        return [(*slot, False), (*slot, True)]

    def group_1(visibility, number, own, q0, q0_other):
        slots = with_other(same) + [("own", 0, 0, False)]
        return tiles(visibility, number, own, [q0, q0_other], slots, "g1")

    def group_2(visibility, number, own, qa, qa_other, qb, qb_other):
        slots = with_other(near) + with_other(away)
        return tiles(visibility, number, own, [qa, qa_other, qb, qb_other], slots, "g2")

    def group_3(visibility, number, own, rc, mixed, q2, q2_other):
        slots = [("two", 0, 0, False), ("mixed", 0, 0, False)] + with_other(twice)
        return tiles(visibility, number, own, [rc, mixed, q2, q2_other], slots, "g3")

    def group_4(visibility, number, own, sa, sa_other, sb, sb_other):
        slots = with_other(("row", 1, 3)) + with_other(("row", 3, 1))
        return tiles(visibility, number, own, [sa, sa_other, sb, sb_other], slots, "g4")

    def group_5(visibility, number, own, x2, x2_other):
        return tiles(visibility, number, own, [x2, x2_other], with_other(("row", 2, 2)), "g5")

    own_0 = corner_turn(0)
    q0_0, w_0 = get_q0(0, own_0)
    own_1 = corner_turn(1, own_0)
    qa_0, qb_0 = get_row(0, q0_0, own_1)
    rc_0 = get_rc(0, q0_0, w_0)
    q0_0x = exchange("q0", 0, q0_0)
    q2_0 = get_q2(0, qa_0)
    vis = group_1(None, 0, own_0, q0_0, q0_0x)
    q0_1, w_1 = get_q0(1, own_1, rc_0)
    sa_0, sb_0, mixed_0 = get_s(0, own_0, rc_0, q2_0, vis)
    qa_0x = exchange("qa", 0, qa_0)
    qb_0x = exchange("qb", 0, qb_0)
    q2_0x = exchange("q2", 0, q2_0)
    vis = group_2(vis, 0, own_0, qa_0, qa_0x, qb_0, qb_0x)
    qa_1, qb_1 = get_row(1, q0_1, sa_0, sb_0, vis)
    rc_1 = get_rc(1, q0_1, w_1)
    x2_0 = get_x2(0, q2_0, q0_1)
    q0_1x = exchange("q0", 1, q0_1)
    vis = group_3(vis, 0, own_0, rc_0, mixed_0, q2_0, q2_0x)
    sa_0x = exchange("sa", 0, sa_0)
    sb_0x = exchange("sb", 0, sb_0)
    q2_1 = get_q2(1, qa_1, vis)
    vis = group_1(vis, 1, own_1, q0_1, q0_1x)
    vis = group_4(vis, 0, own_0, sa_0, sa_0x, sb_0, sb_0x)
    sa_1, sb_1, mixed_1 = get_s(1, own_1, rc_1, q2_1, vis)
    qa_1x = exchange("qa", 1, qa_1)
    qb_1x = exchange("qb", 1, qb_1)
    x2_0x = exchange("x2", 0, x2_0)
    x2_1 = get_x2(1, q2_1)
    q2_1x = exchange("q2", 1, q2_1)
    vis = group_5(vis, 0, own_0, x2_0, x2_0x)
    vis = group_2(vis, 1, own_1, qa_1, qa_1x, qb_1, qb_1x)
    vis = group_3(vis, 1, own_1, rc_1, mixed_1, q2_1, q2_1x)
    sa_1x = exchange("sa", 1, after(sa_1, vis))
    sb_1x = exchange("sb", 1, sb_1)
    vis = group_4(vis, 1, own_1, sa_1, sa_1x, sb_1, sb_1x)
    x2_1x = exchange("x2", 1, x2_1)
    return group_5(vis, 1, own_1, x2_1, x2_1x)


def solution(mesh):
    placed = (P("blk", None, None, "freq", None), P("blk", None), P())
    return jax.shard_map(
        shards,
        mesh=mesh,
        in_specs=placed,
        out_specs=P("blk", "freq", None, None, None),
        check_vma=False,
    )
```

time: 689 us -> 201 us (0.29)
  waiting for transfers between devices: 388 us -> 97.5 us
  matrix products: 92.1 us -> 0 us
  local copies, waits for them, and re-layouts: 66.7 us -> 0.68 us
  Pallas kernels: 0 us -> 44.6 us
  other arithmetic: 44.5 us -> 2.68 us
  starting transfers between devices: 86 us -> 52.7 us
  loops' own time: 9.53 us -> 0 us
    ppermute x16 -> x40, waiting for transfers between devices: 363 us -> 97.5 us  [the longest x34 75.2 us: fetch(): return lax.ppermute(value, 'blk', pairs)]
    dot_general x17 -> x0, matrix products: 92.1 us -> none  [correlate(): jnp.einsum('gcokps,gckqs->gcopq', stacked, right, precision=prec) * scale]
    pallas_call x0 -> x16, Pallas kernels: none -> 44.6 us  [the longest x10 41.7 us: correlate(): pl.pallas_call(functools.partial(tiles_kernel, slots, first), in_specs=[p...]
    dynamic_update_slice x16 -> x0, other arithmetic: 36.9 us -> none  [place_group(): lax.dynamic_update_slice_in_dim(visibility, correlate_group(pair_rows, fa...]
    ppermute x16 -> x40, starting transfers between devices: 81.3 us -> 52.7 us  [the longest x34 42.7 us: fetch(): return lax.ppermute(value, 'blk', pairs)]
    all_to_all x1 -> x0, waiting for transfers between devices: 25 us -> none  [shards(): lax.all_to_all(voltages, 'freq', split_axis=1, concat_axis=3, tiled=True)]
    mul x17 -> x0, local copies, waits for them, and re-layouts: 22.7 us -> none  [correlate(): jnp.einsum('gcokps,gckqs->gcopq', stacked, right, precision=prec) * scale]
    while x15 -> x0, local copies, waits for them, and re-layouts: 20.5 us -> none
  transfers between devices with their start and end apart: 17 -> 40, of which waited for: 17 -> 14; matrix products, arithmetic and copies ran while one was open for 1% -> 0% of each run, Pallas kernels for 0% -> 21%
where the time goes in v1:
time: 201 us; the launch traced here: 199 us
  waiting for transfers between devices  97.5 us (49%)
  starting transfers between devices  52.7 us (26%)
  Pallas kernels  44.6 us (22%)
  other arithmetic  2.68 us (1%)
    ppermute x34, waiting for transfers between devices, fetch(): return lax.ppermute(value, 'blk', pairs)  75.2 us
    ppermute x34, starting transfers between devices, fetch(): return lax.ppermute(value, 'blk', pairs)  42.7 us
    pallas_call x10, Pallas kernels, correlate(): pl.pallas_call(functools.partial(tiles_kernel, slots, first), in_specs=[p...  41.7 us
    ppermute x6, waiting for transfers between devices, corner_turn(): pieces.append(lax.ppermute(after(piece(shift), *earlier), 'freq', pairs))  22.3 us
    ppermute x6, starting transfers between devices, corner_turn(): pieces.append(lax.ppermute(after(piece(shift), *earlier), 'freq', pairs))  9.98 us
  transfers between devices with their start and end apart: 40, of which 14 were waited for; matrix products, arithmetic and copies ran while one was open for 0% of the time, Pallas kernels for 21%

profile of v1, /device:TPU:0, one launch (start us, length us, event | category | flops | bytes accessed | tf_op | source)
XLA Modules:
  0.0 198.7 jit_solution(194311284470727508)
XLA Ops:
  4.4 2.9 %collective-permute-start.1 = (f32[4,2,32,256]{3,2,1,0:T(8,128)S(1)}, f32[4,2,32,256]{3,2,1,0:T(8,128)S(1)}, u32[]{:S(2)}, u32[]{:S(2)}) collective-permute-start(f32[4,2,32,256]{3,2,1,0:T(8,128)S(1)} %get-tuple-element.41), channel_id=1, source_target_pairs={{0,64},{32,96},{64,0},{96,32},{1,65},{33,97},{65,1},{97,33},{2,66}... | collective-permute-start | bytes 786440 | tf_op jit(solution)/shard_map/turn_0/ppermute | solution.py:234
  8.6 3.5 %collective-permute-done.refs_1_ = f32[4,2,32,256]{3,2,1,0:T(8,128)S(1)} collective-permute-done((f32[4,2,32,256]{3,2,1,0:T(8,128)S(1)}, f32[4,2,32,256]{3,2,1,0:T(8,128)S(1)}, u32[]{:S(2)}, u32[]{:S(2)}) %collective-permute-start) | collective-permute-done | bytes 262176 | tf_op jit(solution)/shard_map/turn_0/ppermute | solution.py:234
  12.1 6.8 %collective-permute-done.1.refs_2_ = f32[4,2,32,256]{3,2,1,0:T(8,128)S(1)} collective-permute-done((f32[4,2,32,256]{3,2,1,0:T(8,128)S(1)}, f32[4,2,32,256]{3,2,1,0:T(8,128)S(1)}, u32[]{:S(2)}, u32[]{:S(2)}) %collective-permute-start.1) | collective-permute-done | bytes 262176 | tf_op jit(solution)/shard_map/turn_0/ppermute | solution.py:234
  19.0 2.8 %collective-permute-start.7 = (f32[4,2,128,256]{3,2,1,0:T(8,128)S(1)}, f32[4,2,128,256]{3,2,1,0:T(8,128)S(1)}, u32[]{:S(2)}, u32[]{:S(2)}) collective-permute-start(f32[4,2,128,256]{3,2,1,0:T(8,128)S(1)} %rows.2.first_ref.own_ref), channel_id=1, source_target_pairs={{8,0},{9,1},{10,2},{11,3},{12,4},{13,5},{14,6},{15,7},{16,8},{17,9... | collective-permute-start | bytes 3145736 | tf_op jit(solution)/shard_map/q0_0/ppermute | solution.py:26
  21.8 2.2 %collective-permute-start.5 = (f32[4,2,32,256]{3,2,1,0:T(8,128)S(1)}, f32[4,2,32,256]{3,2,1,0:T(8,128)S(1)}, u32[]{:S(2)}, u32[]{:S(2)}) collective-permute-start(f32[4,2,32,256]{3,2,1,0:T(8,128)S(1)} %get-tuple-element.24), channel_id=1, source_target_pairs={{0,96},{32,0},{64,32},{96,64},{1,97},{33,1},{65,33},{97,65},{2,98}... | collective-permute-start | bytes 786440 | tf_op jit(solution)/shard_map/turn_1/ppermute | solution.py:234
  26.6 8.5 %collective-permute-done.5.refs_3_ = f32[4,2,32,256]{3,2,1,0:T(8,128)S(1)} collective-permute-done((f32[4,2,32,256]{3,2,1,0:T(8,128)S(1)}, f32[4,2,32,256]{3,2,1,0:T(8,128)S(1)}, u32[]{:S(2)}, u32[]{:S(2)}) %collective-permute-start.5) | collective-permute-done | bytes 262176 | tf_op jit(solution)/shard_map/turn_1/ppermute | solution.py:234
  35.1 3.5 %collective-permute-done.3.refs_1_ = f32[4,2,32,256]{3,2,1,0:T(8,128)S(1)} collective-permute-done((f32[4,2,32,256]{3,2,1,0:T(8,128)S(1)}, f32[4,2,32,256]{3,2,1,0:T(8,128)S(1)}, u32[]{:S(2)}, u32[]{:S(2)}) %collective-permute-start.3) | collective-permute-done | bytes 262176 | tf_op jit(solution)/shard_map/turn_1/ppermute | solution.py:234
  38.7 4.7 %collective-permute-done.7.second_ref.refs_0_ = f32[4,2,128,256]{3,2,1,0:T(8,128)S(1)} collective-permute-done((f32[4,2,128,256]{3,2,1,0:T(8,128)S(1)}, f32[4,2,128,256]{3,2,1,0:T(8,128)S(1)}, u32[]{:S(2)}, u32[]{:S(2)}) %collective-permute-start.7) | collective-permute-done | bytes 1048608 | tf_op jit(solution)/shard_map/q0_0/ppermute | solution.py:26
  43.4 4.0 %collective-permute-start.11 = (f32[4,2,128,256]{3,2,1,0:T(8,128)S(1)}, f32[4,2,128,256]{3,2,1,0:T(8,128)S(1)}, u32[]{:S(2)}, u32[]{:S(2)}) collective-permute-start(f32[4,2,128,256]{3,2,1,0:T(8,128)S(1)} %collective-permute-done.7.second_ref.refs_0_), channel_id=1, source_target_pairs={{2,0},{7,1},{4,2},{1,3},{6,4},{3,5},{0,6},{5,7},{10,8},{15,9},{12,... | collective-permute-start | bytes 3145736 | tf_op jit(solution)/shard_map/qa_0/ppermute | solution.py:26
  48.8 3.8 %collective-permute-start.8 = (f32[4,2,128,256]{3,2,1,0:T(8,128)S(1)}, f32[4,2,128,256]{3,2,1,0:T(8,128)S(1)}, u32[]{:S(2)}, u32[]{:S(2)}) collective-permute-start(f32[4,2,128,256]{3,2,1,0:T(8,128)S(1)} %pick_0.1), channel_id=1, source_target_pairs={{8,0},{9,1},{10,2},{11,3},{28,4},{29,5},{30,6},{31,7},{16,8},{17,9... | collective-permute-start | bytes 3145736 | tf_op jit(solution)/shard_map/rc_0/ppermute | solution.py:26
  52.6 16.5 %collective-permute-done.11.refs_0_ = f32[4,2,128,256]{3,2,1,0:T(8,128)S(1)} collective-permute-done((f32[4,2,128,256]{3,2,1,0:T(8,128)S(1)}, f32[4,2,128,256]{3,2,1,0:T(8,128)S(1)}, u32[]{:S(2)}, u32[]{:S(2)}) %collective-permute-start.11) | collective-permute-done | bytes 1048608 | tf_op jit(solution)/shard_map/qa_0/ppermute | solution.py:26
  69.1 3.4 %collective-permute-start.12 = (f32[4,2,128,256]{3,2,1,0:T(8,128)S(1)}, f32[4,2,128,256]{3,2,1,0:T(8,128)S(1)}, u32[]{:S(2)}, u32[]{:S(2)}) collective-permute-start(f32[4,2,128,256]{3,2,1,0:T(8,128)S(1)} %collective-permute-done.11.refs_0_), channel_id=1, source_target_pairs={{2,0},{7,1},{4,2},{1,3},{6,4},{3,5},{0,6},{5,7},{10,8},{15,9},{12,... | collective-permute-start | bytes 3145736 | tf_op jit(solution)/shard_map/q2_0/ppermute | solution.py:26
  73.8 7.5 %collective-permute-start.10 = (f32[4,2,128,256]{3,2,1,0:T(8,128)S(1)}, f32[4,2,128,256]{3,2,1,0:T(8,128)S(1)}, u32[]{:S(2)}, u32[]{:S(2)}) collective-permute-start(f32[4,2,128,256]{3,2,1,0:T(8,128)S(1)} %get-tuple-element.26), channel_id=1, source_target_pairs={{2,0},{7,1},{4,2},{1,3},{6,4},{3,5},{0,6},{5,7},{10,8},{15,9},{12,... | collective-permute-start | bytes 3145736 | tf_op jit(solution)/shard_map/sa_0/ppermute | solution.py:26
  81.3 3.8 %tiles_g1_0.1.refs_4_ = f32[17,8,2,128,128]{4,3,2,1,0:T(8,128)} custom-call(s32[18]{0:T(128)S(1)} %pad_add_fusion.info, f32[4,2,128,256]{3,2,1,0:T(8,128)S(1)} %rows.2.first_ref.own_ref, f32[4,2,128,256]{3,2,1,0:T(8,128)S(1)} %collective-permute-done.7.second_ref.refs_0_, f32[4,2,128,256]{3,2,1,0:T(8,128)S(1)} %collective-permute-done.13.refs_1_), custom_call_target="tpu_custom_call" | custom-call | flops 1207959552 | bytes 4718592 | tf_op jit(solution)/shard_map/tiles_g1_0/pallas_call | solution.py:134
  88.1 19.2 %collective-permute-done.10.refs_0_ = f32[4,2,128,256]{3,2,1,0:T(8,128)S(1)} collective-permute-done((f32[4,2,128,256]{3,2,1,0:T(8,128)S(1)}, f32[4,2,128,256]{3,2,1,0:T(8,128)S(1)}, u32[]{:S(2)}, u32[]{:S(2)}) %collective-permute-start.10) | collective-permute-done | bytes 1048608 | tf_op jit(solution)/shard_map/sa_0/ppermute | solution.py:26
  107.3 4.5 %tiles_g2_0.1.refs_4_ = f32[17,8,2,128,128]{4,3,2,1,0:T(8,128)} custom-call(s32[18]{0:T(128)S(1)} %pad_add_fusion.info, f32[4,2,128,256]{3,2,1,0:T(8,128)S(1)} %rows.2.first_ref.own_ref, f32[4,2,128,256]{3,2,1,0:T(8,128)S(1)} %collective-permute-done.11.refs_0_, ...), custom_call_target="tpu_custom_call", output_to_operand_aliasing={{}: (6, {})} | custom-call | flops 1610612736 | bytes 7340032 | tf_op jit(solution)/shard_map/tiles_g2_0/pallas_call | solution.py:134
  111.9 3.8 %collective-permute-start.18 = (f32[4,2,128,256]{3,2,1,0:T(8,128)S(1)}, f32[4,2,128,256]{3,2,1,0:T(8,128)S(1)}, u32[]{:S(2)}, u32[]{:S(2)}) collective-permute-start(f32[4,2,128,256]{3,2,1,0:T(8,128)S(1)} %collective-permute-done.9.second_ref.refs_0_), channel_id=1, source_target_pairs={{2,0},{7,1},{4,2},{1,3},{6,4},{3,5},{0,6},{5,7},{10,8},{15,9},{12,... | collective-permute-start | bytes 3145736 | tf_op jit(solution)/shard_map/qa_1/ppermute | solution.py:26
  118.0 2.5 %collective-permute-start.25 = (f32[4,2,128,256]{3,2,1,0:T(8,128)S(1)}, f32[4,2,128,256]{3,2,1,0:T(8,128)S(1)}, u32[]{:S(2)}, u32[]{:S(2)}) collective-permute-start(f32[4,2,128,256]{3,2,1,0:T(8,128)S(1)} %pick_1.1), channel_id=1, source_target_pairs={{8,0},{9,1},{10,2},{11,3},{28,4},{29,5},{30,6},{31,7},{16,8},{17,9... | collective-permute-start | bytes 3145736 | tf_op jit(solution)/shard_map/rc_1/ppermute | solution.py:26
  120.6 7.4 %collective-permute-done.18.refs_0_ = f32[4,2,128,256]{3,2,1,0:T(8,128)S(1)} collective-permute-done((f32[4,2,128,256]{3,2,1,0:T(8,128)S(1)}, f32[4,2,128,256]{3,2,1,0:T(8,128)S(1)}, u32[]{:S(2)}, u32[]{:S(2)}) %collective-permute-start.18) | collective-permute-done | bytes 1048608 | tf_op jit(solution)/shard_map/qa_1/ppermute | solution.py:26
  128.0 4.5 %tiles_g3_0.1.refs_2_ = f32[17,8,2,128,128]{4,3,2,1,0:T(8,128)} custom-call(s32[18]{0:T(128)S(1)} %pad_add_fusion.info, f32[4,2,128,256]{3,2,1,0:T(8,128)S(1)} %rows.2.first_ref.own_ref, f32[4,2,128,256]{3,2,1,0:T(8,128)S(1)} %collective-permute-done.8.second_ref.refs_0_, ...), custom_call_target="tpu_custom_call", output_to_operand_aliasing={{}: (6, {})} | custom-call | flops 1610612736 | bytes 7340032 | tf_op jit(solution)/shard_map/tiles_g3_0/pallas_call | solution.py:134
  136.4 6.9 %collective-permute-done.32.refs_0_ = f32[4,2,128,256]{3,2,1,0:T(8,128)S(1)} collective-permute-done((f32[4,2,128,256]{3,2,1,0:T(8,128)S(1)}, f32[4,2,128,256]{3,2,1,0:T(8,128)S(1)}, u32[]{:S(2)}, u32[]{:S(2)}) %collective-permute-start.32) | collective-permute-done | bytes 1048608 | tf_op jit(solution)/shard_map/x2_0/ppermute | solution.py:26
  143.8 6.7 %collective-permute-done.30.refs_2_ = f32[4,2,128,256]{3,2,1,0:T(8,128)S(1)} collective-permute-done((f32[4,2,128,256]{3,2,1,0:T(8,128)S(1)}, f32[4,2,128,256]{3,2,1,0:T(8,128)S(1)}, u32[]{:S(2)}, u32[]{:S(2)}) %collective-permute-start.30) | collective-permute-done | bytes 1048608 | tf_op jit(solution)/shard_map/qb_1/ppermute | solution.py:26
  151.2 3.8 %tiles_g1_1.1.refs_4_ = f32[17,8,2,128,128]{4,3,2,1,0:T(8,128)} custom-call(s32[18]{0:T(128)S(1)} %pad_add_fusion.info, f32[4,2,128,256]{3,2,1,0:T(8,128)S(1)} %rows.3.first_ref.own_ref, f32[4,2,128,256]{3,2,1,0:T(8,128)S(1)} %collective-permute-done.9.second_ref.refs_0_, ...), custom_call_target="tpu_custom_call", output_to_operand_aliasing={{}: (4, {})} | custom-call | flops 1207959552 | bytes 4718592 | tf_op jit(solution)/shard_map/tiles_g1_1/pallas_call | solution.py:134
  155.7 4.5 %tiles_g4_0.1.refs_2_ = f32[17,8,2,128,128]{4,3,2,1,0:T(8,128)} custom-call(s32[18]{0:T(128)S(1)} %pad_add_fusion.info, f32[4,2,128,256]{3,2,1,0:T(8,128)S(1)} %rows.2.first_ref.own_ref, f32[4,2,128,256]{3,2,1,0:T(8,128)S(1)} %collective-permute-done.10.refs_0_, ...), custom_call_target="tpu_custom_call", output_to_operand_aliasing={{}: (6, {})} | custom-call | flops 1610612736 | bytes 7340032 | tf_op jit(solution)/shard_map/tiles_g4_0/pallas_call | solution.py:134
  160.3 2.8 %collective-permute-start.26 = (f32[4,2,128,256]{3,2,1,0:T(8,128)S(1)}, f32[4,2,128,256]{3,2,1,0:T(8,128)S(1)}, u32[]{:S(2)}, u32[]{:S(2)}) collective-permute-start(f32[4,2,128,256]{3,2,1,0:T(8,128)S(1)} %get-tuple-element.33), channel_id=1, source_target_pairs={{2,0},{7,1},{4,2},{1,3},{6,4},{3,5},{0,6},{5,7},{10,8},{15,9},{12,... | collective-permute-start | bytes 3145736 | tf_op jit(solution)/shard_map/sa_1/ppermute | solution.py:26
  164.3 3.4 %tiles_g5_0.1.refs_4_ = f32[17,8,2,128,128]{4,3,2,1,0:T(8,128)} custom-call(s32[18]{0:T(128)S(1)} %pad_add_fusion.info, f32[4,2,128,256]{3,2,1,0:T(8,128)S(1)} %rows.2.first_ref.own_ref, f32[4,2,128,256]{3,2,1,0:T(8,128)S(1)} %collective-permute-done.32.refs_0_, ...), custom_call_target="tpu_custom_call", output_to_operand_aliasing={{}: (4, {})} | custom-call | flops 805306368 | bytes 4194304 | tf_op jit(solution)/shard_map/tiles_g5_0/pallas_call | solution.py:134
  167.8 4.5 %tiles_g2_1.1.refs_4_ = f32[17,8,2,128,128]{4,3,2,1,0:T(8,128)} custom-call(s32[18]{0:T(128)S(1)} %pad_add_fusion.info, f32[4,2,128,256]{3,2,1,0:T(8,128)S(1)} %rows.3.first_ref.own_ref, f32[4,2,128,256]{3,2,1,0:T(8,128)S(1)} %collective-permute-done.18.refs_0_, ...), custom_call_target="tpu_custom_call", output_to_operand_aliasing={{}: (6, {})} | custom-call | flops 1610612736 | bytes 7340032 | tf_op jit(solution)/shard_map/tiles_g2_1/pallas_call | solution.py:134
  172.3 4.5 %tiles_g3_1.1.refs_4_ = f32[17,8,2,128,128]{4,3,2,1,0:T(8,128)} custom-call(s32[18]{0:T(128)S(1)} %pad_add_fusion.info, f32[4,2,128,256]{3,2,1,0:T(8,128)S(1)} %rows.3.first_ref.own_ref, f32[4,2,128,256]{3,2,1,0:T(8,128)S(1)} %collective-permute-done.25.second_ref.refs_0_, ...), custom_call_target="tpu_custom_call", output_to_operand_aliasing={{}: (6, {})} | custom-call | flops 1610612736 | bytes 7340032 | tf_op jit(solution)/shard_map/tiles_g3_1/pallas_call | solution.py:134
  176.9 9.4 %collective-permute-done.26.refs_0_ = f32[4,2,128,256]{3,2,1,0:T(8,128)S(1)} collective-permute-done((f32[4,2,128,256]{3,2,1,0:T(8,128)S(1)}, f32[4,2,128,256]{3,2,1,0:T(8,128)S(1)}, u32[]{:S(2)}, u32[]{:S(2)}) %collective-permute-start.26) | collective-permute-done | bytes 1048608 | tf_op jit(solution)/shard_map/sa_1/ppermute | solution.py:26
  187.0 3.4 %collective-permute-done.22.refs_0_ = f32[4,2,128,256]{3,2,1,0:T(8,128)S(1)} collective-permute-done((f32[4,2,128,256]{3,2,1,0:T(8,128)S(1)}, f32[4,2,128,256]{3,2,1,0:T(8,128)S(1)}, u32[]{:S(2)}, u32[]{:S(2)}) %collective-permute-start.22) | collective-permute-done | bytes 1048608 | tf_op jit(solution)/shard_map/x2_1/ppermute | solution.py:26
  190.5 4.6 %tiles_g4_1.1.refs_2_ = f32[17,8,2,128,128]{4,3,2,1,0:T(8,128)} custom-call(s32[18]{0:T(128)S(1)} %pad_add_fusion.info, f32[4,2,128,256]{3,2,1,0:T(8,128)S(1)} %rows.3.first_ref.own_ref, f32[4,2,128,256]{3,2,1,0:T(8,128)S(1)} %collective-permute-done.26.refs_0_, ...), custom_call_target="tpu_custom_call", output_to_operand_aliasing={{}: (6, {})} | custom-call | flops 1610612736 | bytes 7340032 | tf_op jit(solution)/shard_map/tiles_g4_1/pallas_call | solution.py:134
  195.1 3.4 %tiles_g5_1.1 = f32[17,8,2,128,128]{4,3,2,1,0:T(8,128)} custom-call(s32[18]{0:T(128)S(1)} %pad_add_fusion.info, f32[4,2,128,256]{3,2,1,0:T(8,128)S(1)} %rows.3.first_ref.own_ref, f32[4,2,128,256]{3,2,1,0:T(8,128)S(1)} %collective-permute-done.22.refs_0_, f32[4,2,128,256]{3,2,1,0:T(8,128)S(1)} %collective-permute-done.23.refs_1_, ...), custom_call_target="tpu_custom_call", output_to_operand_aliasing={{}: (4, {})} | custom-call | flops 805306368 | bytes 4194304 | tf_op jit(solution)/shard_map/tiles_g5_1/pallas_call | solution.py:134
  (70 shorter events, 24.3 us)
Async XLA Ops:
  4.4 14.5 %collective-permute-start.1 = (f32[4,2,32,256]{3,2,1,0:T(8,128)S(1)}, f32[4,2,32,256]{3,2,1,0:T(8,128)S(1)}, u32[]{:S(2)}, u32[]{:S(2)}) collective-permute-start(f32[4,2,32,256]{3,2,1,0:T(8,128)S(1)} %get-tuple-element.41), channel_id=1, source_target_pairs={{0,64},{32,96},{64,0},{96,32},{1,65},{33,97},{65,1},{97,33},{2,66}... | collective-permute-start | bytes 786440 | tf_op jit(solution)/shard_map/turn_0/ppermute | solution.py:234
  19.0 24.4 %collective-permute-start.7 = (f32[4,2,128,256]{3,2,1,0:T(8,128)S(1)}, f32[4,2,128,256]{3,2,1,0:T(8,128)S(1)}, u32[]{:S(2)}, u32[]{:S(2)}) collective-permute-start(f32[4,2,128,256]{3,2,1,0:T(8,128)S(1)} %rows.2.first_ref.own_ref), channel_id=1, source_target_pairs={{8,0},{9,1},{10,2},{11,3},{12,4},{13,5},{14,6},{15,7},{16,8},{17,9... | collective-permute-start | bytes 3145736 | tf_op jit(solution)/shard_map/q0_0/ppermute | solution.py:26
  21.8 13.2 %collective-permute-start.5 = (f32[4,2,32,256]{3,2,1,0:T(8,128)S(1)}, f32[4,2,32,256]{3,2,1,0:T(8,128)S(1)}, u32[]{:S(2)}, u32[]{:S(2)}) collective-permute-start(f32[4,2,32,256]{3,2,1,0:T(8,128)S(1)} %get-tuple-element.24), channel_id=1, source_target_pairs={{0,96},{32,0},{64,32},{96,64},{1,97},{33,1},{65,33},{97,65},{2,98}... | collective-permute-start | bytes 786440 | tf_op jit(solution)/shard_map/turn_1/ppermute | solution.py:234
  25.1 13.5 %collective-permute-start.3 = (f32[4,2,32,256]{3,2,1,0:T(8,128)S(1)}, f32[4,2,32,256]{3,2,1,0:T(8,128)S(1)}, u32[]{:S(2)}, u32[]{:S(2)}) collective-permute-start(f32[4,2,32,256]{3,2,1,0:T(8,128)S(1)} %get-tuple-element.22), channel_id=1, source_target_pairs={{0,32},{32,64},{64,96},{96,0},{1,33},{33,65},{65,97},{97,1},{2,34}... | collective-permute-start | bytes 786440 | tf_op jit(solution)/shard_map/turn_1/ppermute | solution.py:234
  25.8 22.4 %collective-permute-start.6 = (f32[4,2,128,256]{3,2,1,0:T(8,128)S(1)}, f32[4,2,128,256]{3,2,1,0:T(8,128)S(1)}, u32[]{:S(2)}, u32[]{:S(2)}) collective-permute-start(f32[4,2,128,256]{3,2,1,0:T(8,128)S(1)} %rows.2.first_ref.own_ref), channel_id=1, source_target_pairs={{28,4},{29,5},{30,6},{31,7},{4,12},{5,13},{6,14},{7,15},{12,20},{1... | collective-permute-start | bytes 3145736 | tf_op jit(solution)/shard_map/w_0/ppermute | solution.py:26
  43.4 25.7 %collective-permute-start.11 = (f32[4,2,128,256]{3,2,1,0:T(8,128)S(1)}, f32[4,2,128,256]{3,2,1,0:T(8,128)S(1)}, u32[]{:S(2)}, u32[]{:S(2)}) collective-permute-start(f32[4,2,128,256]{3,2,1,0:T(8,128)S(1)} %collective-permute-done.7.second_ref.refs_0_), channel_id=1, source_target_pairs={{2,0},{7,1},{4,2},{1,3},{6,4},{3,5},{0,6},{5,7},{10,8},{15,9},{12,... | collective-permute-start | bytes 3145736 | tf_op jit(solution)/shard_map/qa_0/ppermute | solution.py:26
  48.2 24.3 %collective-permute-start.16 = (f32[4,2,128,256]{3,2,1,0:T(8,128)S(1)}, f32[4,2,128,256]{3,2,1,0:T(8,128)S(1)}, u32[]{:S(2)}, u32[]{:S(2)}) collective-permute-start(f32[4,2,128,256]{3,2,1,0:T(8,128)S(1)} %collective-permute-done.7.second_ref.refs_0_), channel_id=1, source_target_pairs={{6,0},{3,1},{0,2},{5,3},{2,4},{7,5},{4,6},{1,7},{14,8},{11,9},{8,1... | collective-permute-start | bytes 3145736 | tf_op jit(solution)/shard_map/qb_0/ppermute | solution.py:26
  48.8 24.2 %collective-permute-start.8 = (f32[4,2,128,256]{3,2,1,0:T(8,128)S(1)}, f32[4,2,128,256]{3,2,1,0:T(8,128)S(1)}, u32[]{:S(2)}, u32[]{:S(2)}) collective-permute-start(f32[4,2,128,256]{3,2,1,0:T(8,128)S(1)} %pick_0.1), channel_id=1, source_target_pairs={{8,0},{9,1},{10,2},{11,3},{28,4},{29,5},{30,6},{31,7},{16,8},{17,9... | collective-permute-start | bytes 3145736 | tf_op jit(solution)/shard_map/rc_0/ppermute | solution.py:26
  52.6 28.7 %collective-permute-start.13 = (f32[4,2,128,256]{3,2,1,0:T(8,128)S(1)}, f32[4,2,128,256]{3,2,1,0:T(8,128)S(1)}, u32[]{:S(2)}, u32[]{:S(2)}) collective-permute-start(f32[4,2,128,256]{3,2,1,0:T(8,128)S(1)} %collective-permute-done.7.second_ref.refs_0_), channel_id=1, source_target_pairs={{1,0},{0,1},{3,2},{2,3},{5,4},{4,5},{7,6},{6,7},{9,8},{8,9},{11,10... | collective-permute-start | bytes 3145736 | tf_op jit(solution)/shard_map/q0_core_0/ppermute | solution.py:26
  69.1 16.3 %collective-permute-start.12 = (f32[4,2,128,256]{3,2,1,0:T(8,128)S(1)}, f32[4,2,128,256]{3,2,1,0:T(8,128)S(1)}, u32[]{:S(2)}, u32[]{:S(2)}) collective-permute-start(f32[4,2,128,256]{3,2,1,0:T(8,128)S(1)} %collective-permute-done.11.refs_0_), channel_id=1, source_target_pairs={{2,0},{7,1},{4,2},{1,3},{6,4},{3,5},{0,6},{5,7},{10,8},{15,9},{12,... | collective-permute-start | bytes 3145736 | tf_op jit(solution)/shard_map/q2_0/ppermute | solution.py:26
  72.5 14.8 %collective-permute-start.15 = (f32[4,2,128,256]{3,2,1,0:T(8,128)S(1)}, f32[4,2,128,256]{3,2,1,0:T(8,128)S(1)}, u32[]{:S(2)}, u32[]{:S(2)}) collective-permute-start(f32[4,2,128,256]{3,2,1,0:T(8,128)S(1)} %collective-permute-done.11.refs_0_), channel_id=1, source_target_pairs={{1,0},{0,1},{3,2},{2,3},{5,4},{4,5},{7,6},{6,7},{9,8},{8,9},{11,10... | collective-permute-start | bytes 3145736 | tf_op jit(solution)/shard_map/qa_core_0/ppermute | solution.py:26
  72.5 14.8 %collective-permute-start.17 = (f32[4,2,128,256]{3,2,1,0:T(8,128)S(1)}, f32[4,2,128,256]{3,2,1,0:T(8,128)S(1)}, u32[]{:S(2)}, u32[]{:S(2)}) collective-permute-start(f32[4,2,128,256]{3,2,1,0:T(8,128)S(1)} %collective-permute-done.16.refs_2_), channel_id=1, source_target_pairs={{1,0},{0,1},{3,2},{2,3},{5,4},{4,5},{7,6},{6,7},{9,8},{8,9},{11,10... | collective-permute-start | bytes 3145736 | tf_op jit(solution)/shard_map/qb_core_0/ppermute | solution.py:26
  73.8 33.5 %collective-permute-start.10 = (f32[4,2,128,256]{3,2,1,0:T(8,128)S(1)}, f32[4,2,128,256]{3,2,1,0:T(8,128)S(1)}, u32[]{:S(2)}, u32[]{:S(2)}) collective-permute-start(f32[4,2,128,256]{3,2,1,0:T(8,128)S(1)} %get-tuple-element.26), channel_id=1, source_target_pairs={{2,0},{7,1},{4,2},{1,3},{6,4},{3,5},{0,6},{5,7},{10,8},{15,9},{12,... | collective-permute-start | bytes 3145736 | tf_op jit(solution)/shard_map/sa_0/ppermute | solution.py:26
  81.3 30.5 %collective-permute-start.9 = (f32[4,2,128,256]{3,2,1,0:T(8,128)S(1)}, f32[4,2,128,256]{3,2,1,0:T(8,128)S(1)}, u32[]{:S(2)}, u32[]{:S(2)}) collective-permute-start(f32[4,2,128,256]{3,2,1,0:T(8,128)S(1)} %rows.3.first_ref.own_ref), channel_id=1, source_target_pairs={{8,0},{9,1},{10,2},{11,3},{12,4},{13,5},{14,6},{15,7},{16,8},{17,9... | collective-permute-start | bytes 3145736 | tf_op jit(solution)/shard_map/q0_1/ppermute | solution.py:26
  85.3 26.5 %collective-permute-start.14 = (f32[4,2,128,256]{3,2,1,0:T(8,128)S(1)}, f32[4,2,128,256]{3,2,1,0:T(8,128)S(1)}, u32[]{:S(2)}, u32[]{:S(2)}) collective-permute-start(f32[4,2,128,256]{3,2,1,0:T(8,128)S(1)} %get-tuple-element.29), channel_id=1, source_target_pairs={{6,0},{3,1},{0,2},{5,3},{2,4},{7,5},{4,6},{1,7},{14,8},{11,9},{8,1... | collective-permute-start | bytes 3145736 | tf_op jit(solution)/shard_map/sb_0/ppermute | solution.py:26
  87.3 28.3 %collective-permute-start.19 = (f32[4,2,128,256]{3,2,1,0:T(8,128)S(1)}, f32[4,2,128,256]{3,2,1,0:T(8,128)S(1)}, u32[]{:S(2)}, u32[]{:S(2)}) collective-permute-start(f32[4,2,128,256]{3,2,1,0:T(8,128)S(1)} %get-tuple-element.31), channel_id=1, source_target_pairs={{1,0},{0,1},{3,2},{2,3},{5,4},{4,5},{7,6},{6,7},{9,8},{8,9},{11,10... | collective-permute-start | bytes 3145736 | tf_op jit(solution)/shard_map/rc_core_0/ppermute | solution.py:26
  87.4 28.8 %collective-permute-start.24 = (f32[4,2,128,256]{3,2,1,0:T(8,128)S(1)}, f32[4,2,128,256]{3,2,1,0:T(8,128)S(1)}, u32[]{:S(2)}, u32[]{:S(2)}) collective-permute-start(f32[4,2,128,256]{3,2,1,0:T(8,128)S(1)} %rows.3.first_ref.own_ref), channel_id=1, source_target_pairs={{28,4},{29,5},{30,6},{31,7},{4,12},{5,13},{6,14},{7,15},{12,20},{1... | collective-permute-start | bytes 3145736 | tf_op jit(solution)/shard_map/w_1/ppermute | solution.py:26
  111.9 16.1 %collective-permute-start.18 = (f32[4,2,128,256]{3,2,1,0:T(8,128)S(1)}, f32[4,2,128,256]{3,2,1,0:T(8,128)S(1)}, u32[]{:S(2)}, u32[]{:S(2)}) collective-permute-start(f32[4,2,128,256]{3,2,1,0:T(8,128)S(1)} %collective-permute-done.9.second_ref.refs_0_), channel_id=1, source_target_pairs={{2,0},{7,1},{4,2},{1,3},{6,4},{3,5},{0,6},{5,7},{10,8},{15,9},{12,... | collective-permute-start | bytes 3145736 | tf_op jit(solution)/shard_map/qa_1/ppermute | solution.py:26
  115.6 16.9 %collective-permute-start.36 = (f32[4,2,128,256]{3,2,1,0:T(8,128)S(1)}, f32[4,2,128,256]{3,2,1,0:T(8,128)S(1)}, u32[]{:S(2)}, u32[]{:S(2)}) collective-permute-start(f32[4,2,128,256]{3,2,1,0:T(8,128)S(1)} %collective-permute-done.9.second_ref.refs_0_), channel_id=1, source_target_pairs={{1,0},{0,1},{3,2},{2,3},{5,4},{4,5},{7,6},{6,7},{9,8},{8,9},{11,10... | collective-permute-start | bytes 3145736 | tf_op jit(solution)/shard_map/q0_core_1/ppermute | solution.py:26
  115.6 18.8 %collective-permute-start.34 = (f32[4,2,128,256]{3,2,1,0:T(8,128)S(1)}, f32[4,2,128,256]{3,2,1,0:T(8,128)S(1)}, u32[]{:S(2)}, u32[]{:S(2)}) collective-permute-start(f32[4,2,128,256]{3,2,1,0:T(8,128)S(1)} %collective-permute-done.10.refs_0_), channel_id=1, source_target_pairs={{1,0},{0,1},{3,2},{2,3},{5,4},{4,5},{7,6},{6,7},{9,8},{8,9},{11,10... | collective-permute-start | bytes 3145736 | tf_op jit(solution)/shard_map/sa_core_0/ppermute | solution.py:26
  116.2 27.1 %collective-permute-start.32 = (f32[4,2,128,256]{3,2,1,0:T(8,128)S(1)}, f32[4,2,128,256]{3,2,1,0:T(8,128)S(1)}, u32[]{:S(2)}, u32[]{:S(2)}) collective-permute-start(f32[4,2,128,256]{3,2,1,0:T(8,128)S(1)} %collective-permute-done.12.refs_2_), channel_id=1, source_target_pairs={{24,0},{25,1},{26,2},{27,3},{12,4},{13,5},{14,6},{15,7},{0,8},{1,9... | collective-permute-start | bytes 3145736 | tf_op jit(solution)/shard_map/x2_0/ppermute | solution.py:26
  118.0 25.2 %collective-permute-start.25 = (f32[4,2,128,256]{3,2,1,0:T(8,128)S(1)}, f32[4,2,128,256]{3,2,1,0:T(8,128)S(1)}, u32[]{:S(2)}, u32[]{:S(2)}) collective-permute-start(f32[4,2,128,256]{3,2,1,0:T(8,128)S(1)} %pick_1.1), channel_id=1, source_target_pairs={{8,0},{9,1},{10,2},{11,3},{28,4},{29,5},{30,6},{31,7},{16,8},{17,9... | collective-permute-start | bytes 3145736 | tf_op jit(solution)/shard_map/rc_1/ppermute | solution.py:26
  128.0 22.5 %collective-permute-start.30 = (f32[4,2,128,256]{3,2,1,0:T(8,128)S(1)}, f32[4,2,128,256]{3,2,1,0:T(8,128)S(1)}, u32[]{:S(2)}, u32[]{:S(2)}) collective-permute-start(f32[4,2,128,256]{3,2,1,0:T(8,128)S(1)} %collective-permute-done.9.second_ref.refs_0_), channel_id=1, source_target_pairs={{6,0},{3,1},{0,2},{5,3},{2,4},{7,5},{4,6},{1,7},{14,8},{11,9},{8,1... | collective-permute-start | bytes 3145736 | tf_op jit(solution)/shard_map/qb_1/ppermute | solution.py:26
  132.5 22.5 %collective-permute-start.35 = (f32[4,2,128,256]{3,2,1,0:T(8,128)S(1)}, f32[4,2,128,256]{3,2,1,0:T(8,128)S(1)}, u32[]{:S(2)}, u32[]{:S(2)}) collective-permute-start(f32[4,2,128,256]{3,2,1,0:T(8,128)S(1)} %collective-permute-done.14.refs_2_), channel_id=1, source_target_pairs={{1,0},{0,1},{3,2},{2,3},{5,4},{4,5},{7,6},{6,7},{9,8},{8,9},{11,10... | collective-permute-start | bytes 3145736 | tf_op jit(solution)/shard_map/sb_core_0/ppermute | solution.py:26
  134.4 21.2 %collective-permute-start.21 = (f32[4,2,128,256]{3,2,1,0:T(8,128)S(1)}, f32[4,2,128,256]{3,2,1,0:T(8,128)S(1)}, u32[]{:S(2)}, u32[]{:S(2)}) collective-permute-start(f32[4,2,128,256]{3,2,1,0:T(8,128)S(1)} %collective-permute-done.18.refs_0_), channel_id=1, source_target_pairs={{2,0},{7,1},{4,2},{1,3},{6,4},{3,5},{0,6},{5,7},{10,8},{15,9},{12,... | collective-permute-start | bytes 3145736 | tf_op jit(solution)/shard_map/q2_1/ppermute | solution.py:26
  143.2 17.0 %collective-permute-start.33 = (f32[4,2,128,256]{3,2,1,0:T(8,128)S(1)}, f32[4,2,128,256]{3,2,1,0:T(8,128)S(1)}, u32[]{:S(2)}, u32[]{:S(2)}) collective-permute-start(f32[4,2,128,256]{3,2,1,0:T(8,128)S(1)} %collective-permute-done.32.refs_0_), channel_id=1, source_target_pairs={{1,0},{0,1},{3,2},{2,3},{5,4},{4,5},{7,6},{6,7},{9,8},{8,9},{11,10... | collective-permute-start | bytes 3145736 | tf_op jit(solution)/shard_map/x2_core_0/ppermute | solution.py:26
  143.2 19.8 %collective-permute-start.29 = (f32[4,2,128,256]{3,2,1,0:T(8,128)S(1)}, f32[4,2,128,256]{3,2,1,0:T(8,128)S(1)}, u32[]{:S(2)}, u32[]{:S(2)}) collective-permute-start(f32[4,2,128,256]{3,2,1,0:T(8,128)S(1)} %collective-permute-done.18.refs_0_), channel_id=1, source_target_pairs={{1,0},{0,1},{3,2},{2,3},{5,4},{4,5},{7,6},{6,7},{9,8},{8,9},{11,10... | collective-permute-start | bytes 3145736 | tf_op jit(solution)/shard_map/qa_core_1/ppermute | solution.py:26
  155.0 17.3 %collective-permute-start.27 = (f32[4,2,128,256]{3,2,1,0:T(8,128)S(1)}, f32[4,2,128,256]{3,2,1,0:T(8,128)S(1)}, u32[]{:S(2)}, u32[]{:S(2)}) collective-permute-start(f32[4,2,128,256]{3,2,1,0:T(8,128)S(1)} %get-tuple-element.34), channel_id=1, source_target_pairs={{1,0},{0,1},{3,2},{2,3},{5,4},{4,5},{7,6},{6,7},{9,8},{8,9},{11,10... | collective-permute-start | bytes 3145736 | tf_op jit(solution)/shard_map/rc_core_1/ppermute | solution.py:26
  155.6 16.7 %collective-permute-start.28 = (f32[4,2,128,256]{3,2,1,0:T(8,128)S(1)}, f32[4,2,128,256]{3,2,1,0:T(8,128)S(1)}, u32[]{:S(2)}, u32[]{:S(2)}) collective-permute-start(f32[4,2,128,256]{3,2,1,0:T(8,128)S(1)} %collective-permute-done.21.refs_2_), channel_id=1, source_target_pairs={{1,0},{0,1},{3,2},{2,3},{5,4},{4,5},{7,6},{6,7},{9,8},{8,9},{11,10... | collective-permute-start | bytes 3145736 | tf_op jit(solution)/shard_map/q2_core_1/ppermute | solution.py:26
  160.3 26.0 %collective-permute-start.26 = (f32[4,2,128,256]{3,2,1,0:T(8,128)S(1)}, f32[4,2,128,256]{3,2,1,0:T(8,128)S(1)}, u32[]{:S(2)}, u32[]{:S(2)}) collective-permute-start(f32[4,2,128,256]{3,2,1,0:T(8,128)S(1)} %get-tuple-element.33), channel_id=1, source_target_pairs={{2,0},{7,1},{4,2},{1,3},{6,4},{3,5},{0,6},{5,7},{10,8},{15,9},{12,... | collective-permute-start | bytes 3145736 | tf_op jit(solution)/shard_map/sa_1/ppermute | solution.py:26
  163.1 24.0 %collective-permute-start.38 = (f32[4,2,128,256]{3,2,1,0:T(8,128)S(1)}, f32[4,2,128,256]{3,2,1,0:T(8,128)S(1)}, u32[]{:S(2)}, u32[]{:S(2)}) collective-permute-start(f32[4,2,128,256]{3,2,1,0:T(8,128)S(1)} %get-tuple-element.38), channel_id=1, source_target_pairs={{6,0},{3,1},{0,2},{5,3},{2,4},{7,5},{4,6},{1,7},{14,8},{11,9},{8,1... | collective-permute-start | bytes 3145736 | tf_op jit(solution)/shard_map/sb_1/ppermute | solution.py:26
  163.1 27.4 %collective-permute-start.22 = (f32[4,2,128,256]{3,2,1,0:T(8,128)S(1)}, f32[4,2,128,256]{3,2,1,0:T(8,128)S(1)}, u32[]{:S(2)}, u32[]{:S(2)}) collective-permute-start(f32[4,2,128,256]{3,2,1,0:T(8,128)S(1)} %collective-permute-done.21.refs_2_), channel_id=1, source_target_pairs={{24,0},{25,1},{26,2},{27,3},{12,4},{13,5},{14,6},{15,7},{0,8},{1,9... | collective-permute-start | bytes 3145736 | tf_op jit(solution)/shard_map/x2_1/ppermute | solution.py:26
  (8 other events, 67.7 us)

commit v2 on v1

--- a/solution.py
+++ b/solution.py
@@ -9,6 +9,10 @@
 
 CHUNKS = (4, 4)
 SIDE = 4
+
+ORDER = (('own', 0), ('q0', 0), ('w', 0), ('own', 1), ('qa', 0), ('qb', 0), ('rc', 0), ('q0x', 0), ('tiles', 0), ('q2', 0), ('q0', 1), ('w', 1), ('qax', 0), ('qbx', 0), ('tiles', 1), ('sa', 0), ('sb', 0), ('rcx', 0), ('q2x', 0), ('tiles', 2), ('qa', 1), ('x2', 0), ('q0x', 1), ('qb', 1), ('tiles', 3), ('rc', 1), ('q2', 1), ('sax', 0), ('sbx', 0), ('tiles', 4), ('x2x', 0), ('qax', 1), ('qbx', 1), ('sa', 1), ('sb', 1), ('rcx', 1), ('x2', 1), ('q2x', 1), ('tiles', 5), ('tiles', 6), ('tiles', 7), ('sax', 1), ('sbx', 1), ('tiles', 8), ('x2x', 1), ('tiles', 9))
+LATER = {('own', 1): (('own', 0),), ('qa', 0): (('own', 1),), ('qb', 0): (('own', 1),), ('q2', 0): (('tiles', 0),), ('q0', 1): (('rc', 0), ('tiles', 0)), ('w', 1): (('tiles', 0),), ('sb', 0): (('q2', 0), ('tiles', 1), ('w', 1)), ('qa', 1): (('tiles', 2), ('w', 1)), ('x2', 0): (('q0', 1), ('tiles', 2)), ('qb', 1): (('sa', 0), ('tiles', 2)), ('q2', 1): (('tiles', 3),), ('x2x', 0): (('tiles', 4),), ('sb', 1): (('q2', 1), ('tiles', 4)), ('x2', 1): (('tiles', 4),), ('sax', 1): (('tiles', 7),), ('sbx', 1): (('tiles', 7),)}
+KERNELS = ((0, ('q0', 'own')), (0, ('qa', 'qb')), (0, ('rc', 'q2')), (1, ('q0', 'own')), (0, ('sa', 'sb')), (0, ('x2',)), (1, ('qa', 'qb')), (1, ('rc', 'q2')), (1, ('sa', 'sb')), (1, ('x2',)))
 
 
 def place(x, z, core):
@@ -152,12 +156,12 @@
 
 
 def gather_kernel(info, *refs):
-    pieces, out_ref = refs[:SIDE], refs[SIDE]
+    pieces, keep_ref, out_ref = refs[:SIDE], refs[SIDE], refs[SIDE + 1]
     rows = pieces[0].shape[2]
     for shift in range(SIDE):
         source = lax.rem(info[0] + SIDE - shift, SIDE)
         start = pl.multiple_of(source * rows, rows)
-        out_ref[:, :, pl.ds(start, rows)] = pieces[shift][...]
+        out_ref[:, :, pl.ds(start, rows)] = pieces[shift][...] * keep_ref[pl.ds(start, rows)]
 
 
 def on_chip(kernel, info, values, shapes, name):
@@ -172,9 +176,9 @@
     )(info, *values)
 
 
-def gather_rows(info, pieces):
+def gather_rows(info, pieces, keep):
     count, parts, rows, samples = pieces[0].shape
-    return on_chip(gather_kernel, info, pieces, [(count, parts, rows * SIDE, samples)], "rows")[0]
+    return on_chip(gather_kernel, info, [*pieces, keep], [(count, parts, rows * SIDE, samples)], "rows")[0]
 
 
 def choose_kernel(rule, info, first_ref, second_ref, *outs):
@@ -202,6 +206,33 @@
     up = z == SIDE - 1
     first = core == 0
     return [jnp.where(first, down, up), jnp.where(first, up, down), core == 1]
+
+
+KINDS = {
+    "q0": ("ahead", 0, 0),
+    "qa": ("ahead", 1, 3),
+    "qb": ("ahead", 3, 1),
+    "q2": ("ahead", 2, 2),
+    "rc": ("two", 0, 0),
+    "sa": ("row", 1, 3),
+    "sb": ("row", 3, 1),
+    "x2": ("row", 2, 2),
+}
+PATHS = {
+    "q0": lambda x, z, c: (x + 1, z, c),
+    "w": lambda x, z, c: (x - 1, z, c) if z >= 2 else None,
+    "rc": lambda x, z, c: (x - 1, z, c) if z >= 2 else (x + 1, z, c),
+    "qa": lambda x, z, c: (x, z + side(c, False), c),
+    "qb": lambda x, z, c: (x, z + side(c, True), c),
+    "q2": lambda x, z, c: (x, z + side(c, False), c),
+    "sa": lambda x, z, c: (x, z + side(c, False), c),
+    "sb": lambda x, z, c: (x, z + side(c, True), c),
+    "x2": lambda x, z, c: (x - 1, z, c) if z <= 1 else (x + 1, z, c),
+}
+
+
+def other_core(x, z, c):
+    return x, z, 1 - c
 
 
 def shards(voltages, pair_table, bad_feeds):
@@ -212,137 +243,74 @@
     group = channels // freq_count
     width = rows * freq_count
 
-    inputs = here * width + freq * rows + jnp.arange(rows, dtype=jnp.int32)
+    inputs = here * width + jnp.arange(width, dtype=jnp.int32)
     flagged = jnp.any((inputs // 2)[:, None] == bad_feeds[None, :], axis=-1)
     keep = jnp.where(flagged, 0.0, 1.0).astype(jnp.float32)[:, None]
+    keep = jnp.broadcast_to(keep, (width, samples))
     info = jnp.concatenate([here[None], pair_table[:, 0]])
-    freq_info = freq[None]
     shape = (pair_table.shape[0], group, parts, width, width)
     firsts = [sum(CHUNKS[:number]) for number in range(len(CHUNKS))]
-
-    def corner_turn(number, *earlier):
+    done = {}
+    picked = {}
+
+    def corner_turn(number, earlier):
         count = CHUNKS[number]
-        with jax.named_scope(f"turn_{number}"):
-
-            def piece(shift):
-                start = ((freq + shift) % freq_count) * group + firsts[number]
-                return lax.dynamic_slice_in_dim(voltages[0], start, count, 0) * keep
-
-            pieces = [piece(0)]
-            for shift in (1, 2, 3):
-                pairs = [(source, (source + shift) % freq_count) for source in range(freq_count)]
-                pieces.append(lax.ppermute(after(piece(shift), *earlier), "freq", pairs))
-            return gather_rows(freq_info, pieces)
-
-    def scoped(name, number, value, source_of):
-        with jax.named_scope(f"{name}_{number}"):
-            return fetch(value, source_of)
-
-    def exchange(name, number, value):
-        return scoped(name + "_core", number, value, lambda x, z, c: (x, z, 1 - c))
-
-    def get_q0(number, own, *earlier):
-        own = after(own, *earlier)
-        q0 = scoped("q0", number, own, lambda x, z, c: (x + 1, z, c))
-        w = scoped("w", number, own, lambda x, z, c: (x - 1, z, c) if z >= 2 else None)
-        return q0, w
-
-    def get_row(number, q0, *earlier):
-        q0 = after(q0, *earlier)
-        qa = scoped("qa", number, q0, lambda x, z, c: (x, z + side(c, False), c))
-        qb = scoped("qb", number, q0, lambda x, z, c: (x, z + side(c, True), c))
-        return qa, qb
-
-    def get_q2(number, qa, *earlier):
-        return scoped("q2", number, after(qa, *earlier), lambda x, z, c: (x, z + side(c, False), c))
-
-    def get_rc(number, q0, w, *earlier):
-        source = choose(far_column, 1, info, after(w, *earlier), q0, f"pick_{number}")[0]
-        return scoped(
-            "rc", number, source, lambda x, z, c: (x - 1, z, c) if z >= 2 else (x + 1, z, c)
+
+        def piece(shift):
+            start = ((freq + shift) % freq_count) * group + firsts[number]
+            return lax.dynamic_slice_in_dim(voltages[0], start, count, 0)
+
+        pieces = [piece(0)]
+        for shift in (1, 2, 3):
+            pairs = [(source, (source + shift) % freq_count) for source in range(freq_count)]
+            pieces.append(lax.ppermute(after(piece(shift), *earlier), "freq", pairs))
+        return gather_rows(freq[None], pieces, keep)
+
+    def pick(number):
+        if number not in picked:
+            picked[number] = choose(
+                row_sources, 3, info, done["own", number], done["rc", number], f"pick3_{number}"
+            )
+        return picked[number]
+
+    def tiles(visibility, index, number, items):
+        slots, fars = [], []
+        for name in items:
+            if name == "own":
+                slots.append(("own", 0, 0, False))
+                continue
+            slots.append((*KINDS[name], False))
+            fars.append(done[name, number])
+            slots.append(("mixed", 0, 0, False) if name == "rc" else (*KINDS[name], True))
+            fars.append(done[name + "x", number])
+        slots.sort(key=lambda slot: slot[0] == "own")
+        return correlate(
+            visibility, shape, info, done["own", number], fars, slots, firsts[number], f"tiles_k{index}"
         )
 
-    def get_s(number, own, rc, *earlier):
-        to_a, to_b, to_mixed = choose(row_sources, 3, info, own, rc, f"pick3_{number}")
-        sa = scoped("sa", number, to_a, lambda x, z, c: (x, z + side(c, False), c))
-        sb = scoped("sb", number, after(to_b, *earlier), lambda x, z, c: (x, z + side(c, True), c))
-        return sa, sb, exchange("rc", number, to_mixed)
-
-    def get_x2(number, q2, *earlier):
-        return scoped(
-            "x2", number, after(q2, *earlier), lambda x, z, c: (x - 1, z, c) if z <= 1 else (x + 1, z, c)
-        )
-
-    def tiles(visibility, number, own, fars, slots, label):
-        return correlate(
-            visibility, shape, info, own, fars, slots, firsts[number], f"tiles_{label}_{number}"
-        )
-
-    near = ("ahead", 1, 3)
-    away = ("ahead", 3, 1)
-    same = ("ahead", 0, 0)
-    twice = ("ahead", 2, 2)
-
-    def with_other(slot):
-        return [(*slot, False), (*slot, True)]
-
-    def group_1(visibility, number, own, q0, q0_other):
-        slots = with_other(same) + [("own", 0, 0, False)]
-        return tiles(visibility, number, own, [q0, q0_other], slots, "g1")
-
-    def group_2(visibility, number, own, qa, qa_other, qb, qb_other):
-        slots = with_other(near) + with_other(away)
-        return tiles(visibility, number, own, [qa, qa_other, qb, qb_other], slots, "g2")
-
-    def group_3(visibility, number, own, rc, mixed, q2, q2_other):
-        slots = [("two", 0, 0, False), ("mixed", 0, 0, False)] + with_other(twice)
-        return tiles(visibility, number, own, [rc, mixed, q2, q2_other], slots, "g3")
-
-    def group_4(visibility, number, own, sa, sa_other, sb, sb_other):
-        slots = with_other(("row", 1, 3)) + with_other(("row", 3, 1))
-        return tiles(visibility, number, own, [sa, sa_other, sb, sb_other], slots, "g4")
-
-    def group_5(visibility, number, own, x2, x2_other):
-        return tiles(visibility, number, own, [x2, x2_other], with_other(("row", 2, 2)), "g5")
-
-    own_0 = corner_turn(0)
-    q0_0, w_0 = get_q0(0, own_0)
-    own_1 = corner_turn(1, own_0)
-    qa_0, qb_0 = get_row(0, q0_0, own_1)
-    rc_0 = get_rc(0, q0_0, w_0)
-    q0_0x = exchange("q0", 0, q0_0)
-    q2_0 = get_q2(0, qa_0)
-    vis = group_1(None, 0, own_0, q0_0, q0_0x)
-    q0_1, w_1 = get_q0(1, own_1, rc_0)
-    sa_0, sb_0, mixed_0 = get_s(0, own_0, rc_0, q2_0, vis)
-    qa_0x = exchange("qa", 0, qa_0)
-    qb_0x = exchange("qb", 0, qb_0)
-    q2_0x = exchange("q2", 0, q2_0)
-    vis = group_2(vis, 0, own_0, qa_0, qa_0x, qb_0, qb_0x)
-    qa_1, qb_1 = get_row(1, q0_1, sa_0, sb_0, vis)
-    rc_1 = get_rc(1, q0_1, w_1)
-    x2_0 = get_x2(0, q2_0, q0_1)
-    q0_1x = exchange("q0", 1, q0_1)
-    vis = group_3(vis, 0, own_0, rc_0, mixed_0, q2_0, q2_0x)
-    sa_0x = exchange("sa", 0, sa_0)
-    sb_0x = exchange("sb", 0, sb_0)
-    q2_1 = get_q2(1, qa_1, vis)
-    vis = group_1(vis, 1, own_1, q0_1, q0_1x)
-    vis = group_4(vis, 0, own_0, sa_0, sa_0x, sb_0, sb_0x)
-    sa_1, sb_1, mixed_1 = get_s(1, own_1, rc_1, q2_1, vis)
-    qa_1x = exchange("qa", 1, qa_1)
-    qb_1x = exchange("qb", 1, qb_1)
-    x2_0x = exchange("x2", 0, x2_0)
-    x2_1 = get_x2(1, q2_1)
-    q2_1x = exchange("q2", 1, q2_1)
-    vis = group_5(vis, 0, own_0, x2_0, x2_0x)
-    vis = group_2(vis, 1, own_1, qa_1, qa_1x, qb_1, qb_1x)
-    vis = group_3(vis, 1, own_1, rc_1, mixed_1, q2_1, q2_1x)
-    sa_1x = exchange("sa", 1, after(sa_1, vis))
-    sb_1x = exchange("sb", 1, sb_1)
-    vis = group_4(vis, 1, own_1, sa_1, sa_1x, sb_1, sb_1x)
-    x2_1x = exchange("x2", 1, x2_1)
-    return group_5(vis, 1, own_1, x2_1, x2_1x)
+    def step(name, number):
+        earlier = [done[other] for other in LATER.get((name, number), ())]
+        if name == "own":
+            return corner_turn(number, earlier)
+        if name == "rc":
+            value = choose(far_column, 1, info, done["w", number], done["q0", number], f"pick_{number}")[0]
+        elif name in ("sa", "sb", "rcx"):
+            value = pick(number)[("sa", "sb", "rcx").index(name)]
+        elif name.endswith("x") and name != "x2":
+            value = done[name[:-1], number]
+        else:
+            value = done[{"q0": "own", "w": "own", "qa": "q0", "qb": "q0", "q2": "qa", "x2": "q2"}[name], number]
+        return fetch(after(value, *earlier), PATHS.get(name, other_core))
+
+    visibility = None
+    for name, number in ORDER:
+        with jax.named_scope(f"n_{name}_{number}"):
+            if name == "tiles":
+                visibility = tiles(visibility, number, *KERNELS[number])
+                done[name, number] = visibility
+            else:
+                done[name, number] = step(name, number)
+    return visibility
 
 
 def solution(mesh):

time: 201 us -> 195 us (0.970)
  starting transfers between devices: 52.7 us -> 48.6 us
    ppermute x6, waiting for transfers between devices: 22.3 us -> 9.53 us  [corner_turn(): pieces.append(lax.ppermute(after(piece(shift), *earlier), 'freq', pairs))]
    ppermute x34, waiting for transfers between devices: 75.2 us -> 86.6 us  [fetch(): return lax.ppermute(value, 'blk', pairs)]
    ppermute x34, starting transfers between devices: 42.7 us -> 38.5 us  [fetch(): return lax.ppermute(value, 'blk', pairs)]
  transfers between devices with their start and end apart: 40 -> 40, of which waited for: 14 -> 14; matrix products, arithmetic and copies ran while one was open for 0% -> 1% of each run, Pallas kernels for 21% -> 21%
where the time goes in v2:
time: 195 us; the launch traced here: 193 us
  waiting for transfers between devices  96.1 us (49%)
  starting transfers between devices  48.6 us (25%)
  Pallas kernels  44.8 us (23%)
  local copies, waits for them, and re-layouts  2.4 us (1%)
    ppermute x34, waiting for transfers between devices, fetch(): return lax.ppermute(value, 'blk', pairs)  86.6 us
    pallas_call x10, Pallas kernels, correlate(): pl.pallas_call(functools.partial(tiles_kernel, slots, first), in_specs=[p...  41.7 us
    ppermute x34, starting transfers between devices, fetch(): return lax.ppermute(value, 'blk', pairs)  38.5 us
    ppermute x6, starting transfers between devices, corner_turn(): pieces.append(lax.ppermute(after(piece(shift), *earlier), 'freq', pairs))  10 us
    ppermute x6, waiting for transfers between devices, corner_turn(): pieces.append(lax.ppermute(after(piece(shift), *earlier), 'freq', pairs))  9.53 us
  transfers between devices with their start and end apart: 40, of which 14 were waited for; matrix products, arithmetic and copies ran while one was open for 1% of the time, Pallas kernels for 21%

profile of v2, /device:TPU:0, one launch (start us, length us, event | category | flops | bytes accessed | tf_op | source)
XLA Modules:
  0.0 193.2 jit_solution(15369037398611528780)
XLA Ops:
  1.7 1.7 collective-permute-start
  3.4 2.9 %collective-permute-start.1 = (f32[4,2,32,256]{3,2,1,0:T(8,128)S(1)}, f32[4,2,32,256]{3,2,1,0:T(8,128)S(1)}, u32[]{:S(2)}, u32[]{:S(2)}) collective-permute-start(f32[4,2,32,256]{3,2,1,0:T(8,128)S(1)} %get-tuple-element.53), channel_id=1, source_target_pairs={{0,64},{32,96},{64,0},{96,32},{1,65},{33,97},{65,1},{97,33},{2,66}... | collective-permute-start | bytes 786440 | tf_op jit(solution)/shard_map/n_own_0/ppermute | solution.py:266
  8.4 2.7 %collective-permute-done.refs_1_ = f32[4,2,32,256]{3,2,1,0:T(8,128)S(1)} collective-permute-done((f32[4,2,32,256]{3,2,1,0:T(8,128)S(1)}, f32[4,2,32,256]{3,2,1,0:T(8,128)S(1)}, u32[]{:S(2)}, u32[]{:S(2)}) %collective-permute-start) | collective-permute-done | bytes 262176 | tf_op jit(solution)/shard_map/n_own_0/ppermute | solution.py:266
  11.1 6.8 %collective-permute-done.1.refs_2_ = f32[4,2,32,256]{3,2,1,0:T(8,128)S(1)} collective-permute-done((f32[4,2,32,256]{3,2,1,0:T(8,128)S(1)}, f32[4,2,32,256]{3,2,1,0:T(8,128)S(1)}, u32[]{:S(2)}, u32[]{:S(2)}) %collective-permute-start.1) | collective-permute-done | bytes 262176 | tf_op jit(solution)/shard_map/n_own_0/ppermute | solution.py:266
  18.1 2.8 %collective-permute-start.7 = (f32[4,2,128,256]{3,2,1,0:T(8,128)S(1)}, f32[4,2,128,256]{3,2,1,0:T(8,128)S(1)}, u32[]{:S(2)}, u32[]{:S(2)}) collective-permute-start(f32[4,2,128,256]{3,2,1,0:T(8,128)S(1)} %rows.2.own_ref.first_ref), channel_id=1, source_target_pairs={{8,0},{9,1},{10,2},{11,3},{12,4},{13,5},{14,6},{15,7},{16,8},{17,9... | collective-permute-start | bytes 3145736 | tf_op jit(solution)/shard_map/n_q0_0/ppermute | solution.py:30
  21.6 2.2 %collective-permute-start.5 = (f32[4,2,32,256]{3,2,1,0:T(8,128)S(1)}, f32[4,2,32,256]{3,2,1,0:T(8,128)S(1)}, u32[]{:S(2)}, u32[]{:S(2)}) collective-permute-start(f32[4,2,32,256]{3,2,1,0:T(8,128)S(1)} %get-tuple-element.30), channel_id=1, source_target_pairs={{0,96},{32,0},{64,32},{96,64},{1,97},{33,1},{65,33},{97,65},{2,98}... | collective-permute-start | bytes 786440 | tf_op jit(solution)/shard_map/n_own_1/ppermute | solution.py:266
  25.7 16.8 %collective-permute-done.7.second_ref.refs_0_ = f32[4,2,128,256]{3,2,1,0:T(8,128)S(1)} collective-permute-done((f32[4,2,128,256]{3,2,1,0:T(8,128)S(1)}, f32[4,2,128,256]{3,2,1,0:T(8,128)S(1)}, u32[]{:S(2)}, u32[]{:S(2)}) %collective-permute-start.7) | collective-permute-done | bytes 1048608 | tf_op jit(solution)/shard_map/n_q0_0/ppermute | solution.py:30
  42.6 4.1 %collective-permute-start.12 = (f32[4,2,128,256]{3,2,1,0:T(8,128)S(1)}, f32[4,2,128,256]{3,2,1,0:T(8,128)S(1)}, u32[]{:S(2)}, u32[]{:S(2)}) collective-permute-start(f32[4,2,128,256]{3,2,1,0:T(8,128)S(1)} %collective-permute-done.7.second_ref.refs_0_), channel_id=1, source_target_pairs={{2,0},{7,1},{4,2},{1,3},{6,4},{3,5},{0,6},{5,7},{10,8},{15,9},{12,... | collective-permute-start | bytes 3145736 | tf_op jit(solution)/shard_map/n_qa_0/ppermute | solution.py:30
  48.1 3.8 %collective-permute-start.8 = (f32[4,2,128,256]{3,2,1,0:T(8,128)S(1)}, f32[4,2,128,256]{3,2,1,0:T(8,128)S(1)}, u32[]{:S(2)}, u32[]{:S(2)}) collective-permute-start(f32[4,2,128,256]{3,2,1,0:T(8,128)S(1)} %pick_0.1), channel_id=1, source_target_pairs={{8,0},{9,1},{10,2},{11,3},{28,4},{29,5},{30,6},{31,7},{16,8},{17,9... | collective-permute-start | bytes 3145736 | tf_op jit(solution)/shard_map/n_rc_0/ppermute | solution.py:30
  51.8 3.8 %tiles_k0.1.refs_4_ = f32[17,8,2,128,128]{4,3,2,1,0:T(8,128)} custom-call(s32[18]{0:T(128)S(1)} %pad_add_fusion.info, f32[4,2,128,256]{3,2,1,0:T(8,128)S(1)} %rows.2.own_ref.first_ref, f32[4,2,128,256]{3,2,1,0:T(8,128)S(1)} %collective-permute-done.7.second_ref.refs_0_, f32[4,2,128,256]{3,2,1,0:T(8,128)S(1)} %collective-permute-done.9.refs_1_), custom_call_target="tpu_custom_call" | custom-call | flops 1207959552 | bytes 4718592 | tf_op jit(solution)/shard_map/n_tiles_0/tiles_k0/pallas_call | solution.py:138
  55.6 14.2 %collective-permute-done.12.refs_0_ = f32[4,2,128,256]{3,2,1,0:T(8,128)S(1)} collective-permute-done((f32[4,2,128,256]{3,2,1,0:T(8,128)S(1)}, f32[4,2,128,256]{3,2,1,0:T(8,128)S(1)}, u32[]{:S(2)}, u32[]{:S(2)}) %collective-permute-start.12) | collective-permute-done | bytes 1048608 | tf_op jit(solution)/shard_map/n_qa_0/ppermute | solution.py:30
  69.9 3.7 %collective-permute-start.13 = (f32[4,2,128,256]{3,2,1,0:T(8,128)S(1)}, f32[4,2,128,256]{3,2,1,0:T(8,128)S(1)}, u32[]{:S(2)}, u32[]{:S(2)}) collective-permute-start(f32[4,2,128,256]{3,2,1,0:T(8,128)S(1)} %collective-permute-done.12.refs_0_), channel_id=1, source_target_pairs={{2,0},{7,1},{4,2},{1,3},{6,4},{3,5},{0,6},{5,7},{10,8},{15,9},{12,... | collective-permute-start | bytes 3145736 | tf_op jit(solution)/shard_map/n_q2_0/ppermute | solution.py:30
  74.8 3.8 %collective-permute-start.10 = (f32[4,2,128,256]{3,2,1,0:T(8,128)S(1)}, f32[4,2,128,256]{3,2,1,0:T(8,128)S(1)}, u32[]{:S(2)}, u32[]{:S(2)}) collective-permute-start(f32[4,2,128,256]{3,2,1,0:T(8,128)S(1)} %rows.3.own_ref.first_ref), channel_id=1, source_target_pairs={{8,0},{9,1},{10,2},{11,3},{12,4},{13,5},{14,6},{15,7},{16,8},{17,9... | collective-permute-start | bytes 3145736 | tf_op jit(solution)/shard_map/n_q0_1/ppermute | solution.py:30
  79.3 6.5 %collective-permute-done.13.refs_2_ = f32[4,2,128,256]{3,2,1,0:T(8,128)S(1)} collective-permute-done((f32[4,2,128,256]{3,2,1,0:T(8,128)S(1)}, f32[4,2,128,256]{3,2,1,0:T(8,128)S(1)}, u32[]{:S(2)}, u32[]{:S(2)}) %collective-permute-start.13) | collective-permute-done | bytes 1048608 | tf_op jit(solution)/shard_map/n_q2_0/ppermute | solution.py:30
  86.4 3.7 %collective-permute-start.22 = (f32[4,2,128,256]{3,2,1,0:T(8,128)S(1)}, f32[4,2,128,256]{3,2,1,0:T(8,128)S(1)}, u32[]{:S(2)}, u32[]{:S(2)}) collective-permute-start(f32[4,2,128,256]{3,2,1,0:T(8,128)S(1)} %get-tuple-element.38), channel_id=1, source_target_pairs={{2,0},{7,1},{4,2},{1,3},{6,4},{3,5},{0,6},{5,7},{10,8},{15,9},{12,... | collective-permute-start | bytes 3145736 | tf_op jit(solution)/shard_map/n_sa_0/ppermute | solution.py:30
  90.1 4.5 %tiles_k1.1.refs_4_ = f32[17,8,2,128,128]{4,3,2,1,0:T(8,128)} custom-call(s32[18]{0:T(128)S(1)} %pad_add_fusion.info, f32[4,2,128,256]{3,2,1,0:T(8,128)S(1)} %rows.2.own_ref.first_ref, f32[4,2,128,256]{3,2,1,0:T(8,128)S(1)} %collective-permute-done.12.refs_0_, ...), custom_call_target="tpu_custom_call", output_to_operand_aliasing={{}: (6, {})} | custom-call | flops 1610612736 | bytes 7340032 | tf_op jit(solution)/shard_map/n_tiles_1/tiles_k1/pallas_call | solution.py:138
  94.7 6.4 %collective-permute-done.10.refs_0_.second_ref = f32[4,2,128,256]{3,2,1,0:T(8,128)S(1)} collective-permute-done((f32[4,2,128,256]{3,2,1,0:T(8,128)S(1)}, f32[4,2,128,256]{3,2,1,0:T(8,128)S(1)}, u32[]{:S(2)}, u32[]{:S(2)}) %collective-permute-start.10) | collective-permute-done | bytes 1048608 | tf_op jit(solution)/shard_map/n_q0_1/ppermute | solution.py:30
  102.3 4.5 %tiles_k2.1.refs_2_ = f32[17,8,2,128,128]{4,3,2,1,0:T(8,128)} custom-call(s32[18]{0:T(128)S(1)} %pad_add_fusion.info, f32[4,2,128,256]{3,2,1,0:T(8,128)S(1)} %rows.2.own_ref.first_ref, f32[4,2,128,256]{3,2,1,0:T(8,128)S(1)} %collective-permute-done.8.second_ref.refs_0_, ...), custom_call_target="tpu_custom_call", output_to_operand_aliasing={{}: (6, {})} | custom-call | flops 1610612736 | bytes 7340032 | tf_op jit(solution)/shard_map/n_tiles_2/tiles_k2/pallas_call | solution.py:138
  108.6 12.2 %collective-permute-done.24.refs_2_ = f32[4,2,128,256]{3,2,1,0:T(8,128)S(1)} collective-permute-done((f32[4,2,128,256]{3,2,1,0:T(8,128)S(1)}, f32[4,2,128,256]{3,2,1,0:T(8,128)S(1)}, u32[]{:S(2)}, u32[]{:S(2)}) %collective-permute-start.24) | collective-permute-done | bytes 1048608 | tf_op jit(solution)/shard_map/n_sb_0/ppermute | solution.py:30
  121.7 3.8 %tiles_k3.1.refs_4_ = f32[17,8,2,128,128]{4,3,2,1,0:T(8,128)} custom-call(s32[18]{0:T(128)S(1)} %pad_add_fusion.info, f32[4,2,128,256]{3,2,1,0:T(8,128)S(1)} %rows.3.own_ref.first_ref, f32[4,2,128,256]{3,2,1,0:T(8,128)S(1)} %collective-permute-done.10.refs_0_.second_ref, ...), custom_call_target="tpu_custom_call", output_to_operand_aliasing={{}: (4, {})} | custom-call | flops 1207959552 | bytes 4718592 | tf_op jit(solution)/shard_map/n_tiles_3/tiles_k3/pallas_call | solution.py:138
  125.5 4.8 %collective-permute-start.28 = (f32[4,2,128,256]{3,2,1,0:T(8,128)S(1)}, f32[4,2,128,256]{3,2,1,0:T(8,128)S(1)}, u32[]{:S(2)}, u32[]{:S(2)}) collective-permute-start(f32[4,2,128,256]{3,2,1,0:T(8,128)S(1)} %pick_1.1), channel_id=1, source_target_pairs={{8,0},{9,1},{10,2},{11,3},{28,4},{29,5},{30,6},{31,7},{16,8},{17,9... | collective-permute-start | bytes 3145736 | tf_op jit(solution)/shard_map/n_rc_1/ppermute | solution.py:30
  131.3 4.5 %tiles_k4.1.refs_2_ = f32[17,8,2,128,128]{4,3,2,1,0:T(8,128)} custom-call(s32[18]{0:T(128)S(1)} %pad_add_fusion.info, f32[4,2,128,256]{3,2,1,0:T(8,128)S(1)} %rows.2.own_ref.first_ref, f32[4,2,128,256]{3,2,1,0:T(8,128)S(1)} %collective-permute-done.22.refs_0_, ...), custom_call_target="tpu_custom_call", output_to_operand_aliasing={{}: (6, {})} | custom-call | flops 1610612736 | bytes 7340032 | tf_op jit(solution)/shard_map/n_tiles_4/tiles_k4/pallas_call | solution.py:138
  135.9 11.7 %collective-permute-done.35.refs_0_ = f32[4,2,128,256]{3,2,1,0:T(8,128)S(1)} collective-permute-done((f32[4,2,128,256]{3,2,1,0:T(8,128)S(1)}, f32[4,2,128,256]{3,2,1,0:T(8,128)S(1)}, u32[]{:S(2)}, u32[]{:S(2)}) %collective-permute-start.35) | collective-permute-done | bytes 1048608 | tf_op jit(solution)/shard_map/n_x2_0/ppermute | solution.py:30
  148.1 5.5 %collective-permute-done.28.second_ref.refs_0_ = f32[4,2,128,256]{3,2,1,0:T(8,128)S(1)} collective-permute-done((f32[4,2,128,256]{3,2,1,0:T(8,128)S(1)}, f32[4,2,128,256]{3,2,1,0:T(8,128)S(1)}, u32[]{:S(2)}, u32[]{:S(2)}) %collective-permute-start.28) | collective-permute-done | bytes 1048608 | tf_op jit(solution)/shard_map/n_rc_1/ppermute | solution.py:30
  155.0 3.7 %collective-permute-start.29 = (f32[4,2,128,256]{3,2,1,0:T(8,128)S(1)}, f32[4,2,128,256]{3,2,1,0:T(8,128)S(1)}, u32[]{:S(2)}, u32[]{:S(2)}) collective-permute-start(f32[4,2,128,256]{3,2,1,0:T(8,128)S(1)} %get-tuple-element.42), channel_id=1, source_target_pairs={{2,0},{7,1},{4,2},{1,3},{6,4},{3,5},{0,6},{5,7},{10,8},{15,9},{12,... | collective-permute-start | bytes 3145736 | tf_op jit(solution)/shard_map/n_sa_1/ppermute | solution.py:30
  158.7 3.4 %tiles_k5.1.refs_4_ = f32[17,8,2,128,128]{4,3,2,1,0:T(8,128)} custom-call(s32[18]{0:T(128)S(1)} %pad_add_fusion.info, f32[4,2,128,256]{3,2,1,0:T(8,128)S(1)} %rows.2.own_ref.first_ref, f32[4,2,128,256]{3,2,1,0:T(8,128)S(1)} %collective-permute-done.35.refs_0_, ...), custom_call_target="tpu_custom_call", output_to_operand_aliasing={{}: (4, {})} | custom-call | flops 805306368 | bytes 4194304 | tf_op jit(solution)/shard_map/n_tiles_5/tiles_k5/pallas_call | solution.py:138
  162.1 4.5 %tiles_k6.1.refs_4_ = f32[17,8,2,128,128]{4,3,2,1,0:T(8,128)} custom-call(s32[18]{0:T(128)S(1)} %pad_add_fusion.info, f32[4,2,128,256]{3,2,1,0:T(8,128)S(1)} %rows.3.own_ref.first_ref, f32[4,2,128,256]{3,2,1,0:T(8,128)S(1)} %collective-permute-done.19.refs_0_, ...), custom_call_target="tpu_custom_call", output_to_operand_aliasing={{}: (6, {})} | custom-call | flops 1610612736 | bytes 7340032 | tf_op jit(solution)/shard_map/n_tiles_6/tiles_k6/pallas_call | solution.py:138
  166.7 4.5 %tiles_k7.1.refs_4_ = f32[17,8,2,128,128]{4,3,2,1,0:T(8,128)} custom-call(s32[18]{0:T(128)S(1)} %pad_add_fusion.info, f32[4,2,128,256]{3,2,1,0:T(8,128)S(1)} %rows.3.own_ref.first_ref, f32[4,2,128,256]{3,2,1,0:T(8,128)S(1)} %collective-permute-done.28.second_ref.refs_0_, ...), custom_call_target="tpu_custom_call", output_to_operand_aliasing={{}: (6, {})} | custom-call | flops 1610612736 | bytes 7340032 | tf_op jit(solution)/shard_map/n_tiles_7/tiles_k7/pallas_call | solution.py:138
  171.2 9.2 %collective-permute-done.38.refs_2_ = f32[4,2,128,256]{3,2,1,0:T(8,128)S(1)} collective-permute-done((f32[4,2,128,256]{3,2,1,0:T(8,128)S(1)}, f32[4,2,128,256]{3,2,1,0:T(8,128)S(1)}, u32[]{:S(2)}, u32[]{:S(2)}) %collective-permute-start.38) | collective-permute-done | bytes 1048608 | tf_op jit(solution)/shard_map/n_sb_1/ppermute | solution.py:30
  182.7 2.0 %collective-permute-done.26.refs_0_ = f32[4,2,128,256]{3,2,1,0:T(8,128)S(1)} collective-permute-done((f32[4,2,128,256]{3,2,1,0:T(8,128)S(1)}, f32[4,2,128,256]{3,2,1,0:T(8,128)S(1)}, u32[]{:S(2)}, u32[]{:S(2)}) %collective-permute-start.26) | collective-permute-done | bytes 1048608 | tf_op jit(solution)/shard_map/n_x2_1/ppermute | solution.py:30
  185.0 4.5 %tiles_k8.1.refs_2_ = f32[17,8,2,128,128]{4,3,2,1,0:T(8,128)} custom-call(s32[18]{0:T(128)S(1)} %pad_add_fusion.info, f32[4,2,128,256]{3,2,1,0:T(8,128)S(1)} %rows.3.own_ref.first_ref, f32[4,2,128,256]{3,2,1,0:T(8,128)S(1)} %collective-permute-done.29.refs_0_, ...), custom_call_target="tpu_custom_call", output_to_operand_aliasing={{}: (6, {})} | custom-call | flops 1610612736 | bytes 7340032 | tf_op jit(solution)/shard_map/n_tiles_8/tiles_k8/pallas_call | solution.py:138
  189.6 3.4 %tiles_k9.1 = f32[17,8,2,128,128]{4,3,2,1,0:T(8,128)} custom-call(s32[18]{0:T(128)S(1)} %pad_add_fusion.info, f32[4,2,128,256]{3,2,1,0:T(8,128)S(1)} %rows.3.own_ref.first_ref, f32[4,2,128,256]{3,2,1,0:T(8,128)S(1)} %collective-permute-done.26.refs_0_, f32[4,2,128,256]{3,2,1,0:T(8,128)S(1)} %collective-permute-done.27.refs_1_, ...), custom_call_target="tpu_custom_call", output_to_operand_aliasing={{}: (4, {})} | custom-call | flops 805306368 | bytes 4194304 | tf_op jit(solution)/shard_map/n_tiles_9/tiles_k9/pallas_call | solution.py:138
  (71 shorter events, 19.8 us)
Async XLA Ops:
  3.4 14.5 %collective-permute-start.1 = (f32[4,2,32,256]{3,2,1,0:T(8,128)S(1)}, f32[4,2,32,256]{3,2,1,0:T(8,128)S(1)}, u32[]{:S(2)}, u32[]{:S(2)}) collective-permute-start(f32[4,2,32,256]{3,2,1,0:T(8,128)S(1)} %get-tuple-element.53), channel_id=1, source_target_pairs={{0,64},{32,96},{64,0},{96,32},{1,65},{33,97},{65,1},{97,33},{2,66}... | collective-permute-start | bytes 786440 | tf_op jit(solution)/shard_map/n_own_0/ppermute | solution.py:266
  6.3 11.6 %collective-permute-start.2 = (f32[4,2,32,256]{3,2,1,0:T(8,128)S(1)}, f32[4,2,32,256]{3,2,1,0:T(8,128)S(1)}, u32[]{:S(2)}, u32[]{:S(2)}) collective-permute-start(f32[4,2,32,256]{3,2,1,0:T(8,128)S(1)} %get-tuple-element.52), channel_id=1, source_target_pairs={{0,96},{32,0},{64,32},{96,64},{1,97},{33,1},{65,33},{97,65},{2,98}... | collective-permute-start | bytes 786440 | tf_op jit(solution)/shard_map/n_own_0/ppermute | solution.py:266
  18.1 24.4 %collective-permute-start.7 = (f32[4,2,128,256]{3,2,1,0:T(8,128)S(1)}, f32[4,2,128,256]{3,2,1,0:T(8,128)S(1)}, u32[]{:S(2)}, u32[]{:S(2)}) collective-permute-start(f32[4,2,128,256]{3,2,1,0:T(8,128)S(1)} %rows.2.own_ref.first_ref), channel_id=1, source_target_pairs={{8,0},{9,1},{10,2},{11,3},{12,4},{13,5},{14,6},{15,7},{16,8},{17,9... | collective-permute-start | bytes 3145736 | tf_op jit(solution)/shard_map/n_q0_0/ppermute | solution.py:30
  20.9 26.5 %collective-permute-start.6 = (f32[4,2,128,256]{3,2,1,0:T(8,128)S(1)}, f32[4,2,128,256]{3,2,1,0:T(8,128)S(1)}, u32[]{:S(2)}, u32[]{:S(2)}) collective-permute-start(f32[4,2,128,256]{3,2,1,0:T(8,128)S(1)} %rows.2.own_ref.first_ref), channel_id=1, source_target_pairs={{28,4},{29,5},{30,6},{31,7},{4,12},{5,13},{6,14},{7,15},{12,20},{1... | collective-permute-start | bytes 3145736 | tf_op jit(solution)/shard_map/n_w_0/ppermute | solution.py:30
  21.6 20.8 %collective-permute-start.5 = (f32[4,2,32,256]{3,2,1,0:T(8,128)S(1)}, f32[4,2,32,256]{3,2,1,0:T(8,128)S(1)}, u32[]{:S(2)}, u32[]{:S(2)}) collective-permute-start(f32[4,2,32,256]{3,2,1,0:T(8,128)S(1)} %get-tuple-element.30), channel_id=1, source_target_pairs={{0,96},{32,0},{64,32},{96,64},{1,97},{33,1},{65,33},{97,65},{2,98}... | collective-permute-start | bytes 786440 | tf_op jit(solution)/shard_map/n_own_1/ppermute | solution.py:266
  23.9 18.6 %collective-permute-start.4 = (f32[4,2,32,256]{3,2,1,0:T(8,128)S(1)}, f32[4,2,32,256]{3,2,1,0:T(8,128)S(1)}, u32[]{:S(2)}, u32[]{:S(2)}) collective-permute-start(f32[4,2,32,256]{3,2,1,0:T(8,128)S(1)} %get-tuple-element.29), channel_id=1, source_target_pairs={{0,64},{32,96},{64,0},{96,32},{1,65},{33,97},{65,1},{97,33},{2,66}... | collective-permute-start | bytes 786440 | tf_op jit(solution)/shard_map/n_own_1/ppermute | solution.py:266
  25.0 17.5 %collective-permute-start.3 = (f32[4,2,32,256]{3,2,1,0:T(8,128)S(1)}, f32[4,2,32,256]{3,2,1,0:T(8,128)S(1)}, u32[]{:S(2)}, u32[]{:S(2)}) collective-permute-start(f32[4,2,32,256]{3,2,1,0:T(8,128)S(1)} %get-tuple-element.28), channel_id=1, source_target_pairs={{0,32},{32,64},{64,96},{96,0},{1,33},{33,65},{65,97},{97,1},{2,34}... | collective-permute-start | bytes 786440 | tf_op jit(solution)/shard_map/n_own_1/ppermute | solution.py:266
  42.6 27.3 %collective-permute-start.12 = (f32[4,2,128,256]{3,2,1,0:T(8,128)S(1)}, f32[4,2,128,256]{3,2,1,0:T(8,128)S(1)}, u32[]{:S(2)}, u32[]{:S(2)}) collective-permute-start(f32[4,2,128,256]{3,2,1,0:T(8,128)S(1)} %collective-permute-done.7.second_ref.refs_0_), channel_id=1, source_target_pairs={{2,0},{7,1},{4,2},{1,3},{6,4},{3,5},{0,6},{5,7},{10,8},{15,9},{12,... | collective-permute-start | bytes 3145736 | tf_op jit(solution)/shard_map/n_qa_0/ppermute | solution.py:30
  46.7 26.9 %collective-permute-start.16 = (f32[4,2,128,256]{3,2,1,0:T(8,128)S(1)}, f32[4,2,128,256]{3,2,1,0:T(8,128)S(1)}, u32[]{:S(2)}, u32[]{:S(2)}) collective-permute-start(f32[4,2,128,256]{3,2,1,0:T(8,128)S(1)} %collective-permute-done.7.second_ref.refs_0_), channel_id=1, source_target_pairs={{6,0},{3,1},{0,2},{5,3},{2,4},{7,5},{4,6},{1,7},{14,8},{11,9},{8,1... | collective-permute-start | bytes 3145736 | tf_op jit(solution)/shard_map/n_qb_0/ppermute | solution.py:30
  48.1 26.7 %collective-permute-start.8 = (f32[4,2,128,256]{3,2,1,0:T(8,128)S(1)}, f32[4,2,128,256]{3,2,1,0:T(8,128)S(1)}, u32[]{:S(2)}, u32[]{:S(2)}) collective-permute-start(f32[4,2,128,256]{3,2,1,0:T(8,128)S(1)} %pick_0.1), channel_id=1, source_target_pairs={{8,0},{9,1},{10,2},{11,3},{28,4},{29,5},{30,6},{31,7},{16,8},{17,9... | collective-permute-start | bytes 3145736 | tf_op jit(solution)/shard_map/n_rc_0/ppermute | solution.py:30
  69.9 16.0 %collective-permute-start.13 = (f32[4,2,128,256]{3,2,1,0:T(8,128)S(1)}, f32[4,2,128,256]{3,2,1,0:T(8,128)S(1)}, u32[]{:S(2)}, u32[]{:S(2)}) collective-permute-start(f32[4,2,128,256]{3,2,1,0:T(8,128)S(1)} %collective-permute-done.12.refs_0_), channel_id=1, source_target_pairs={{2,0},{7,1},{4,2},{1,3},{6,4},{3,5},{0,6},{5,7},{10,8},{15,9},{12,... | collective-permute-start | bytes 3145736 | tf_op jit(solution)/shard_map/n_q2_0/ppermute | solution.py:30
  73.5 12.3 %collective-permute-start.15 = (f32[4,2,128,256]{3,2,1,0:T(8,128)S(1)}, f32[4,2,128,256]{3,2,1,0:T(8,128)S(1)}, u32[]{:S(2)}, u32[]{:S(2)}) collective-permute-start(f32[4,2,128,256]{3,2,1,0:T(8,128)S(1)} %collective-permute-done.12.refs_0_), channel_id=1, source_target_pairs={{1,0},{0,1},{3,2},{2,3},{5,4},{4,5},{7,6},{6,7},{9,8},{8,9},{11,10... | collective-permute-start | bytes 3145736 | tf_op jit(solution)/shard_map/n_qax_0/ppermute | solution.py:30
  73.6 12.8 %collective-permute-start.17 = (f32[4,2,128,256]{3,2,1,0:T(8,128)S(1)}, f32[4,2,128,256]{3,2,1,0:T(8,128)S(1)}, u32[]{:S(2)}, u32[]{:S(2)}) collective-permute-start(f32[4,2,128,256]{3,2,1,0:T(8,128)S(1)} %collective-permute-done.16.refs_2_), channel_id=1, source_target_pairs={{1,0},{0,1},{3,2},{2,3},{5,4},{4,5},{7,6},{6,7},{9,8},{8,9},{11,10... | collective-permute-start | bytes 3145736 | tf_op jit(solution)/shard_map/n_qbx_0/ppermute | solution.py:30
  74.1 20.6 %collective-permute-start.18 = (f32[4,2,128,256]{3,2,1,0:T(8,128)S(1)}, f32[4,2,128,256]{3,2,1,0:T(8,128)S(1)}, u32[]{:S(2)}, u32[]{:S(2)}) collective-permute-start(f32[4,2,128,256]{3,2,1,0:T(8,128)S(1)} %rows.3.own_ref.first_ref), channel_id=1, source_target_pairs={{28,4},{29,5},{30,6},{31,7},{4,12},{5,13},{6,14},{7,15},{12,20},{1... | collective-permute-start | bytes 3145736 | tf_op jit(solution)/shard_map/n_w_1/ppermute | solution.py:30
  74.8 26.3 %collective-permute-start.10 = (f32[4,2,128,256]{3,2,1,0:T(8,128)S(1)}, f32[4,2,128,256]{3,2,1,0:T(8,128)S(1)}, u32[]{:S(2)}, u32[]{:S(2)}) collective-permute-start(f32[4,2,128,256]{3,2,1,0:T(8,128)S(1)} %rows.3.own_ref.first_ref), channel_id=1, source_target_pairs={{8,0},{9,1},{10,2},{11,3},{12,4},{13,5},{14,6},{15,7},{16,8},{17,9... | collective-permute-start | bytes 3145736 | tf_op jit(solution)/shard_map/n_q0_1/ppermute | solution.py:30
  85.9 16.5 %collective-permute-start.11 = (f32[4,2,128,256]{3,2,1,0:T(8,128)S(1)}, f32[4,2,128,256]{3,2,1,0:T(8,128)S(1)}, u32[]{:S(2)}, u32[]{:S(2)}) collective-permute-start(f32[4,2,128,256]{3,2,1,0:T(8,128)S(1)} %get-tuple-element.32), channel_id=1, source_target_pairs={{1,0},{0,1},{3,2},{2,3},{5,4},{4,5},{7,6},{6,7},{9,8},{8,9},{11,10... | collective-permute-start | bytes 3145736 | tf_op jit(solution)/shard_map/n_rcx_0/ppermute | solution.py:30
  85.9 16.5 %collective-permute-start.14 = (f32[4,2,128,256]{3,2,1,0:T(8,128)S(1)}, f32[4,2,128,256]{3,2,1,0:T(8,128)S(1)}, u32[]{:S(2)}, u32[]{:S(2)}) collective-permute-start(f32[4,2,128,256]{3,2,1,0:T(8,128)S(1)} %collective-permute-done.13.refs_2_), channel_id=1, source_target_pairs={{1,0},{0,1},{3,2},{2,3},{5,4},{4,5},{7,6},{6,7},{9,8},{8,9},{11,10... | collective-permute-start | bytes 3145736 | tf_op jit(solution)/shard_map/n_q2x_0/ppermute | solution.py:30
  86.4 22.2 %collective-permute-start.22 = (f32[4,2,128,256]{3,2,1,0:T(8,128)S(1)}, f32[4,2,128,256]{3,2,1,0:T(8,128)S(1)}, u32[]{:S(2)}, u32[]{:S(2)}) collective-permute-start(f32[4,2,128,256]{3,2,1,0:T(8,128)S(1)} %get-tuple-element.38), channel_id=1, source_target_pairs={{2,0},{7,1},{4,2},{1,3},{6,4},{3,5},{0,6},{5,7},{10,8},{15,9},{12,... | collective-permute-start | bytes 3145736 | tf_op jit(solution)/shard_map/n_sa_0/ppermute | solution.py:30
  94.6 26.2 %collective-permute-start.24 = (f32[4,2,128,256]{3,2,1,0:T(8,128)S(1)}, f32[4,2,128,256]{3,2,1,0:T(8,128)S(1)}, u32[]{:S(2)}, u32[]{:S(2)}) collective-permute-start(f32[4,2,128,256]{3,2,1,0:T(8,128)S(1)} %get-tuple-element.40), channel_id=1, source_target_pairs={{6,0},{3,1},{0,2},{5,3},{2,4},{7,5},{4,6},{1,7},{14,8},{11,9},{8,1... | collective-permute-start | bytes 3145736 | tf_op jit(solution)/shard_map/n_sb_0/ppermute | solution.py:30
  101.1 19.7 %collective-permute-start.20 = (f32[4,2,128,256]{3,2,1,0:T(8,128)S(1)}, f32[4,2,128,256]{3,2,1,0:T(8,128)S(1)}, u32[]{:S(2)}, u32[]{:S(2)}) collective-permute-start(f32[4,2,128,256]{3,2,1,0:T(8,128)S(1)} %collective-permute-done.10.refs_0_.second_ref), channel_id=1, source_target_pairs={{1,0},{0,1},{3,2},{2,3},{5,4},{4,5},{7,6},{6,7},{9,8},{8,9},{11,10... | collective-permute-start | bytes 3145736 | tf_op jit(solution)/shard_map/n_q0x_1/ppermute | solution.py:30
  106.9 18.6 %collective-permute-start.19 = (f32[4,2,128,256]{3,2,1,0:T(8,128)S(1)}, f32[4,2,128,256]{3,2,1,0:T(8,128)S(1)}, u32[]{:S(2)}, u32[]{:S(2)}) collective-permute-start(f32[4,2,128,256]{3,2,1,0:T(8,128)S(1)} %collective-permute-done.10.refs_0_.second_ref), channel_id=1, source_target_pairs={{2,0},{7,1},{4,2},{1,3},{6,4},{3,5},{0,6},{5,7},{10,8},{15,9},{12,... | collective-permute-start | bytes 3145736 | tf_op jit(solution)/shard_map/n_qa_1/ppermute | solution.py:30
  108.6 21.7 %collective-permute-start.23 = (f32[4,2,128,256]{3,2,1,0:T(8,128)S(1)}, f32[4,2,128,256]{3,2,1,0:T(8,128)S(1)}, u32[]{:S(2)}, u32[]{:S(2)}) collective-permute-start(f32[4,2,128,256]{3,2,1,0:T(8,128)S(1)} %collective-permute-done.22.refs_0_), channel_id=1, source_target_pairs={{1,0},{0,1},{3,2},{2,3},{5,4},{4,5},{7,6},{6,7},{9,8},{8,9},{11,10... | collective-permute-start | bytes 3145736 | tf_op jit(solution)/shard_map/n_sax_0/ppermute | solution.py:30
  120.8 26.8 %collective-permute-start.35 = (f32[4,2,128,256]{3,2,1,0:T(8,128)S(1)}, f32[4,2,128,256]{3,2,1,0:T(8,128)S(1)}, u32[]{:S(2)}, u32[]{:S(2)}) collective-permute-start(f32[4,2,128,256]{3,2,1,0:T(8,128)S(1)} %collective-permute-done.13.refs_2_), channel_id=1, source_target_pairs={{24,0},{25,1},{26,2},{27,3},{12,4},{13,5},{14,6},{15,7},{0,8},{1,9... | collective-permute-start | bytes 3145736 | tf_op jit(solution)/shard_map/n_x2_0/ppermute | solution.py:30
  120.8 27.3 %collective-permute-start.33 = (f32[4,2,128,256]{3,2,1,0:T(8,128)S(1)}, f32[4,2,128,256]{3,2,1,0:T(8,128)S(1)}, u32[]{:S(2)}, u32[]{:S(2)}) collective-permute-start(f32[4,2,128,256]{3,2,1,0:T(8,128)S(1)} %collective-permute-done.10.refs_0_.second_ref), channel_id=1, source_target_pairs={{6,0},{3,1},{0,2},{5,3},{2,4},{7,5},{4,6},{1,7},{14,8},{11,9},{8,1... | collective-permute-start | bytes 3145736 | tf_op jit(solution)/shard_map/n_qb_1/ppermute | solution.py:30
  125.5 28.1 %collective-permute-start.28 = (f32[4,2,128,256]{3,2,1,0:T(8,128)S(1)}, f32[4,2,128,256]{3,2,1,0:T(8,128)S(1)}, u32[]{:S(2)}, u32[]{:S(2)}) collective-permute-start(f32[4,2,128,256]{3,2,1,0:T(8,128)S(1)} %pick_1.1), channel_id=1, source_target_pairs={{8,0},{9,1},{10,2},{11,3},{28,4},{29,5},{30,6},{31,7},{16,8},{17,9... | collective-permute-start | bytes 3145736 | tf_op jit(solution)/shard_map/n_rc_1/ppermute | solution.py:30
  130.3 24.2 %collective-permute-start.21 = (f32[4,2,128,256]{3,2,1,0:T(8,128)S(1)}, f32[4,2,128,256]{3,2,1,0:T(8,128)S(1)}, u32[]{:S(2)}, u32[]{:S(2)}) collective-permute-start(f32[4,2,128,256]{3,2,1,0:T(8,128)S(1)} %collective-permute-done.19.refs_0_), channel_id=1, source_target_pairs={{2,0},{7,1},{4,2},{1,3},{6,4},{3,5},{0,6},{5,7},{10,8},{15,9},{12,... | collective-permute-start | bytes 3145736 | tf_op jit(solution)/shard_map/n_q2_1/ppermute | solution.py:30
  148.1 10.6 %collective-permute-start.34 = (f32[4,2,128,256]{3,2,1,0:T(8,128)S(1)}, f32[4,2,128,256]{3,2,1,0:T(8,128)S(1)}, u32[]{:S(2)}, u32[]{:S(2)}) collective-permute-start(f32[4,2,128,256]{3,2,1,0:T(8,128)S(1)} %collective-permute-done.33.refs_2_), channel_id=1, source_target_pairs={{1,0},{0,1},{3,2},{2,3},{5,4},{4,5},{7,6},{6,7},{9,8},{8,9},{11,10... | collective-permute-start | bytes 3145736 | tf_op jit(solution)/shard_map/n_qbx_1/ppermute | solution.py:30
  154.4 12.3 %collective-permute-start.30 = (f32[4,2,128,256]{3,2,1,0:T(8,128)S(1)}, f32[4,2,128,256]{3,2,1,0:T(8,128)S(1)}, u32[]{:S(2)}, u32[]{:S(2)}) collective-permute-start(f32[4,2,128,256]{3,2,1,0:T(8,128)S(1)} %get-tuple-element.43), channel_id=1, source_target_pairs={{1,0},{0,1},{3,2},{2,3},{5,4},{4,5},{7,6},{6,7},{9,8},{8,9},{11,10... | collective-permute-start | bytes 3145736 | tf_op jit(solution)/shard_map/n_rcx_1/ppermute | solution.py:30
  154.5 12.2 %collective-permute-start.31 = (f32[4,2,128,256]{3,2,1,0:T(8,128)S(1)}, f32[4,2,128,256]{3,2,1,0:T(8,128)S(1)}, u32[]{:S(2)}, u32[]{:S(2)}) collective-permute-start(f32[4,2,128,256]{3,2,1,0:T(8,128)S(1)} %collective-permute-done.21.refs_2_), channel_id=1, source_target_pairs={{1,0},{0,1},{3,2},{2,3},{5,4},{4,5},{7,6},{6,7},{9,8},{8,9},{11,10... | collective-permute-start | bytes 3145736 | tf_op jit(solution)/shard_map/n_q2x_1/ppermute | solution.py:30
  155.0 25.5 %collective-permute-start.38 = (f32[4,2,128,256]{3,2,1,0:T(8,128)S(1)}, f32[4,2,128,256]{3,2,1,0:T(8,128)S(1)}, u32[]{:S(2)}, u32[]{:S(2)}) collective-permute-start(f32[4,2,128,256]{3,2,1,0:T(8,128)S(1)} %get-tuple-element.49), channel_id=1, source_target_pairs={{6,0},{3,1},{0,2},{5,3},{2,4},{7,5},{4,6},{1,7},{14,8},{11,9},{8,1... | collective-permute-start | bytes 3145736 | tf_op jit(solution)/shard_map/n_sb_1/ppermute | solution.py:30
  155.0 26.3 %collective-permute-start.29 = (f32[4,2,128,256]{3,2,1,0:T(8,128)S(1)}, f32[4,2,128,256]{3,2,1,0:T(8,128)S(1)}, u32[]{:S(2)}, u32[]{:S(2)}) collective-permute-start(f32[4,2,128,256]{3,2,1,0:T(8,128)S(1)} %get-tuple-element.42), channel_id=1, source_target_pairs={{2,0},{7,1},{4,2},{1,3},{6,4},{3,5},{0,6},{5,7},{10,8},{15,9},{12,... | collective-permute-start | bytes 3145736 | tf_op jit(solution)/shard_map/n_sa_1/ppermute | solution.py:30
  158.7 26.1 %collective-permute-start.26 = (f32[4,2,128,256]{3,2,1,0:T(8,128)S(1)}, f32[4,2,128,256]{3,2,1,0:T(8,128)S(1)}, u32[]{:S(2)}, u32[]{:S(2)}) collective-permute-start(f32[4,2,128,256]{3,2,1,0:T(8,128)S(1)} %collective-permute-done.21.refs_2_), channel_id=1, source_target_pairs={{24,0},{25,1},{26,2},{27,3},{12,4},{13,5},{14,6},{15,7},{0,8},{1,9... | collective-permute-start | bytes 3145736 | tf_op jit(solution)/shard_map/n_x2_1/ppermute | solution.py:30
  (8 other events, 57.0 us)

commit v3 on v2

--- a/solution.py
+++ b/solution.py
@@ -10,8 +10,8 @@
 CHUNKS = (4, 4)
 SIDE = 4
 
-ORDER = (('own', 0), ('q0', 0), ('w', 0), ('own', 1), ('qa', 0), ('qb', 0), ('rc', 0), ('q0x', 0), ('tiles', 0), ('q2', 0), ('q0', 1), ('w', 1), ('qax', 0), ('qbx', 0), ('tiles', 1), ('sa', 0), ('sb', 0), ('rcx', 0), ('q2x', 0), ('tiles', 2), ('qa', 1), ('x2', 0), ('q0x', 1), ('qb', 1), ('tiles', 3), ('rc', 1), ('q2', 1), ('sax', 0), ('sbx', 0), ('tiles', 4), ('x2x', 0), ('qax', 1), ('qbx', 1), ('sa', 1), ('sb', 1), ('rcx', 1), ('x2', 1), ('q2x', 1), ('tiles', 5), ('tiles', 6), ('tiles', 7), ('sax', 1), ('sbx', 1), ('tiles', 8), ('x2x', 1), ('tiles', 9))
-LATER = {('own', 1): (('own', 0),), ('qa', 0): (('own', 1),), ('qb', 0): (('own', 1),), ('q2', 0): (('tiles', 0),), ('q0', 1): (('rc', 0), ('tiles', 0)), ('w', 1): (('tiles', 0),), ('sb', 0): (('q2', 0), ('tiles', 1), ('w', 1)), ('qa', 1): (('tiles', 2), ('w', 1)), ('x2', 0): (('q0', 1), ('tiles', 2)), ('qb', 1): (('sa', 0), ('tiles', 2)), ('q2', 1): (('tiles', 3),), ('x2x', 0): (('tiles', 4),), ('sb', 1): (('q2', 1), ('tiles', 4)), ('x2', 1): (('tiles', 4),), ('sax', 1): (('tiles', 7),), ('sbx', 1): (('tiles', 7),)}
+ORDER = (('own', 0), ('q0', 0), ('w', 0), ('own', 1), ('qa', 0), ('qb', 0), ('rc', 0), ('q0x', 0), ('tiles', 0), ('q2', 0), ('q0', 1), ('w', 1), ('qax', 0), ('qbx', 0), ('tiles', 1), ('sa', 0), ('sb', 0), ('rcx', 0), ('q2x', 0), ('tiles', 2), ('qa', 1), ('q0x', 1), ('qb', 1), ('tiles', 3), ('x2', 0), ('rc', 1), ('q2', 1), ('sax', 0), ('sbx', 0), ('tiles', 4), ('x2x', 0), ('qax', 1), ('qbx', 1), ('sa', 1), ('sb', 1), ('rcx', 1), ('x2', 1), ('q2x', 1), ('tiles', 5), ('tiles', 6), ('tiles', 7), ('sax', 1), ('sbx', 1), ('tiles', 8), ('x2x', 1), ('tiles', 9))
+LATER = {('own', 1): (('own', 0),), ('qa', 0): (('own', 1),), ('qb', 0): (('own', 1),), ('q2', 0): (('tiles', 0),), ('q0', 1): (('rc', 0), ('tiles', 0)), ('w', 1): (('tiles', 0),), ('sb', 0): (('q2', 0), ('tiles', 1), ('w', 1)), ('qa', 1): (('tiles', 2), ('w', 1)), ('x2', 0): (('q0', 1), ('tiles', 3)), ('qb', 1): (('sa', 0), ('tiles', 2)), ('q2', 1): (('tiles', 3),), ('x2x', 0): (('tiles', 4),), ('sb', 1): (('q2', 1), ('tiles', 4)), ('x2', 1): (('tiles', 4),), ('sax', 1): (('tiles', 7),), ('sbx', 1): (('tiles', 7),)}
 KERNELS = ((0, ('q0', 'own')), (0, ('qa', 'qb')), (0, ('rc', 'q2')), (1, ('q0', 'own')), (0, ('sa', 'sb')), (0, ('x2',)), (1, ('qa', 'qb')), (1, ('rc', 'q2')), (1, ('sa', 'sb')), (1, ('x2',)))
 
 

time: 195 us -> 193 us (0.990)
  starting transfers between devices: 48.6 us -> 45.9 us
    ppermute x34, waiting for transfers between devices: 86.6 us -> 73.1 us  [fetch(): return lax.ppermute(value, 'blk', pairs)]
    ppermute x6, waiting for transfers between devices: 9.53 us -> 22.3 us  [corner_turn(): pieces.append(lax.ppermute(after(piece(shift), *earlier), 'freq', pairs))]
    ppermute x34, starting transfers between devices: 38.5 us -> 35.9 us  [fetch(): return lax.ppermute(value, 'blk', pairs)]
  transfers between devices with their start and end apart: 40 -> 40, of which waited for: 14 -> 18; matrix products, arithmetic and copies ran while one was open for 1% -> 1% of each run, Pallas kernels for 21% -> 22%
where the time goes in v3:
time: 193 us; the launch traced here: 190 us
  waiting for transfers between devices  95.4 us (49%)
  starting transfers between devices  45.9 us (24%)
  Pallas kernels  44.6 us (23%)
  local copies, waits for them, and re-layouts  2.4 us (1%)
    ppermute x34, waiting for transfers between devices, fetch(): return lax.ppermute(value, 'blk', pairs)  73.1 us
    pallas_call x10, Pallas kernels, correlate(): pl.pallas_call(functools.partial(tiles_kernel, slots, first), in_specs=[p...  41.7 us
    ppermute x34, starting transfers between devices, fetch(): return lax.ppermute(value, 'blk', pairs)  35.9 us
    ppermute x6, waiting for transfers between devices, corner_turn(): pieces.append(lax.ppermute(after(piece(shift), *earlier), 'freq', pairs))  22.3 us
    ppermute x6, starting transfers between devices, corner_turn(): pieces.append(lax.ppermute(after(piece(shift), *earlier), 'freq', pairs))  10 us
  transfers between devices with their start and end apart: 40, of which 18 were waited for; matrix products, arithmetic and copies ran while one was open for 1% of the time, Pallas kernels for 22%

profile of v3, /device:TPU:0, one launch (start us, length us, event | category | flops | bytes accessed | tf_op | source)
XLA Modules:
  0.0 189.6 jit_solution(7357589548739443424)
XLA Ops:
  3.4 2.9 %collective-permute-start.1 = (f32[4,2,32,256]{3,2,1,0:T(8,128)S(1)}, f32[4,2,32,256]{3,2,1,0:T(8,128)S(1)}, u32[]{:S(2)}, u32[]{:S(2)}) collective-permute-start(f32[4,2,32,256]{3,2,1,0:T(8,128)S(1)} %get-tuple-element.53), channel_id=1, source_target_pairs={{0,64},{32,96},{64,0},{96,32},{1,65},{33,97},{65,1},{97,33},{2,66}... | collective-permute-start | bytes 786440 | tf_op jit(solution)/shard_map/n_own_0/ppermute | solution.py:266
  8.4 2.7 %collective-permute-done.refs_1_ = f32[4,2,32,256]{3,2,1,0:T(8,128)S(1)} collective-permute-done((f32[4,2,32,256]{3,2,1,0:T(8,128)S(1)}, f32[4,2,32,256]{3,2,1,0:T(8,128)S(1)}, u32[]{:S(2)}, u32[]{:S(2)}) %collective-permute-start) | collective-permute-done | bytes 262176 | tf_op jit(solution)/shard_map/n_own_0/ppermute | solution.py:266
  11.1 6.8 %collective-permute-done.1.refs_2_ = f32[4,2,32,256]{3,2,1,0:T(8,128)S(1)} collective-permute-done((f32[4,2,32,256]{3,2,1,0:T(8,128)S(1)}, f32[4,2,32,256]{3,2,1,0:T(8,128)S(1)}, u32[]{:S(2)}, u32[]{:S(2)}) %collective-permute-start.1) | collective-permute-done | bytes 262176 | tf_op jit(solution)/shard_map/n_own_0/ppermute | solution.py:266
  18.1 2.8 %collective-permute-start.7 = (f32[4,2,128,256]{3,2,1,0:T(8,128)S(1)}, f32[4,2,128,256]{3,2,1,0:T(8,128)S(1)}, u32[]{:S(2)}, u32[]{:S(2)}) collective-permute-start(f32[4,2,128,256]{3,2,1,0:T(8,128)S(1)} %rows.2.own_ref.first_ref), channel_id=1, source_target_pairs={{8,0},{9,1},{10,2},{11,3},{12,4},{13,5},{14,6},{15,7},{16,8},{17,9... | collective-permute-start | bytes 3145736 | tf_op jit(solution)/shard_map/n_q0_0/ppermute | solution.py:30
  21.6 2.2 %collective-permute-start.5 = (f32[4,2,32,256]{3,2,1,0:T(8,128)S(1)}, f32[4,2,32,256]{3,2,1,0:T(8,128)S(1)}, u32[]{:S(2)}, u32[]{:S(2)}) collective-permute-start(f32[4,2,32,256]{3,2,1,0:T(8,128)S(1)} %get-tuple-element.30), channel_id=1, source_target_pairs={{0,96},{32,0},{64,32},{96,64},{1,97},{33,1},{65,33},{97,65},{2,98}... | collective-permute-start | bytes 786440 | tf_op jit(solution)/shard_map/n_own_1/ppermute | solution.py:266
  25.7 9.2 %collective-permute-done.5.refs_3_ = f32[4,2,32,256]{3,2,1,0:T(8,128)S(1)} collective-permute-done((f32[4,2,32,256]{3,2,1,0:T(8,128)S(1)}, f32[4,2,32,256]{3,2,1,0:T(8,128)S(1)}, u32[]{:S(2)}, u32[]{:S(2)}) %collective-permute-start.5) | collective-permute-done | bytes 262176 | tf_op jit(solution)/shard_map/n_own_1/ppermute | solution.py:266
  35.0 3.5 %collective-permute-done.3.refs_1_ = f32[4,2,32,256]{3,2,1,0:T(8,128)S(1)} collective-permute-done((f32[4,2,32,256]{3,2,1,0:T(8,128)S(1)}, f32[4,2,32,256]{3,2,1,0:T(8,128)S(1)}, u32[]{:S(2)}, u32[]{:S(2)}) %collective-permute-start.3) | collective-permute-done | bytes 262176 | tf_op jit(solution)/shard_map/n_own_1/ppermute | solution.py:266
  38.6 3.9 %collective-permute-done.7.second_ref.refs_0_ = f32[4,2,128,256]{3,2,1,0:T(8,128)S(1)} collective-permute-done((f32[4,2,128,256]{3,2,1,0:T(8,128)S(1)}, f32[4,2,128,256]{3,2,1,0:T(8,128)S(1)}, u32[]{:S(2)}, u32[]{:S(2)}) %collective-permute-start.7) | collective-permute-done | bytes 1048608 | tf_op jit(solution)/shard_map/n_q0_0/ppermute | solution.py:30
  42.5 4.0 %collective-permute-start.12 = (f32[4,2,128,256]{3,2,1,0:T(8,128)S(1)}, f32[4,2,128,256]{3,2,1,0:T(8,128)S(1)}, u32[]{:S(2)}, u32[]{:S(2)}) collective-permute-start(f32[4,2,128,256]{3,2,1,0:T(8,128)S(1)} %collective-permute-done.7.second_ref.refs_0_), channel_id=1, source_target_pairs={{2,0},{7,1},{4,2},{1,3},{6,4},{3,5},{0,6},{5,7},{10,8},{15,9},{12,... | collective-permute-start | bytes 3145736 | tf_op jit(solution)/shard_map/n_qa_0/ppermute | solution.py:30
  47.9 3.8 %collective-permute-start.8 = (f32[4,2,128,256]{3,2,1,0:T(8,128)S(1)}, f32[4,2,128,256]{3,2,1,0:T(8,128)S(1)}, u32[]{:S(2)}, u32[]{:S(2)}) collective-permute-start(f32[4,2,128,256]{3,2,1,0:T(8,128)S(1)} %pick_0.1), channel_id=1, source_target_pairs={{8,0},{9,1},{10,2},{11,3},{28,4},{29,5},{30,6},{31,7},{16,8},{17,9... | collective-permute-start | bytes 3145736 | tf_op jit(solution)/shard_map/n_rc_0/ppermute | solution.py:30
  51.7 3.8 %tiles_k0.1.refs_4_ = f32[17,8,2,128,128]{4,3,2,1,0:T(8,128)} custom-call(s32[18]{0:T(128)S(1)} %pad_add_fusion.info, f32[4,2,128,256]{3,2,1,0:T(8,128)S(1)} %rows.2.own_ref.first_ref, f32[4,2,128,256]{3,2,1,0:T(8,128)S(1)} %collective-permute-done.7.second_ref.refs_0_, f32[4,2,128,256]{3,2,1,0:T(8,128)S(1)} %collective-permute-done.9.refs_1_), custom_call_target="tpu_custom_call" | custom-call | flops 1207959552 | bytes 4718592 | tf_op jit(solution)/shard_map/n_tiles_0/tiles_k0/pallas_call | solution.py:138
  55.5 11.9 %collective-permute-done.12.refs_0_ = f32[4,2,128,256]{3,2,1,0:T(8,128)S(1)} collective-permute-done((f32[4,2,128,256]{3,2,1,0:T(8,128)S(1)}, f32[4,2,128,256]{3,2,1,0:T(8,128)S(1)}, u32[]{:S(2)}, u32[]{:S(2)}) %collective-permute-start.12) | collective-permute-done | bytes 1048608 | tf_op jit(solution)/shard_map/n_qa_0/ppermute | solution.py:30
  67.4 3.4 %collective-permute-start.13 = (f32[4,2,128,256]{3,2,1,0:T(8,128)S(1)}, f32[4,2,128,256]{3,2,1,0:T(8,128)S(1)}, u32[]{:S(2)}, u32[]{:S(2)}) collective-permute-start(f32[4,2,128,256]{3,2,1,0:T(8,128)S(1)} %collective-permute-done.12.refs_0_), channel_id=1, source_target_pairs={{2,0},{7,1},{4,2},{1,3},{6,4},{3,5},{0,6},{5,7},{10,8},{15,9},{12,... | collective-permute-start | bytes 3145736 | tf_op jit(solution)/shard_map/n_q2_0/ppermute | solution.py:30
  72.1 2.7 %collective-permute-done.8.second_ref.refs_0_ = f32[4,2,128,256]{3,2,1,0:T(8,128)S(1)} collective-permute-done((f32[4,2,128,256]{3,2,1,0:T(8,128)S(1)}, f32[4,2,128,256]{3,2,1,0:T(8,128)S(1)}, u32[]{:S(2)}, u32[]{:S(2)}) %collective-permute-start.8) | collective-permute-done | bytes 1048608 | tf_op jit(solution)/shard_map/n_rc_0/ppermute | solution.py:30
  74.8 3.7 %collective-permute-start.10 = (f32[4,2,128,256]{3,2,1,0:T(8,128)S(1)}, f32[4,2,128,256]{3,2,1,0:T(8,128)S(1)}, u32[]{:S(2)}, u32[]{:S(2)}) collective-permute-start(f32[4,2,128,256]{3,2,1,0:T(8,128)S(1)} %rows.3.own_ref.first_ref), channel_id=1, source_target_pairs={{8,0},{9,1},{10,2},{11,3},{12,4},{13,5},{14,6},{15,7},{16,8},{17,9... | collective-permute-start | bytes 3145736 | tf_op jit(solution)/shard_map/n_q0_1/ppermute | solution.py:30
  79.2 3.9 %collective-permute-done.13.refs_2_ = f32[4,2,128,256]{3,2,1,0:T(8,128)S(1)} collective-permute-done((f32[4,2,128,256]{3,2,1,0:T(8,128)S(1)}, f32[4,2,128,256]{3,2,1,0:T(8,128)S(1)}, u32[]{:S(2)}, u32[]{:S(2)}) %collective-permute-start.13) | collective-permute-done | bytes 1048608 | tf_op jit(solution)/shard_map/n_q2_0/ppermute | solution.py:30
  83.7 3.7 %collective-permute-start.22 = (f32[4,2,128,256]{3,2,1,0:T(8,128)S(1)}, f32[4,2,128,256]{3,2,1,0:T(8,128)S(1)}, u32[]{:S(2)}, u32[]{:S(2)}) collective-permute-start(f32[4,2,128,256]{3,2,1,0:T(8,128)S(1)} %get-tuple-element.38), channel_id=1, source_target_pairs={{2,0},{7,1},{4,2},{1,3},{6,4},{3,5},{0,6},{5,7},{10,8},{15,9},{12,... | collective-permute-start | bytes 3145736 | tf_op jit(solution)/shard_map/n_sa_0/ppermute | solution.py:30
  87.4 4.5 %tiles_k1.1.refs_4_ = f32[17,8,2,128,128]{4,3,2,1,0:T(8,128)} custom-call(s32[18]{0:T(128)S(1)} %pad_add_fusion.info, f32[4,2,128,256]{3,2,1,0:T(8,128)S(1)} %rows.2.own_ref.first_ref, f32[4,2,128,256]{3,2,1,0:T(8,128)S(1)} %collective-permute-done.12.refs_0_, ...), custom_call_target="tpu_custom_call", output_to_operand_aliasing={{}: (6, {})} | custom-call | flops 1610612736 | bytes 7340032 | tf_op jit(solution)/shard_map/n_tiles_1/tiles_k1/pallas_call | solution.py:138
  92.0 8.8 %collective-permute-done.10.refs_0_.second_ref = f32[4,2,128,256]{3,2,1,0:T(8,128)S(1)} collective-permute-done((f32[4,2,128,256]{3,2,1,0:T(8,128)S(1)}, f32[4,2,128,256]{3,2,1,0:T(8,128)S(1)}, u32[]{:S(2)}, u32[]{:S(2)}) %collective-permute-start.10) | collective-permute-done | bytes 1048608 | tf_op jit(solution)/shard_map/n_q0_1/ppermute | solution.py:30
  100.8 4.5 %tiles_k2.1.refs_2_ = f32[17,8,2,128,128]{4,3,2,1,0:T(8,128)} custom-call(s32[18]{0:T(128)S(1)} %pad_add_fusion.info, f32[4,2,128,256]{3,2,1,0:T(8,128)S(1)} %rows.2.own_ref.first_ref, f32[4,2,128,256]{3,2,1,0:T(8,128)S(1)} %collective-permute-done.8.second_ref.refs_0_, ...), custom_call_target="tpu_custom_call", output_to_operand_aliasing={{}: (6, {})} | custom-call | flops 1610612736 | bytes 7340032 | tf_op jit(solution)/shard_map/n_tiles_2/tiles_k2/pallas_call | solution.py:138
  105.3 2.2 %collective-permute-start.19 = (f32[4,2,128,256]{3,2,1,0:T(8,128)S(1)}, f32[4,2,128,256]{3,2,1,0:T(8,128)S(1)}, u32[]{:S(2)}, u32[]{:S(2)}) collective-permute-start(f32[4,2,128,256]{3,2,1,0:T(8,128)S(1)} %collective-permute-done.10.refs_0_.second_ref), channel_id=1, source_target_pairs={{2,0},{7,1},{4,2},{1,3},{6,4},{3,5},{0,6},{5,7},{10,8},{15,9},{12,... | collective-permute-start | bytes 3145736 | tf_op jit(solution)/shard_map/n_qa_1/ppermute | solution.py:30
  107.5 10.6 %collective-permute-done.24.refs_2_ = f32[4,2,128,256]{3,2,1,0:T(8,128)S(1)} collective-permute-done((f32[4,2,128,256]{3,2,1,0:T(8,128)S(1)}, f32[4,2,128,256]{3,2,1,0:T(8,128)S(1)}, u32[]{:S(2)}, u32[]{:S(2)}) %collective-permute-start.24) | collective-permute-done | bytes 1048608 | tf_op jit(solution)/shard_map/n_sb_0/ppermute | solution.py:30
  118.2 3.8 %tiles_k3.1.refs_4_ = f32[17,8,2,128,128]{4,3,2,1,0:T(8,128)} custom-call(s32[18]{0:T(128)S(1)} %pad_add_fusion.info, f32[4,2,128,256]{3,2,1,0:T(8,128)S(1)} %rows.3.own_ref.first_ref, f32[4,2,128,256]{3,2,1,0:T(8,128)S(1)} %collective-permute-done.10.refs_0_.second_ref, ...), custom_call_target="tpu_custom_call", output_to_operand_aliasing={{}: (4, {})} | custom-call | flops 1207959552 | bytes 4718592 | tf_op jit(solution)/shard_map/n_tiles_3/tiles_k3/pallas_call | solution.py:138
  123.5 2.5 %collective-permute-start.28 = (f32[4,2,128,256]{3,2,1,0:T(8,128)S(1)}, f32[4,2,128,256]{3,2,1,0:T(8,128)S(1)}, u32[]{:S(2)}, u32[]{:S(2)}) collective-permute-start(f32[4,2,128,256]{3,2,1,0:T(8,128)S(1)} %pick_1.1), channel_id=1, source_target_pairs={{8,0},{9,1},{10,2},{11,3},{28,4},{29,5},{30,6},{31,7},{16,8},{17,9... | collective-permute-start | bytes 3145736 | tf_op jit(solution)/shard_map/n_rc_1/ppermute | solution.py:30
  127.9 4.5 %tiles_k4.1.refs_2_ = f32[17,8,2,128,128]{4,3,2,1,0:T(8,128)} custom-call(s32[18]{0:T(128)S(1)} %pad_add_fusion.info, f32[4,2,128,256]{3,2,1,0:T(8,128)S(1)} %rows.2.own_ref.first_ref, f32[4,2,128,256]{3,2,1,0:T(8,128)S(1)} %collective-permute-done.22.refs_0_, ...), custom_call_target="tpu_custom_call", output_to_operand_aliasing={{}: (6, {})} | custom-call | flops 1610612736 | bytes 7340032 | tf_op jit(solution)/shard_map/n_tiles_4/tiles_k4/pallas_call | solution.py:138
  132.5 16.4 %collective-permute-done.35.refs_0_ = f32[4,2,128,256]{3,2,1,0:T(8,128)S(1)} collective-permute-done((f32[4,2,128,256]{3,2,1,0:T(8,128)S(1)}, f32[4,2,128,256]{3,2,1,0:T(8,128)S(1)}, u32[]{:S(2)}, u32[]{:S(2)}) %collective-permute-start.35) | collective-permute-done | bytes 1048608 | tf_op jit(solution)/shard_map/n_x2_0/ppermute | solution.py:30
  155.1 3.4 %tiles_k5.1.refs_4_ = f32[17,8,2,128,128]{4,3,2,1,0:T(8,128)} custom-call(s32[18]{0:T(128)S(1)} %pad_add_fusion.info, f32[4,2,128,256]{3,2,1,0:T(8,128)S(1)} %rows.2.own_ref.first_ref, f32[4,2,128,256]{3,2,1,0:T(8,128)S(1)} %collective-permute-done.35.refs_0_, ...), custom_call_target="tpu_custom_call", output_to_operand_aliasing={{}: (4, {})} | custom-call | flops 805306368 | bytes 4194304 | tf_op jit(solution)/shard_map/n_tiles_5/tiles_k5/pallas_call | solution.py:138
  158.5 4.5 %tiles_k6.1.refs_4_ = f32[17,8,2,128,128]{4,3,2,1,0:T(8,128)} custom-call(s32[18]{0:T(128)S(1)} %pad_add_fusion.info, f32[4,2,128,256]{3,2,1,0:T(8,128)S(1)} %rows.3.own_ref.first_ref, f32[4,2,128,256]{3,2,1,0:T(8,128)S(1)} %collective-permute-done.19.refs_0_, ...), custom_call_target="tpu_custom_call", output_to_operand_aliasing={{}: (6, {})} | custom-call | flops 1610612736 | bytes 7340032 | tf_op jit(solution)/shard_map/n_tiles_6/tiles_k6/pallas_call | solution.py:138
  163.1 4.5 %tiles_k7.1.refs_4_ = f32[17,8,2,128,128]{4,3,2,1,0:T(8,128)} custom-call(s32[18]{0:T(128)S(1)} %pad_add_fusion.info, f32[4,2,128,256]{3,2,1,0:T(8,128)S(1)} %rows.3.own_ref.first_ref, f32[4,2,128,256]{3,2,1,0:T(8,128)S(1)} %collective-permute-done.28.second_ref.refs_0_, ...), custom_call_target="tpu_custom_call", output_to_operand_aliasing={{}: (6, {})} | custom-call | flops 1610612736 | bytes 7340032 | tf_op jit(solution)/shard_map/n_tiles_7/tiles_k7/pallas_call | solution.py:138
  167.6 9.2 %collective-permute-done.38.refs_2_ = f32[4,2,128,256]{3,2,1,0:T(8,128)S(1)} collective-permute-done((f32[4,2,128,256]{3,2,1,0:T(8,128)S(1)}, f32[4,2,128,256]{3,2,1,0:T(8,128)S(1)}, u32[]{:S(2)}, u32[]{:S(2)}) %collective-permute-start.38) | collective-permute-done | bytes 1048608 | tf_op jit(solution)/shard_map/n_sb_1/ppermute | solution.py:30
  181.4 4.6 %tiles_k8.1.refs_2_ = f32[17,8,2,128,128]{4,3,2,1,0:T(8,128)} custom-call(s32[18]{0:T(128)S(1)} %pad_add_fusion.info, f32[4,2,128,256]{3,2,1,0:T(8,128)S(1)} %rows.3.own_ref.first_ref, f32[4,2,128,256]{3,2,1,0:T(8,128)S(1)} %collective-permute-done.29.refs_0_, ...), custom_call_target="tpu_custom_call", output_to_operand_aliasing={{}: (6, {})} | custom-call | flops 1610612736 | bytes 7340032 | tf_op jit(solution)/shard_map/n_tiles_8/tiles_k8/pallas_call | solution.py:138
  186.0 3.4 %tiles_k9.1 = f32[17,8,2,128,128]{4,3,2,1,0:T(8,128)} custom-call(s32[18]{0:T(128)S(1)} %pad_add_fusion.info, f32[4,2,128,256]{3,2,1,0:T(8,128)S(1)} %rows.3.own_ref.first_ref, f32[4,2,128,256]{3,2,1,0:T(8,128)S(1)} %collective-permute-done.26.refs_0_, f32[4,2,128,256]{3,2,1,0:T(8,128)S(1)} %collective-permute-done.27.refs_1_, ...), custom_call_target="tpu_custom_call", output_to_operand_aliasing={{}: (4, {})} | custom-call | flops 805306368 | bytes 4194304 | tf_op jit(solution)/shard_map/n_tiles_9/tiles_k9/pallas_call | solution.py:138
  (71 shorter events, 26.5 us)
Async XLA Ops:
  3.4 14.5 %collective-permute-start.1 = (f32[4,2,32,256]{3,2,1,0:T(8,128)S(1)}, f32[4,2,32,256]{3,2,1,0:T(8,128)S(1)}, u32[]{:S(2)}, u32[]{:S(2)}) collective-permute-start(f32[4,2,32,256]{3,2,1,0:T(8,128)S(1)} %get-tuple-element.53), channel_id=1, source_target_pairs={{0,64},{32,96},{64,0},{96,32},{1,65},{33,97},{65,1},{97,33},{2,66}... | collective-permute-start | bytes 786440 | tf_op jit(solution)/shard_map/n_own_0/ppermute | solution.py:266
  6.3 11.6 %collective-permute-start.2 = (f32[4,2,32,256]{3,2,1,0:T(8,128)S(1)}, f32[4,2,32,256]{3,2,1,0:T(8,128)S(1)}, u32[]{:S(2)}, u32[]{:S(2)}) collective-permute-start(f32[4,2,32,256]{3,2,1,0:T(8,128)S(1)} %get-tuple-element.52), channel_id=1, source_target_pairs={{0,96},{32,0},{64,32},{96,64},{1,97},{33,1},{65,33},{97,65},{2,98}... | collective-permute-start | bytes 786440 | tf_op jit(solution)/shard_map/n_own_0/ppermute | solution.py:266
  18.1 24.4 %collective-permute-start.7 = (f32[4,2,128,256]{3,2,1,0:T(8,128)S(1)}, f32[4,2,128,256]{3,2,1,0:T(8,128)S(1)}, u32[]{:S(2)}, u32[]{:S(2)}) collective-permute-start(f32[4,2,128,256]{3,2,1,0:T(8,128)S(1)} %rows.2.own_ref.first_ref), channel_id=1, source_target_pairs={{8,0},{9,1},{10,2},{11,3},{12,4},{13,5},{14,6},{15,7},{16,8},{17,9... | collective-permute-start | bytes 3145736 | tf_op jit(solution)/shard_map/n_q0_0/ppermute | solution.py:30
  20.9 26.4 %collective-permute-start.6 = (f32[4,2,128,256]{3,2,1,0:T(8,128)S(1)}, f32[4,2,128,256]{3,2,1,0:T(8,128)S(1)}, u32[]{:S(2)}, u32[]{:S(2)}) collective-permute-start(f32[4,2,128,256]{3,2,1,0:T(8,128)S(1)} %rows.2.own_ref.first_ref), channel_id=1, source_target_pairs={{28,4},{29,5},{30,6},{31,7},{4,12},{5,13},{6,14},{7,15},{12,20},{1... | collective-permute-start | bytes 3145736 | tf_op jit(solution)/shard_map/n_w_0/ppermute | solution.py:30
  21.6 13.3 %collective-permute-start.5 = (f32[4,2,32,256]{3,2,1,0:T(8,128)S(1)}, f32[4,2,32,256]{3,2,1,0:T(8,128)S(1)}, u32[]{:S(2)}, u32[]{:S(2)}) collective-permute-start(f32[4,2,32,256]{3,2,1,0:T(8,128)S(1)} %get-tuple-element.30), channel_id=1, source_target_pairs={{0,96},{32,0},{64,32},{96,64},{1,97},{33,1},{65,33},{97,65},{2,98}... | collective-permute-start | bytes 786440 | tf_op jit(solution)/shard_map/n_own_1/ppermute | solution.py:266
  23.9 11.1 %collective-permute-start.4 = (f32[4,2,32,256]{3,2,1,0:T(8,128)S(1)}, f32[4,2,32,256]{3,2,1,0:T(8,128)S(1)}, u32[]{:S(2)}, u32[]{:S(2)}) collective-permute-start(f32[4,2,32,256]{3,2,1,0:T(8,128)S(1)} %get-tuple-element.29), channel_id=1, source_target_pairs={{0,64},{32,96},{64,0},{96,32},{1,65},{33,97},{65,1},{97,33},{2,66}... | collective-permute-start | bytes 786440 | tf_op jit(solution)/shard_map/n_own_1/ppermute | solution.py:266
  25.0 13.5 %collective-permute-start.3 = (f32[4,2,32,256]{3,2,1,0:T(8,128)S(1)}, f32[4,2,32,256]{3,2,1,0:T(8,128)S(1)}, u32[]{:S(2)}, u32[]{:S(2)}) collective-permute-start(f32[4,2,32,256]{3,2,1,0:T(8,128)S(1)} %get-tuple-element.28), channel_id=1, source_target_pairs={{0,32},{32,64},{64,96},{96,0},{1,33},{33,65},{65,97},{97,1},{2,34}... | collective-permute-start | bytes 786440 | tf_op jit(solution)/shard_map/n_own_1/ppermute | solution.py:266
  42.5 24.9 %collective-permute-start.12 = (f32[4,2,128,256]{3,2,1,0:T(8,128)S(1)}, f32[4,2,128,256]{3,2,1,0:T(8,128)S(1)}, u32[]{:S(2)}, u32[]{:S(2)}) collective-permute-start(f32[4,2,128,256]{3,2,1,0:T(8,128)S(1)} %collective-permute-done.7.second_ref.refs_0_), channel_id=1, source_target_pairs={{2,0},{7,1},{4,2},{1,3},{6,4},{3,5},{0,6},{5,7},{10,8},{15,9},{12,... | collective-permute-start | bytes 3145736 | tf_op jit(solution)/shard_map/n_qa_0/ppermute | solution.py:30
  46.5 24.3 %collective-permute-start.16 = (f32[4,2,128,256]{3,2,1,0:T(8,128)S(1)}, f32[4,2,128,256]{3,2,1,0:T(8,128)S(1)}, u32[]{:S(2)}, u32[]{:S(2)}) collective-permute-start(f32[4,2,128,256]{3,2,1,0:T(8,128)S(1)} %collective-permute-done.7.second_ref.refs_0_), channel_id=1, source_target_pairs={{6,0},{3,1},{0,2},{5,3},{2,4},{7,5},{4,6},{1,7},{14,8},{11,9},{8,1... | collective-permute-start | bytes 3145736 | tf_op jit(solution)/shard_map/n_qb_0/ppermute | solution.py:30
  47.9 26.9 %collective-permute-start.8 = (f32[4,2,128,256]{3,2,1,0:T(8,128)S(1)}, f32[4,2,128,256]{3,2,1,0:T(8,128)S(1)}, u32[]{:S(2)}, u32[]{:S(2)}) collective-permute-start(f32[4,2,128,256]{3,2,1,0:T(8,128)S(1)} %pick_0.1), channel_id=1, source_target_pairs={{8,0},{9,1},{10,2},{11,3},{28,4},{29,5},{30,6},{31,7},{16,8},{17,9... | collective-permute-start | bytes 3145736 | tf_op jit(solution)/shard_map/n_rc_0/ppermute | solution.py:30
  67.4 15.8 %collective-permute-start.13 = (f32[4,2,128,256]{3,2,1,0:T(8,128)S(1)}, f32[4,2,128,256]{3,2,1,0:T(8,128)S(1)}, u32[]{:S(2)}, u32[]{:S(2)}) collective-permute-start(f32[4,2,128,256]{3,2,1,0:T(8,128)S(1)} %collective-permute-done.12.refs_0_), channel_id=1, source_target_pairs={{2,0},{7,1},{4,2},{1,3},{6,4},{3,5},{0,6},{5,7},{10,8},{15,9},{12,... | collective-permute-start | bytes 3145736 | tf_op jit(solution)/shard_map/n_q2_0/ppermute | solution.py:30
  70.8 12.3 %collective-permute-start.15 = (f32[4,2,128,256]{3,2,1,0:T(8,128)S(1)}, f32[4,2,128,256]{3,2,1,0:T(8,128)S(1)}, u32[]{:S(2)}, u32[]{:S(2)}) collective-permute-start(f32[4,2,128,256]{3,2,1,0:T(8,128)S(1)} %collective-permute-done.12.refs_0_), channel_id=1, source_target_pairs={{1,0},{0,1},{3,2},{2,3},{5,4},{4,5},{7,6},{6,7},{9,8},{8,9},{11,10... | collective-permute-start | bytes 3145736 | tf_op jit(solution)/shard_map/n_qax_0/ppermute | solution.py:30
  70.8 12.8 %collective-permute-start.17 = (f32[4,2,128,256]{3,2,1,0:T(8,128)S(1)}, f32[4,2,128,256]{3,2,1,0:T(8,128)S(1)}, u32[]{:S(2)}, u32[]{:S(2)}) collective-permute-start(f32[4,2,128,256]{3,2,1,0:T(8,128)S(1)} %collective-permute-done.16.refs_2_), channel_id=1, source_target_pairs={{1,0},{0,1},{3,2},{2,3},{5,4},{4,5},{7,6},{6,7},{9,8},{8,9},{11,10... | collective-permute-start | bytes 3145736 | tf_op jit(solution)/shard_map/n_qbx_0/ppermute | solution.py:30
  71.3 20.6 %collective-permute-start.18 = (f32[4,2,128,256]{3,2,1,0:T(8,128)S(1)}, f32[4,2,128,256]{3,2,1,0:T(8,128)S(1)}, u32[]{:S(2)}, u32[]{:S(2)}) collective-permute-start(f32[4,2,128,256]{3,2,1,0:T(8,128)S(1)} %rows.3.own_ref.first_ref), channel_id=1, source_target_pairs={{28,4},{29,5},{30,6},{31,7},{4,12},{5,13},{6,14},{7,15},{12,20},{1... | collective-permute-start | bytes 3145736 | tf_op jit(solution)/shard_map/n_w_1/ppermute | solution.py:30
  74.8 26.0 %collective-permute-start.10 = (f32[4,2,128,256]{3,2,1,0:T(8,128)S(1)}, f32[4,2,128,256]{3,2,1,0:T(8,128)S(1)}, u32[]{:S(2)}, u32[]{:S(2)}) collective-permute-start(f32[4,2,128,256]{3,2,1,0:T(8,128)S(1)} %rows.3.own_ref.first_ref), channel_id=1, source_target_pairs={{8,0},{9,1},{10,2},{11,3},{12,4},{13,5},{14,6},{15,7},{16,8},{17,9... | collective-permute-start | bytes 3145736 | tf_op jit(solution)/shard_map/n_q0_1/ppermute | solution.py:30
  83.1 17.6 %collective-permute-start.11 = (f32[4,2,128,256]{3,2,1,0:T(8,128)S(1)}, f32[4,2,128,256]{3,2,1,0:T(8,128)S(1)}, u32[]{:S(2)}, u32[]{:S(2)}) collective-permute-start(f32[4,2,128,256]{3,2,1,0:T(8,128)S(1)} %get-tuple-element.32), channel_id=1, source_target_pairs={{1,0},{0,1},{3,2},{2,3},{5,4},{4,5},{7,6},{6,7},{9,8},{8,9},{11,10... | collective-permute-start | bytes 3145736 | tf_op jit(solution)/shard_map/n_rcx_0/ppermute | solution.py:30
  83.2 17.6 %collective-permute-start.14 = (f32[4,2,128,256]{3,2,1,0:T(8,128)S(1)}, f32[4,2,128,256]{3,2,1,0:T(8,128)S(1)}, u32[]{:S(2)}, u32[]{:S(2)}) collective-permute-start(f32[4,2,128,256]{3,2,1,0:T(8,128)S(1)} %collective-permute-done.13.refs_2_), channel_id=1, source_target_pairs={{1,0},{0,1},{3,2},{2,3},{5,4},{4,5},{7,6},{6,7},{9,8},{8,9},{11,10... | collective-permute-start | bytes 3145736 | tf_op jit(solution)/shard_map/n_q2x_0/ppermute | solution.py:30
  83.7 23.9 %collective-permute-start.22 = (f32[4,2,128,256]{3,2,1,0:T(8,128)S(1)}, f32[4,2,128,256]{3,2,1,0:T(8,128)S(1)}, u32[]{:S(2)}, u32[]{:S(2)}) collective-permute-start(f32[4,2,128,256]{3,2,1,0:T(8,128)S(1)} %get-tuple-element.38), channel_id=1, source_target_pairs={{2,0},{7,1},{4,2},{1,3},{6,4},{3,5},{0,6},{5,7},{10,8},{15,9},{12,... | collective-permute-start | bytes 3145736 | tf_op jit(solution)/shard_map/n_sa_0/ppermute | solution.py:30
  91.9 26.3 %collective-permute-start.24 = (f32[4,2,128,256]{3,2,1,0:T(8,128)S(1)}, f32[4,2,128,256]{3,2,1,0:T(8,128)S(1)}, u32[]{:S(2)}, u32[]{:S(2)}) collective-permute-start(f32[4,2,128,256]{3,2,1,0:T(8,128)S(1)} %get-tuple-element.40), channel_id=1, source_target_pairs={{6,0},{3,1},{0,2},{5,3},{2,4},{7,5},{4,6},{1,7},{14,8},{11,9},{8,1... | collective-permute-start | bytes 3145736 | tf_op jit(solution)/shard_map/n_sb_0/ppermute | solution.py:30
  100.8 17.4 %collective-permute-start.20 = (f32[4,2,128,256]{3,2,1,0:T(8,128)S(1)}, f32[4,2,128,256]{3,2,1,0:T(8,128)S(1)}, u32[]{:S(2)}, u32[]{:S(2)}) collective-permute-start(f32[4,2,128,256]{3,2,1,0:T(8,128)S(1)} %collective-permute-done.10.refs_0_.second_ref), channel_id=1, source_target_pairs={{1,0},{0,1},{3,2},{2,3},{5,4},{4,5},{7,6},{6,7},{9,8},{8,9},{11,10... | collective-permute-start | bytes 3145736 | tf_op jit(solution)/shard_map/n_q0x_1/ppermute | solution.py:30
  105.3 18.2 %collective-permute-start.19 = (f32[4,2,128,256]{3,2,1,0:T(8,128)S(1)}, f32[4,2,128,256]{3,2,1,0:T(8,128)S(1)}, u32[]{:S(2)}, u32[]{:S(2)}) collective-permute-start(f32[4,2,128,256]{3,2,1,0:T(8,128)S(1)} %collective-permute-done.10.refs_0_.second_ref), channel_id=1, source_target_pairs={{2,0},{7,1},{4,2},{1,3},{6,4},{3,5},{0,6},{5,7},{10,8},{15,9},{12,... | collective-permute-start | bytes 3145736 | tf_op jit(solution)/shard_map/n_qa_1/ppermute | solution.py:30
  107.5 18.5 %collective-permute-start.23 = (f32[4,2,128,256]{3,2,1,0:T(8,128)S(1)}, f32[4,2,128,256]{3,2,1,0:T(8,128)S(1)}, u32[]{:S(2)}, u32[]{:S(2)}) collective-permute-start(f32[4,2,128,256]{3,2,1,0:T(8,128)S(1)} %collective-permute-done.22.refs_0_), channel_id=1, source_target_pairs={{1,0},{0,1},{3,2},{2,3},{5,4},{4,5},{7,6},{6,7},{9,8},{8,9},{11,10... | collective-permute-start | bytes 3145736 | tf_op jit(solution)/shard_map/n_sax_0/ppermute | solution.py:30
  118.2 9.7 %collective-permute-start.25 = (f32[4,2,128,256]{3,2,1,0:T(8,128)S(1)}, f32[4,2,128,256]{3,2,1,0:T(8,128)S(1)}, u32[]{:S(2)}, u32[]{:S(2)}) collective-permute-start(f32[4,2,128,256]{3,2,1,0:T(8,128)S(1)} %collective-permute-done.24.refs_2_), channel_id=1, source_target_pairs={{1,0},{0,1},{3,2},{2,3},{5,4},{4,5},{7,6},{6,7},{9,8},{8,9},{11,10... | collective-permute-start | bytes 3145736 | tf_op jit(solution)/shard_map/n_sbx_0/ppermute | solution.py:30
  122.0 26.9 %collective-permute-start.35 = (f32[4,2,128,256]{3,2,1,0:T(8,128)S(1)}, f32[4,2,128,256]{3,2,1,0:T(8,128)S(1)}, u32[]{:S(2)}, u32[]{:S(2)}) collective-permute-start(f32[4,2,128,256]{3,2,1,0:T(8,128)S(1)} %collective-permute-done.13.refs_2_), channel_id=1, source_target_pairs={{24,0},{25,1},{26,2},{27,3},{12,4},{13,5},{14,6},{15,7},{0,8},{1,9... | collective-permute-start | bytes 3145736 | tf_op jit(solution)/shard_map/n_x2_0/ppermute | solution.py:30
  122.1 27.3 %collective-permute-start.33 = (f32[4,2,128,256]{3,2,1,0:T(8,128)S(1)}, f32[4,2,128,256]{3,2,1,0:T(8,128)S(1)}, u32[]{:S(2)}, u32[]{:S(2)}) collective-permute-start(f32[4,2,128,256]{3,2,1,0:T(8,128)S(1)} %collective-permute-done.10.refs_0_.second_ref), channel_id=1, source_target_pairs={{6,0},{3,1},{0,2},{5,3},{2,4},{7,5},{4,6},{1,7},{14,8},{11,9},{8,1... | collective-permute-start | bytes 3145736 | tf_op jit(solution)/shard_map/n_qb_1/ppermute | solution.py:30
  123.5 25.8 %collective-permute-start.28 = (f32[4,2,128,256]{3,2,1,0:T(8,128)S(1)}, f32[4,2,128,256]{3,2,1,0:T(8,128)S(1)}, u32[]{:S(2)}, u32[]{:S(2)}) collective-permute-start(f32[4,2,128,256]{3,2,1,0:T(8,128)S(1)} %pick_1.1), channel_id=1, source_target_pairs={{8,0},{9,1},{10,2},{11,3},{28,4},{29,5},{30,6},{31,7},{16,8},{17,9... | collective-permute-start | bytes 3145736 | tf_op jit(solution)/shard_map/n_rc_1/ppermute | solution.py:30
  126.0 24.7 %collective-permute-start.21 = (f32[4,2,128,256]{3,2,1,0:T(8,128)S(1)}, f32[4,2,128,256]{3,2,1,0:T(8,128)S(1)}, u32[]{:S(2)}, u32[]{:S(2)}) collective-permute-start(f32[4,2,128,256]{3,2,1,0:T(8,128)S(1)} %collective-permute-done.19.refs_0_), channel_id=1, source_target_pairs={{2,0},{7,1},{4,2},{1,3},{6,4},{3,5},{0,6},{5,7},{10,8},{15,9},{12,... | collective-permute-start | bytes 3145736 | tf_op jit(solution)/shard_map/n_q2_1/ppermute | solution.py:30
  150.1 12.9 %collective-permute-start.30 = (f32[4,2,128,256]{3,2,1,0:T(8,128)S(1)}, f32[4,2,128,256]{3,2,1,0:T(8,128)S(1)}, u32[]{:S(2)}, u32[]{:S(2)}) collective-permute-start(f32[4,2,128,256]{3,2,1,0:T(8,128)S(1)} %get-tuple-element.43), channel_id=1, source_target_pairs={{1,0},{0,1},{3,2},{2,3},{5,4},{4,5},{7,6},{6,7},{9,8},{8,9},{11,10... | collective-permute-start | bytes 3145736 | tf_op jit(solution)/shard_map/n_rcx_1/ppermute | solution.py:30
  150.7 12.3 %collective-permute-start.31 = (f32[4,2,128,256]{3,2,1,0:T(8,128)S(1)}, f32[4,2,128,256]{3,2,1,0:T(8,128)S(1)}, u32[]{:S(2)}, u32[]{:S(2)}) collective-permute-start(f32[4,2,128,256]{3,2,1,0:T(8,128)S(1)} %collective-permute-done.21.refs_2_), channel_id=1, source_target_pairs={{1,0},{0,1},{3,2},{2,3},{5,4},{4,5},{7,6},{6,7},{9,8},{8,9},{11,10... | collective-permute-start | bytes 3145736 | tf_op jit(solution)/shard_map/n_q2x_1/ppermute | solution.py:30
  151.5 25.4 %collective-permute-start.38 = (f32[4,2,128,256]{3,2,1,0:T(8,128)S(1)}, f32[4,2,128,256]{3,2,1,0:T(8,128)S(1)}, u32[]{:S(2)}, u32[]{:S(2)}) collective-permute-start(f32[4,2,128,256]{3,2,1,0:T(8,128)S(1)} %get-tuple-element.49), channel_id=1, source_target_pairs={{6,0},{3,1},{0,2},{5,3},{2,4},{7,5},{4,6},{1,7},{14,8},{11,9},{8,1... | collective-permute-start | bytes 3145736 | tf_op jit(solution)/shard_map/n_sb_1/ppermute | solution.py:30
  153.0 24.7 %collective-permute-start.29 = (f32[4,2,128,256]{3,2,1,0:T(8,128)S(1)}, f32[4,2,128,256]{3,2,1,0:T(8,128)S(1)}, u32[]{:S(2)}, u32[]{:S(2)}) collective-permute-start(f32[4,2,128,256]{3,2,1,0:T(8,128)S(1)} %get-tuple-element.42), channel_id=1, source_target_pairs={{2,0},{7,1},{4,2},{1,3},{6,4},{3,5},{0,6},{5,7},{10,8},{15,9},{12,... | collective-permute-start | bytes 3145736 | tf_op jit(solution)/shard_map/n_sa_1/ppermute | solution.py:30
  155.1 26.1 %collective-permute-start.26 = (f32[4,2,128,256]{3,2,1,0:T(8,128)S(1)}, f32[4,2,128,256]{3,2,1,0:T(8,128)S(1)}, u32[]{:S(2)}, u32[]{:S(2)}) collective-permute-start(f32[4,2,128,256]{3,2,1,0:T(8,128)S(1)} %collective-permute-done.21.refs_2_), channel_id=1, source_target_pairs={{24,0},{25,1},{26,2},{27,3},{12,4},{13,5},{14,6},{15,7},{0,8},{1,9... | collective-permute-start | bytes 3145736 | tf_op jit(solution)/shard_map/n_x2_1/ppermute | solution.py:30
  (8 other events, 40.0 us)

commit v4 on v3

--- a/solution.py
+++ b/solution.py
@@ -10,8 +10,8 @@
 CHUNKS = (4, 4)
 SIDE = 4
 
-ORDER = (('own', 0), ('q0', 0), ('w', 0), ('own', 1), ('qa', 0), ('qb', 0), ('rc', 0), ('q0x', 0), ('tiles', 0), ('q2', 0), ('q0', 1), ('w', 1), ('qax', 0), ('qbx', 0), ('tiles', 1), ('sa', 0), ('sb', 0), ('rcx', 0), ('q2x', 0), ('tiles', 2), ('qa', 1), ('q0x', 1), ('qb', 1), ('tiles', 3), ('x2', 0), ('rc', 1), ('q2', 1), ('sax', 0), ('sbx', 0), ('tiles', 4), ('x2x', 0), ('qax', 1), ('qbx', 1), ('sa', 1), ('sb', 1), ('rcx', 1), ('x2', 1), ('q2x', 1), ('tiles', 5), ('tiles', 6), ('tiles', 7), ('sax', 1), ('sbx', 1), ('tiles', 8), ('x2x', 1), ('tiles', 9))
-LATER = {('own', 1): (('own', 0),), ('qa', 0): (('own', 1),), ('qb', 0): (('own', 1),), ('q2', 0): (('tiles', 0),), ('q0', 1): (('rc', 0), ('tiles', 0)), ('w', 1): (('tiles', 0),), ('sb', 0): (('q2', 0), ('tiles', 1), ('w', 1)), ('qa', 1): (('tiles', 2), ('w', 1)), ('x2', 0): (('q0', 1), ('tiles', 3)), ('qb', 1): (('sa', 0), ('tiles', 2)), ('q2', 1): (('tiles', 3),), ('x2x', 0): (('tiles', 4),), ('sb', 1): (('q2', 1), ('tiles', 4)), ('x2', 1): (('tiles', 4),), ('sax', 1): (('tiles', 7),), ('sbx', 1): (('tiles', 7),)}
+ORDER = (('own', 0), ('q0', 0), ('w', 0), ('own', 1), ('qa', 0), ('qb', 0), ('rc', 0), ('q0x', 0), ('tiles', 0), ('q2', 0), ('q0', 1), ('w', 1), ('qax', 0), ('qbx', 0), ('tiles', 1), ('sa', 0), ('sb', 0), ('rcx', 0), ('q2x', 0), ('tiles', 2), ('qa', 1), ('q0x', 1), ('qb', 1), ('tiles', 3), ('rc', 1), ('q2', 1), ('sax', 0), ('x2', 0), ('sbx', 0), ('tiles', 4), ('x2x', 0), ('qax', 1), ('qbx', 1), ('sa', 1), ('sb', 1), ('rcx', 1), ('x2', 1), ('q2x', 1), ('tiles', 5), ('tiles', 6), ('tiles', 7), ('sax', 1), ('sbx', 1), ('tiles', 8), ('x2x', 1), ('tiles', 9))
+LATER = {('own', 1): (('own', 0),), ('qa', 0): (('own', 1),), ('qb', 0): (('own', 1),), ('q2', 0): (('tiles', 0),), ('q0', 1): (('rc', 0), ('tiles', 0)), ('w', 1): (('tiles', 0),), ('sb', 0): (('q2', 0), ('tiles', 1), ('w', 1)), ('qa', 1): (('tiles', 2), ('w', 1)), ('x2', 0): (('q0', 1), ('tiles', 3), ('sax', 0)), ('qb', 1): (('sa', 0), ('tiles', 2)), ('q2', 1): (('tiles', 3),), ('x2x', 0): (('tiles', 4),), ('sb', 1): (('q2', 1), ('tiles', 4)), ('x2', 1): (('tiles', 4),), ('sax', 1): (('tiles', 7),), ('sbx', 1): (('tiles', 7),)}
 KERNELS = ((0, ('q0', 'own')), (0, ('qa', 'qb')), (0, ('rc', 'q2')), (1, ('q0', 'own')), (0, ('sa', 'sb')), (0, ('x2',)), (1, ('qa', 'qb')), (1, ('rc', 'q2')), (1, ('sa', 'sb')), (1, ('x2',)))
 
 

time: 193 us -> 193 us (level)
  starting transfers between devices: 45.9 us -> 48.2 us
    ppermute x6, waiting for transfers between devices: 22.3 us -> 9.53 us  [corner_turn(): pieces.append(lax.ppermute(after(piece(shift), *earlier), 'freq', pairs))]
    ppermute x34, waiting for transfers between devices: 73.1 us -> 83.9 us  [fetch(): return lax.ppermute(value, 'blk', pairs)]
    ppermute x34, starting transfers between devices: 35.9 us -> 38.2 us  [fetch(): return lax.ppermute(value, 'blk', pairs)]
  transfers between devices with their start and end apart: 40 -> 40, of which waited for: 18 -> 16; matrix products, arithmetic and copies ran while one was open for 1% -> 1% of each run, Pallas kernels for 22% -> 22%
where the time goes in v4:
time: 193 us; the launch traced here: 190 us
  waiting for transfers between devices  93.5 us (48%)
  starting transfers between devices  48.2 us (25%)
  Pallas kernels  44.6 us (23%)
  local copies, waits for them, and re-layouts  2.4 us (1%)
    ppermute x34, waiting for transfers between devices, fetch(): return lax.ppermute(value, 'blk', pairs)  83.9 us
    pallas_call x10, Pallas kernels, correlate(): pl.pallas_call(functools.partial(tiles_kernel, slots, first), in_specs=[p...  41.7 us
    ppermute x34, starting transfers between devices, fetch(): return lax.ppermute(value, 'blk', pairs)  38.2 us
    ppermute x6, starting transfers between devices, corner_turn(): pieces.append(lax.ppermute(after(piece(shift), *earlier), 'freq', pairs))  9.97 us
    ppermute x6, waiting for transfers between devices, corner_turn(): pieces.append(lax.ppermute(after(piece(shift), *earlier), 'freq', pairs))  9.53 us
  transfers between devices with their start and end apart: 40, of which 16 were waited for; matrix products, arithmetic and copies ran while one was open for 1% of the time, Pallas kernels for 22%

profile of v4, /device:TPU:0, one launch (start us, length us, event | category | flops | bytes accessed | tf_op | source)
XLA Modules:
  0.0 189.9 jit_solution(5621722923776817753)
XLA Ops:
  3.4 2.9 %collective-permute-start.1 = (f32[4,2,32,256]{3,2,1,0:T(8,128)S(1)}, f32[4,2,32,256]{3,2,1,0:T(8,128)S(1)}, u32[]{:S(2)}, u32[]{:S(2)}) collective-permute-start(f32[4,2,32,256]{3,2,1,0:T(8,128)S(1)} %get-tuple-element.53), channel_id=1, source_target_pairs={{0,64},{32,96},{64,0},{96,32},{1,65},{33,97},{65,1},{97,33},{2,66}... | collective-permute-start | bytes 786440 | tf_op jit(solution)/shard_map/n_own_0/ppermute | solution.py:266
  8.4 2.7 %collective-permute-done.refs_1_ = f32[4,2,32,256]{3,2,1,0:T(8,128)S(1)} collective-permute-done((f32[4,2,32,256]{3,2,1,0:T(8,128)S(1)}, f32[4,2,32,256]{3,2,1,0:T(8,128)S(1)}, u32[]{:S(2)}, u32[]{:S(2)}) %collective-permute-start) | collective-permute-done | bytes 262176 | tf_op jit(solution)/shard_map/n_own_0/ppermute | solution.py:266
  11.1 6.8 %collective-permute-done.1.refs_2_ = f32[4,2,32,256]{3,2,1,0:T(8,128)S(1)} collective-permute-done((f32[4,2,32,256]{3,2,1,0:T(8,128)S(1)}, f32[4,2,32,256]{3,2,1,0:T(8,128)S(1)}, u32[]{:S(2)}, u32[]{:S(2)}) %collective-permute-start.1) | collective-permute-done | bytes 262176 | tf_op jit(solution)/shard_map/n_own_0/ppermute | solution.py:266
  18.1 2.8 %collective-permute-start.7 = (f32[4,2,128,256]{3,2,1,0:T(8,128)S(1)}, f32[4,2,128,256]{3,2,1,0:T(8,128)S(1)}, u32[]{:S(2)}, u32[]{:S(2)}) collective-permute-start(f32[4,2,128,256]{3,2,1,0:T(8,128)S(1)} %rows.2.own_ref.first_ref), channel_id=1, source_target_pairs={{8,0},{9,1},{10,2},{11,3},{12,4},{13,5},{14,6},{15,7},{16,8},{17,9... | collective-permute-start | bytes 3145736 | tf_op jit(solution)/shard_map/n_q0_0/ppermute | solution.py:30
  20.9 2.2 %collective-permute-start.5 = (f32[4,2,32,256]{3,2,1,0:T(8,128)S(1)}, f32[4,2,32,256]{3,2,1,0:T(8,128)S(1)}, u32[]{:S(2)}, u32[]{:S(2)}) collective-permute-start(f32[4,2,32,256]{3,2,1,0:T(8,128)S(1)} %get-tuple-element.30), channel_id=1, source_target_pairs={{0,96},{32,0},{64,32},{96,64},{1,97},{33,1},{65,33},{97,65},{2,98}... | collective-permute-start | bytes 786440 | tf_op jit(solution)/shard_map/n_own_1/ppermute | solution.py:266
  25.6 16.8 %collective-permute-done.7.second_ref.refs_0_ = f32[4,2,128,256]{3,2,1,0:T(8,128)S(1)} collective-permute-done((f32[4,2,128,256]{3,2,1,0:T(8,128)S(1)}, f32[4,2,128,256]{3,2,1,0:T(8,128)S(1)}, u32[]{:S(2)}, u32[]{:S(2)}) %collective-permute-start.7) | collective-permute-done | bytes 1048608 | tf_op jit(solution)/shard_map/n_q0_0/ppermute | solution.py:30
  42.6 4.1 %collective-permute-start.12 = (f32[4,2,128,256]{3,2,1,0:T(8,128)S(1)}, f32[4,2,128,256]{3,2,1,0:T(8,128)S(1)}, u32[]{:S(2)}, u32[]{:S(2)}) collective-permute-start(f32[4,2,128,256]{3,2,1,0:T(8,128)S(1)} %collective-permute-done.7.second_ref.refs_0_), channel_id=1, source_target_pairs={{2,0},{7,1},{4,2},{1,3},{6,4},{3,5},{0,6},{5,7},{10,8},{15,9},{12,... | collective-permute-start | bytes 3145736 | tf_op jit(solution)/shard_map/n_qa_0/ppermute | solution.py:30
  48.1 3.8 %collective-permute-start.8 = (f32[4,2,128,256]{3,2,1,0:T(8,128)S(1)}, f32[4,2,128,256]{3,2,1,0:T(8,128)S(1)}, u32[]{:S(2)}, u32[]{:S(2)}) collective-permute-start(f32[4,2,128,256]{3,2,1,0:T(8,128)S(1)} %pick_0.1), channel_id=1, source_target_pairs={{8,0},{9,1},{10,2},{11,3},{28,4},{29,5},{30,6},{31,7},{16,8},{17,9... | collective-permute-start | bytes 3145736 | tf_op jit(solution)/shard_map/n_rc_0/ppermute | solution.py:30
  51.8 3.8 %tiles_k0.1.refs_4_ = f32[17,8,2,128,128]{4,3,2,1,0:T(8,128)} custom-call(s32[18]{0:T(128)S(1)} %pad_add_fusion.info, f32[4,2,128,256]{3,2,1,0:T(8,128)S(1)} %rows.2.own_ref.first_ref, f32[4,2,128,256]{3,2,1,0:T(8,128)S(1)} %collective-permute-done.7.second_ref.refs_0_, f32[4,2,128,256]{3,2,1,0:T(8,128)S(1)} %collective-permute-done.9.refs_1_), custom_call_target="tpu_custom_call" | custom-call | flops 1207959552 | bytes 4718592 | tf_op jit(solution)/shard_map/n_tiles_0/tiles_k0/pallas_call | solution.py:138
  55.6 14.2 %collective-permute-done.12.refs_0_ = f32[4,2,128,256]{3,2,1,0:T(8,128)S(1)} collective-permute-done((f32[4,2,128,256]{3,2,1,0:T(8,128)S(1)}, f32[4,2,128,256]{3,2,1,0:T(8,128)S(1)}, u32[]{:S(2)}, u32[]{:S(2)}) %collective-permute-start.12) | collective-permute-done | bytes 1048608 | tf_op jit(solution)/shard_map/n_qa_0/ppermute | solution.py:30
  69.9 3.7 %collective-permute-start.13 = (f32[4,2,128,256]{3,2,1,0:T(8,128)S(1)}, f32[4,2,128,256]{3,2,1,0:T(8,128)S(1)}, u32[]{:S(2)}, u32[]{:S(2)}) collective-permute-start(f32[4,2,128,256]{3,2,1,0:T(8,128)S(1)} %collective-permute-done.12.refs_0_), channel_id=1, source_target_pairs={{2,0},{7,1},{4,2},{1,3},{6,4},{3,5},{0,6},{5,7},{10,8},{15,9},{12,... | collective-permute-start | bytes 3145736 | tf_op jit(solution)/shard_map/n_q2_0/ppermute | solution.py:30
  74.8 3.8 %collective-permute-start.10 = (f32[4,2,128,256]{3,2,1,0:T(8,128)S(1)}, f32[4,2,128,256]{3,2,1,0:T(8,128)S(1)}, u32[]{:S(2)}, u32[]{:S(2)}) collective-permute-start(f32[4,2,128,256]{3,2,1,0:T(8,128)S(1)} %rows.3.own_ref.first_ref), channel_id=1, source_target_pairs={{8,0},{9,1},{10,2},{11,3},{12,4},{13,5},{14,6},{15,7},{16,8},{17,9... | collective-permute-start | bytes 3145736 | tf_op jit(solution)/shard_map/n_q0_1/ppermute | solution.py:30
  79.3 6.5 %collective-permute-done.13.refs_2_ = f32[4,2,128,256]{3,2,1,0:T(8,128)S(1)} collective-permute-done((f32[4,2,128,256]{3,2,1,0:T(8,128)S(1)}, f32[4,2,128,256]{3,2,1,0:T(8,128)S(1)}, u32[]{:S(2)}, u32[]{:S(2)}) %collective-permute-start.13) | collective-permute-done | bytes 1048608 | tf_op jit(solution)/shard_map/n_q2_0/ppermute | solution.py:30
  85.9 3.7 %collective-permute-start.22 = (f32[4,2,128,256]{3,2,1,0:T(8,128)S(1)}, f32[4,2,128,256]{3,2,1,0:T(8,128)S(1)}, u32[]{:S(2)}, u32[]{:S(2)}) collective-permute-start(f32[4,2,128,256]{3,2,1,0:T(8,128)S(1)} %get-tuple-element.38), channel_id=1, source_target_pairs={{2,0},{7,1},{4,2},{1,3},{6,4},{3,5},{0,6},{5,7},{10,8},{15,9},{12,... | collective-permute-start | bytes 3145736 | tf_op jit(solution)/shard_map/n_sa_0/ppermute | solution.py:30
  90.1 4.5 %tiles_k1.1.refs_4_ = f32[17,8,2,128,128]{4,3,2,1,0:T(8,128)} custom-call(s32[18]{0:T(128)S(1)} %pad_add_fusion.info, f32[4,2,128,256]{3,2,1,0:T(8,128)S(1)} %rows.2.own_ref.first_ref, f32[4,2,128,256]{3,2,1,0:T(8,128)S(1)} %collective-permute-done.12.refs_0_, ...), custom_call_target="tpu_custom_call", output_to_operand_aliasing={{}: (6, {})} | custom-call | flops 1610612736 | bytes 7340032 | tf_op jit(solution)/shard_map/n_tiles_1/tiles_k1/pallas_call | solution.py:138
  94.7 6.4 %collective-permute-done.10.refs_0_.second_ref = f32[4,2,128,256]{3,2,1,0:T(8,128)S(1)} collective-permute-done((f32[4,2,128,256]{3,2,1,0:T(8,128)S(1)}, f32[4,2,128,256]{3,2,1,0:T(8,128)S(1)}, u32[]{:S(2)}, u32[]{:S(2)}) %collective-permute-start.10) | collective-permute-done | bytes 1048608 | tf_op jit(solution)/shard_map/n_q0_1/ppermute | solution.py:30
  103.9 4.5 %tiles_k2.1.refs_2_ = f32[17,8,2,128,128]{4,3,2,1,0:T(8,128)} custom-call(s32[18]{0:T(128)S(1)} %pad_add_fusion.info, f32[4,2,128,256]{3,2,1,0:T(8,128)S(1)} %rows.2.own_ref.first_ref, f32[4,2,128,256]{3,2,1,0:T(8,128)S(1)} %collective-permute-done.8.second_ref.refs_0_, ...), custom_call_target="tpu_custom_call", output_to_operand_aliasing={{}: (6, {})} | custom-call | flops 1610612736 | bytes 7340032 | tf_op jit(solution)/shard_map/n_tiles_2/tiles_k2/pallas_call | solution.py:138
  108.4 1.8 collective-permute-start.19
  110.2 8.6 %collective-permute-done.24.refs_2_ = f32[4,2,128,256]{3,2,1,0:T(8,128)S(1)} collective-permute-done((f32[4,2,128,256]{3,2,1,0:T(8,128)S(1)}, f32[4,2,128,256]{3,2,1,0:T(8,128)S(1)}, u32[]{:S(2)}, u32[]{:S(2)}) %collective-permute-start.24) | collective-permute-done | bytes 1048608 | tf_op jit(solution)/shard_map/n_sb_0/ppermute | solution.py:30
  118.8 3.8 %tiles_k3.1.refs_4_ = f32[17,8,2,128,128]{4,3,2,1,0:T(8,128)} custom-call(s32[18]{0:T(128)S(1)} %pad_add_fusion.info, f32[4,2,128,256]{3,2,1,0:T(8,128)S(1)} %rows.3.own_ref.first_ref, f32[4,2,128,256]{3,2,1,0:T(8,128)S(1)} %collective-permute-done.10.refs_0_.second_ref, ...), custom_call_target="tpu_custom_call", output_to_operand_aliasing={{}: (4, {})} | custom-call | flops 1207959552 | bytes 4718592 | tf_op jit(solution)/shard_map/n_tiles_3/tiles_k3/pallas_call | solution.py:138
  123.7 3.0 %collective-permute-start.28 = (f32[4,2,128,256]{3,2,1,0:T(8,128)S(1)}, f32[4,2,128,256]{3,2,1,0:T(8,128)S(1)}, u32[]{:S(2)}, u32[]{:S(2)}) collective-permute-start(f32[4,2,128,256]{3,2,1,0:T(8,128)S(1)} %pick_1.1), channel_id=1, source_target_pairs={{8,0},{9,1},{10,2},{11,3},{28,4},{29,5},{30,6},{31,7},{16,8},{17,9... | collective-permute-start | bytes 3145736 | tf_op jit(solution)/shard_map/n_rc_1/ppermute | solution.py:30
  126.7 2.2 %collective-permute-start.21 = (f32[4,2,128,256]{3,2,1,0:T(8,128)S(1)}, f32[4,2,128,256]{3,2,1,0:T(8,128)S(1)}, u32[]{:S(2)}, u32[]{:S(2)}) collective-permute-start(f32[4,2,128,256]{3,2,1,0:T(8,128)S(1)} %collective-permute-done.19.refs_0_), channel_id=1, source_target_pairs={{2,0},{7,1},{4,2},{1,3},{6,4},{3,5},{0,6},{5,7},{10,8},{15,9},{12,... | collective-permute-start | bytes 3145736 | tf_op jit(solution)/shard_map/n_q2_1/ppermute | solution.py:30
  129.0 4.5 %tiles_k4.1.refs_2_ = f32[17,8,2,128,128]{4,3,2,1,0:T(8,128)} custom-call(s32[18]{0:T(128)S(1)} %pad_add_fusion.info, f32[4,2,128,256]{3,2,1,0:T(8,128)S(1)} %rows.2.own_ref.first_ref, f32[4,2,128,256]{3,2,1,0:T(8,128)S(1)} %collective-permute-done.22.refs_0_, ...), custom_call_target="tpu_custom_call", output_to_operand_aliasing={{}: (6, {})} | custom-call | flops 1610612736 | bytes 7340032 | tf_op jit(solution)/shard_map/n_tiles_4/tiles_k4/pallas_call | solution.py:138
  133.5 15.9 %collective-permute-done.35.refs_0_ = f32[4,2,128,256]{3,2,1,0:T(8,128)S(1)} collective-permute-done((f32[4,2,128,256]{3,2,1,0:T(8,128)S(1)}, f32[4,2,128,256]{3,2,1,0:T(8,128)S(1)}, u32[]{:S(2)}, u32[]{:S(2)}) %collective-permute-start.35) | collective-permute-done | bytes 1048608 | tf_op jit(solution)/shard_map/n_x2_0/ppermute | solution.py:30
  153.6 2.4 %collective-permute-start.29 = (f32[4,2,128,256]{3,2,1,0:T(8,128)S(1)}, f32[4,2,128,256]{3,2,1,0:T(8,128)S(1)}, u32[]{:S(2)}, u32[]{:S(2)}) collective-permute-start(f32[4,2,128,256]{3,2,1,0:T(8,128)S(1)} %get-tuple-element.42), channel_id=1, source_target_pairs={{2,0},{7,1},{4,2},{1,3},{6,4},{3,5},{0,6},{5,7},{10,8},{15,9},{12,... | collective-permute-start | bytes 3145736 | tf_op jit(solution)/shard_map/n_sa_1/ppermute | solution.py:30
  156.0 3.4 %tiles_k5.1.refs_4_ = f32[17,8,2,128,128]{4,3,2,1,0:T(8,128)} custom-call(s32[18]{0:T(128)S(1)} %pad_add_fusion.info, f32[4,2,128,256]{3,2,1,0:T(8,128)S(1)} %rows.2.own_ref.first_ref, f32[4,2,128,256]{3,2,1,0:T(8,128)S(1)} %collective-permute-done.35.refs_0_, ...), custom_call_target="tpu_custom_call", output_to_operand_aliasing={{}: (4, {})} | custom-call | flops 805306368 | bytes 4194304 | tf_op jit(solution)/shard_map/n_tiles_5/tiles_k5/pallas_call | solution.py:138
  159.4 4.5 %tiles_k6.1.refs_4_ = f32[17,8,2,128,128]{4,3,2,1,0:T(8,128)} custom-call(s32[18]{0:T(128)S(1)} %pad_add_fusion.info, f32[4,2,128,256]{3,2,1,0:T(8,128)S(1)} %rows.3.own_ref.first_ref, f32[4,2,128,256]{3,2,1,0:T(8,128)S(1)} %collective-permute-done.19.refs_0_, ...), custom_call_target="tpu_custom_call", output_to_operand_aliasing={{}: (6, {})} | custom-call | flops 1610612736 | bytes 7340032 | tf_op jit(solution)/shard_map/n_tiles_6/tiles_k6/pallas_call | solution.py:138
  163.9 4.5 %tiles_k7.1.refs_4_ = f32[17,8,2,128,128]{4,3,2,1,0:T(8,128)} custom-call(s32[18]{0:T(128)S(1)} %pad_add_fusion.info, f32[4,2,128,256]{3,2,1,0:T(8,128)S(1)} %rows.3.own_ref.first_ref, f32[4,2,128,256]{3,2,1,0:T(8,128)S(1)} %collective-permute-done.28.second_ref.refs_0_, ...), custom_call_target="tpu_custom_call", output_to_operand_aliasing={{}: (6, {})} | custom-call | flops 1610612736 | bytes 7340032 | tf_op jit(solution)/shard_map/n_tiles_7/tiles_k7/pallas_call | solution.py:138
  168.5 8.7 %collective-permute-done.38.refs_2_ = f32[4,2,128,256]{3,2,1,0:T(8,128)S(1)} collective-permute-done((f32[4,2,128,256]{3,2,1,0:T(8,128)S(1)}, f32[4,2,128,256]{3,2,1,0:T(8,128)S(1)}, u32[]{:S(2)}, u32[]{:S(2)}) %collective-permute-start.38) | collective-permute-done | bytes 1048608 | tf_op jit(solution)/shard_map/n_sb_1/ppermute | solution.py:30
  179.5 2.0 %collective-permute-done.26.refs_0_ = f32[4,2,128,256]{3,2,1,0:T(8,128)S(1)} collective-permute-done((f32[4,2,128,256]{3,2,1,0:T(8,128)S(1)}, f32[4,2,128,256]{3,2,1,0:T(8,128)S(1)}, u32[]{:S(2)}, u32[]{:S(2)}) %collective-permute-start.26) | collective-permute-done | bytes 1048608 | tf_op jit(solution)/shard_map/n_x2_1/ppermute | solution.py:30
  181.8 4.5 %tiles_k8.1.refs_2_ = f32[17,8,2,128,128]{4,3,2,1,0:T(8,128)} custom-call(s32[18]{0:T(128)S(1)} %pad_add_fusion.info, f32[4,2,128,256]{3,2,1,0:T(8,128)S(1)} %rows.3.own_ref.first_ref, f32[4,2,128,256]{3,2,1,0:T(8,128)S(1)} %collective-permute-done.29.refs_0_, ...), custom_call_target="tpu_custom_call", output_to_operand_aliasing={{}: (6, {})} | custom-call | flops 1610612736 | bytes 7340032 | tf_op jit(solution)/shard_map/n_tiles_8/tiles_k8/pallas_call | solution.py:138
  186.3 3.4 %tiles_k9.1 = f32[17,8,2,128,128]{4,3,2,1,0:T(8,128)} custom-call(s32[18]{0:T(128)S(1)} %pad_add_fusion.info, f32[4,2,128,256]{3,2,1,0:T(8,128)S(1)} %rows.3.own_ref.first_ref, f32[4,2,128,256]{3,2,1,0:T(8,128)S(1)} %collective-permute-done.26.refs_0_, f32[4,2,128,256]{3,2,1,0:T(8,128)S(1)} %collective-permute-done.27.refs_1_, ...), custom_call_target="tpu_custom_call", output_to_operand_aliasing={{}: (4, {})} | custom-call | flops 805306368 | bytes 4194304 | tf_op jit(solution)/shard_map/n_tiles_9/tiles_k9/pallas_call | solution.py:138
  (71 shorter events, 22.8 us)
Async XLA Ops:
  3.4 14.5 %collective-permute-start.1 = (f32[4,2,32,256]{3,2,1,0:T(8,128)S(1)}, f32[4,2,32,256]{3,2,1,0:T(8,128)S(1)}, u32[]{:S(2)}, u32[]{:S(2)}) collective-permute-start(f32[4,2,32,256]{3,2,1,0:T(8,128)S(1)} %get-tuple-element.53), channel_id=1, source_target_pairs={{0,64},{32,96},{64,0},{96,32},{1,65},{33,97},{65,1},{97,33},{2,66}... | collective-permute-start | bytes 786440 | tf_op jit(solution)/shard_map/n_own_0/ppermute | solution.py:266
  6.3 11.6 %collective-permute-start.2 = (f32[4,2,32,256]{3,2,1,0:T(8,128)S(1)}, f32[4,2,32,256]{3,2,1,0:T(8,128)S(1)}, u32[]{:S(2)}, u32[]{:S(2)}) collective-permute-start(f32[4,2,32,256]{3,2,1,0:T(8,128)S(1)} %get-tuple-element.52), channel_id=1, source_target_pairs={{0,96},{32,0},{64,32},{96,64},{1,97},{33,1},{65,33},{97,65},{2,98}... | collective-permute-start | bytes 786440 | tf_op jit(solution)/shard_map/n_own_0/ppermute | solution.py:266
  18.1 24.4 %collective-permute-start.7 = (f32[4,2,128,256]{3,2,1,0:T(8,128)S(1)}, f32[4,2,128,256]{3,2,1,0:T(8,128)S(1)}, u32[]{:S(2)}, u32[]{:S(2)}) collective-permute-start(f32[4,2,128,256]{3,2,1,0:T(8,128)S(1)} %rows.2.own_ref.first_ref), channel_id=1, source_target_pairs={{8,0},{9,1},{10,2},{11,3},{12,4},{13,5},{14,6},{15,7},{16,8},{17,9... | collective-permute-start | bytes 3145736 | tf_op jit(solution)/shard_map/n_q0_0/ppermute | solution.py:30
  20.9 21.6 %collective-permute-start.5 = (f32[4,2,32,256]{3,2,1,0:T(8,128)S(1)}, f32[4,2,32,256]{3,2,1,0:T(8,128)S(1)}, u32[]{:S(2)}, u32[]{:S(2)}) collective-permute-start(f32[4,2,32,256]{3,2,1,0:T(8,128)S(1)} %get-tuple-element.30), channel_id=1, source_target_pairs={{0,96},{32,0},{64,32},{96,64},{1,97},{33,1},{65,33},{97,65},{2,98}... | collective-permute-start | bytes 786440 | tf_op jit(solution)/shard_map/n_own_1/ppermute | solution.py:266
  23.1 19.4 %collective-permute-start.4 = (f32[4,2,32,256]{3,2,1,0:T(8,128)S(1)}, f32[4,2,32,256]{3,2,1,0:T(8,128)S(1)}, u32[]{:S(2)}, u32[]{:S(2)}) collective-permute-start(f32[4,2,32,256]{3,2,1,0:T(8,128)S(1)} %get-tuple-element.29), channel_id=1, source_target_pairs={{0,64},{32,96},{64,0},{96,32},{1,65},{33,97},{65,1},{97,33},{2,66}... | collective-permute-start | bytes 786440 | tf_op jit(solution)/shard_map/n_own_1/ppermute | solution.py:266
  24.2 18.3 %collective-permute-start.3 = (f32[4,2,32,256]{3,2,1,0:T(8,128)S(1)}, f32[4,2,32,256]{3,2,1,0:T(8,128)S(1)}, u32[]{:S(2)}, u32[]{:S(2)}) collective-permute-start(f32[4,2,32,256]{3,2,1,0:T(8,128)S(1)} %get-tuple-element.28), channel_id=1, source_target_pairs={{0,32},{32,64},{64,96},{96,0},{1,33},{33,65},{65,97},{97,1},{2,34}... | collective-permute-start | bytes 786440 | tf_op jit(solution)/shard_map/n_own_1/ppermute | solution.py:266
  24.9 22.5 %collective-permute-start.6 = (f32[4,2,128,256]{3,2,1,0:T(8,128)S(1)}, f32[4,2,128,256]{3,2,1,0:T(8,128)S(1)}, u32[]{:S(2)}, u32[]{:S(2)}) collective-permute-start(f32[4,2,128,256]{3,2,1,0:T(8,128)S(1)} %rows.2.own_ref.first_ref), channel_id=1, source_target_pairs={{28,4},{29,5},{30,6},{31,7},{4,12},{5,13},{6,14},{7,15},{12,20},{1... | collective-permute-start | bytes 3145736 | tf_op jit(solution)/shard_map/n_w_0/ppermute | solution.py:30
  42.6 27.3 %collective-permute-start.12 = (f32[4,2,128,256]{3,2,1,0:T(8,128)S(1)}, f32[4,2,128,256]{3,2,1,0:T(8,128)S(1)}, u32[]{:S(2)}, u32[]{:S(2)}) collective-permute-start(f32[4,2,128,256]{3,2,1,0:T(8,128)S(1)} %collective-permute-done.7.second_ref.refs_0_), channel_id=1, source_target_pairs={{2,0},{7,1},{4,2},{1,3},{6,4},{3,5},{0,6},{5,7},{10,8},{15,9},{12,... | collective-permute-start | bytes 3145736 | tf_op jit(solution)/shard_map/n_qa_0/ppermute | solution.py:30
  46.7 26.9 %collective-permute-start.16 = (f32[4,2,128,256]{3,2,1,0:T(8,128)S(1)}, f32[4,2,128,256]{3,2,1,0:T(8,128)S(1)}, u32[]{:S(2)}, u32[]{:S(2)}) collective-permute-start(f32[4,2,128,256]{3,2,1,0:T(8,128)S(1)} %collective-permute-done.7.second_ref.refs_0_), channel_id=1, source_target_pairs={{6,0},{3,1},{0,2},{5,3},{2,4},{7,5},{4,6},{1,7},{14,8},{11,9},{8,1... | collective-permute-start | bytes 3145736 | tf_op jit(solution)/shard_map/n_qb_0/ppermute | solution.py:30
  48.1 26.7 %collective-permute-start.8 = (f32[4,2,128,256]{3,2,1,0:T(8,128)S(1)}, f32[4,2,128,256]{3,2,1,0:T(8,128)S(1)}, u32[]{:S(2)}, u32[]{:S(2)}) collective-permute-start(f32[4,2,128,256]{3,2,1,0:T(8,128)S(1)} %pick_0.1), channel_id=1, source_target_pairs={{8,0},{9,1},{10,2},{11,3},{28,4},{29,5},{30,6},{31,7},{16,8},{17,9... | collective-permute-start | bytes 3145736 | tf_op jit(solution)/shard_map/n_rc_0/ppermute | solution.py:30
  69.9 16.0 %collective-permute-start.13 = (f32[4,2,128,256]{3,2,1,0:T(8,128)S(1)}, f32[4,2,128,256]{3,2,1,0:T(8,128)S(1)}, u32[]{:S(2)}, u32[]{:S(2)}) collective-permute-start(f32[4,2,128,256]{3,2,1,0:T(8,128)S(1)} %collective-permute-done.12.refs_0_), channel_id=1, source_target_pairs={{2,0},{7,1},{4,2},{1,3},{6,4},{3,5},{0,6},{5,7},{10,8},{15,9},{12,... | collective-permute-start | bytes 3145736 | tf_op jit(solution)/shard_map/n_q2_0/ppermute | solution.py:30
  73.5 16.0 %collective-permute-start.15 = (f32[4,2,128,256]{3,2,1,0:T(8,128)S(1)}, f32[4,2,128,256]{3,2,1,0:T(8,128)S(1)}, u32[]{:S(2)}, u32[]{:S(2)}) collective-permute-start(f32[4,2,128,256]{3,2,1,0:T(8,128)S(1)} %collective-permute-done.12.refs_0_), channel_id=1, source_target_pairs={{1,0},{0,1},{3,2},{2,3},{5,4},{4,5},{7,6},{6,7},{9,8},{8,9},{11,10... | collective-permute-start | bytes 3145736 | tf_op jit(solution)/shard_map/n_qax_0/ppermute | solution.py:30
  73.6 16.0 %collective-permute-start.17 = (f32[4,2,128,256]{3,2,1,0:T(8,128)S(1)}, f32[4,2,128,256]{3,2,1,0:T(8,128)S(1)}, u32[]{:S(2)}, u32[]{:S(2)}) collective-permute-start(f32[4,2,128,256]{3,2,1,0:T(8,128)S(1)} %collective-permute-done.16.refs_2_), channel_id=1, source_target_pairs={{1,0},{0,1},{3,2},{2,3},{5,4},{4,5},{7,6},{6,7},{9,8},{8,9},{11,10... | collective-permute-start | bytes 3145736 | tf_op jit(solution)/shard_map/n_qbx_0/ppermute | solution.py:30
  74.1 20.6 %collective-permute-start.18 = (f32[4,2,128,256]{3,2,1,0:T(8,128)S(1)}, f32[4,2,128,256]{3,2,1,0:T(8,128)S(1)}, u32[]{:S(2)}, u32[]{:S(2)}) collective-permute-start(f32[4,2,128,256]{3,2,1,0:T(8,128)S(1)} %rows.3.own_ref.first_ref), channel_id=1, source_target_pairs={{28,4},{29,5},{30,6},{31,7},{4,12},{5,13},{6,14},{7,15},{12,20},{1... | collective-permute-start | bytes 3145736 | tf_op jit(solution)/shard_map/n_w_1/ppermute | solution.py:30
  74.8 26.3 %collective-permute-start.10 = (f32[4,2,128,256]{3,2,1,0:T(8,128)S(1)}, f32[4,2,128,256]{3,2,1,0:T(8,128)S(1)}, u32[]{:S(2)}, u32[]{:S(2)}) collective-permute-start(f32[4,2,128,256]{3,2,1,0:T(8,128)S(1)} %rows.3.own_ref.first_ref), channel_id=1, source_target_pairs={{8,0},{9,1},{10,2},{11,3},{12,4},{13,5},{14,6},{15,7},{16,8},{17,9... | collective-permute-start | bytes 3145736 | tf_op jit(solution)/shard_map/n_q0_1/ppermute | solution.py:30
  85.9 18.0 %collective-permute-start.22 = (f32[4,2,128,256]{3,2,1,0:T(8,128)S(1)}, f32[4,2,128,256]{3,2,1,0:T(8,128)S(1)}, u32[]{:S(2)}, u32[]{:S(2)}) collective-permute-start(f32[4,2,128,256]{3,2,1,0:T(8,128)S(1)} %get-tuple-element.38), channel_id=1, source_target_pairs={{2,0},{7,1},{4,2},{1,3},{6,4},{3,5},{0,6},{5,7},{10,8},{15,9},{12,... | collective-permute-start | bytes 3145736 | tf_op jit(solution)/shard_map/n_sa_0/ppermute | solution.py:30
  89.6 14.3 %collective-permute-start.11 = (f32[4,2,128,256]{3,2,1,0:T(8,128)S(1)}, f32[4,2,128,256]{3,2,1,0:T(8,128)S(1)}, u32[]{:S(2)}, u32[]{:S(2)}) collective-permute-start(f32[4,2,128,256]{3,2,1,0:T(8,128)S(1)} %get-tuple-element.32), channel_id=1, source_target_pairs={{1,0},{0,1},{3,2},{2,3},{5,4},{4,5},{7,6},{6,7},{9,8},{8,9},{11,10... | collective-permute-start | bytes 3145736 | tf_op jit(solution)/shard_map/n_rcx_0/ppermute | solution.py:30
  89.6 14.3 %collective-permute-start.14 = (f32[4,2,128,256]{3,2,1,0:T(8,128)S(1)}, f32[4,2,128,256]{3,2,1,0:T(8,128)S(1)}, u32[]{:S(2)}, u32[]{:S(2)}) collective-permute-start(f32[4,2,128,256]{3,2,1,0:T(8,128)S(1)} %collective-permute-done.13.refs_2_), channel_id=1, source_target_pairs={{1,0},{0,1},{3,2},{2,3},{5,4},{4,5},{7,6},{6,7},{9,8},{8,9},{11,10... | collective-permute-start | bytes 3145736 | tf_op jit(solution)/shard_map/n_q2x_0/ppermute | solution.py:30
  94.6 24.1 %collective-permute-start.24 = (f32[4,2,128,256]{3,2,1,0:T(8,128)S(1)}, f32[4,2,128,256]{3,2,1,0:T(8,128)S(1)}, u32[]{:S(2)}, u32[]{:S(2)}) collective-permute-start(f32[4,2,128,256]{3,2,1,0:T(8,128)S(1)} %get-tuple-element.40), channel_id=1, source_target_pairs={{6,0},{3,1},{0,2},{5,3},{2,4},{7,5},{4,6},{1,7},{14,8},{11,9},{8,1... | collective-permute-start | bytes 3145736 | tf_op jit(solution)/shard_map/n_sb_0/ppermute | solution.py:30
  101.1 17.6 %collective-permute-start.20 = (f32[4,2,128,256]{3,2,1,0:T(8,128)S(1)}, f32[4,2,128,256]{3,2,1,0:T(8,128)S(1)}, u32[]{:S(2)}, u32[]{:S(2)}) collective-permute-start(f32[4,2,128,256]{3,2,1,0:T(8,128)S(1)} %collective-permute-done.10.refs_0_.second_ref), channel_id=1, source_target_pairs={{1,0},{0,1},{3,2},{2,3},{5,4},{4,5},{7,6},{6,7},{9,8},{8,9},{11,10... | collective-permute-start | bytes 3145736 | tf_op jit(solution)/shard_map/n_q0x_1/ppermute | solution.py:30
  103.9 18.7 %collective-permute-start.23 = (f32[4,2,128,256]{3,2,1,0:T(8,128)S(1)}, f32[4,2,128,256]{3,2,1,0:T(8,128)S(1)}, u32[]{:S(2)}, u32[]{:S(2)}) collective-permute-start(f32[4,2,128,256]{3,2,1,0:T(8,128)S(1)} %collective-permute-done.22.refs_0_), channel_id=1, source_target_pairs={{1,0},{0,1},{3,2},{2,3},{5,4},{4,5},{7,6},{6,7},{9,8},{8,9},{11,10... | collective-permute-start | bytes 3145736 | tf_op jit(solution)/shard_map/n_sax_0/ppermute | solution.py:30
  108.4 18.3 %collective-permute-start.19 = (f32[4,2,128,256]{3,2,1,0:T(8,128)S(1)}, f32[4,2,128,256]{3,2,1,0:T(8,128)S(1)}, u32[]{:S(2)}, u32[]{:S(2)}) collective-permute-start(f32[4,2,128,256]{3,2,1,0:T(8,128)S(1)} %collective-permute-done.10.refs_0_.second_ref), channel_id=1, source_target_pairs={{2,0},{7,1},{4,2},{1,3},{6,4},{3,5},{0,6},{5,7},{10,8},{15,9},{12,... | collective-permute-start | bytes 3145736 | tf_op jit(solution)/shard_map/n_qa_1/ppermute | solution.py:30
  118.8 10.2 %collective-permute-start.25 = (f32[4,2,128,256]{3,2,1,0:T(8,128)S(1)}, f32[4,2,128,256]{3,2,1,0:T(8,128)S(1)}, u32[]{:S(2)}, u32[]{:S(2)}) collective-permute-start(f32[4,2,128,256]{3,2,1,0:T(8,128)S(1)} %collective-permute-done.24.refs_2_), channel_id=1, source_target_pairs={{1,0},{0,1},{3,2},{2,3},{5,4},{4,5},{7,6},{6,7},{9,8},{8,9},{11,10... | collective-permute-start | bytes 3145736 | tf_op jit(solution)/shard_map/n_sbx_0/ppermute | solution.py:30
  122.6 26.9 %collective-permute-start.35 = (f32[4,2,128,256]{3,2,1,0:T(8,128)S(1)}, f32[4,2,128,256]{3,2,1,0:T(8,128)S(1)}, u32[]{:S(2)}, u32[]{:S(2)}) collective-permute-start(f32[4,2,128,256]{3,2,1,0:T(8,128)S(1)} %collective-permute-done.13.refs_2_), channel_id=1, source_target_pairs={{24,0},{25,1},{26,2},{27,3},{12,4},{13,5},{14,6},{15,7},{0,8},{1,9... | collective-permute-start | bytes 3145736 | tf_op jit(solution)/shard_map/n_x2_0/ppermute | solution.py:30
  122.7 27.3 %collective-permute-start.33 = (f32[4,2,128,256]{3,2,1,0:T(8,128)S(1)}, f32[4,2,128,256]{3,2,1,0:T(8,128)S(1)}, u32[]{:S(2)}, u32[]{:S(2)}) collective-permute-start(f32[4,2,128,256]{3,2,1,0:T(8,128)S(1)} %collective-permute-done.10.refs_0_.second_ref), channel_id=1, source_target_pairs={{6,0},{3,1},{0,2},{5,3},{2,4},{7,5},{4,6},{1,7},{14,8},{11,9},{8,1... | collective-permute-start | bytes 3145736 | tf_op jit(solution)/shard_map/n_qb_1/ppermute | solution.py:30
  123.7 26.6 %collective-permute-start.28 = (f32[4,2,128,256]{3,2,1,0:T(8,128)S(1)}, f32[4,2,128,256]{3,2,1,0:T(8,128)S(1)}, u32[]{:S(2)}, u32[]{:S(2)}) collective-permute-start(f32[4,2,128,256]{3,2,1,0:T(8,128)S(1)} %pick_1.1), channel_id=1, source_target_pairs={{8,0},{9,1},{10,2},{11,3},{28,4},{29,5},{30,6},{31,7},{16,8},{17,9... | collective-permute-start | bytes 3145736 | tf_op jit(solution)/shard_map/n_rc_1/ppermute | solution.py:30
  126.7 24.6 %collective-permute-start.21 = (f32[4,2,128,256]{3,2,1,0:T(8,128)S(1)}, f32[4,2,128,256]{3,2,1,0:T(8,128)S(1)}, u32[]{:S(2)}, u32[]{:S(2)}) collective-permute-start(f32[4,2,128,256]{3,2,1,0:T(8,128)S(1)} %collective-permute-done.19.refs_0_), channel_id=1, source_target_pairs={{2,0},{7,1},{4,2},{1,3},{6,4},{3,5},{0,6},{5,7},{10,8},{15,9},{12,... | collective-permute-start | bytes 3145736 | tf_op jit(solution)/shard_map/n_q2_1/ppermute | solution.py:30
  151.0 12.9 %collective-permute-start.30 = (f32[4,2,128,256]{3,2,1,0:T(8,128)S(1)}, f32[4,2,128,256]{3,2,1,0:T(8,128)S(1)}, u32[]{:S(2)}, u32[]{:S(2)}) collective-permute-start(f32[4,2,128,256]{3,2,1,0:T(8,128)S(1)} %get-tuple-element.43), channel_id=1, source_target_pairs={{1,0},{0,1},{3,2},{2,3},{5,4},{4,5},{7,6},{6,7},{9,8},{8,9},{11,10... | collective-permute-start | bytes 3145736 | tf_op jit(solution)/shard_map/n_rcx_1/ppermute | solution.py:30
  151.3 12.6 %collective-permute-start.31 = (f32[4,2,128,256]{3,2,1,0:T(8,128)S(1)}, f32[4,2,128,256]{3,2,1,0:T(8,128)S(1)}, u32[]{:S(2)}, u32[]{:S(2)}) collective-permute-start(f32[4,2,128,256]{3,2,1,0:T(8,128)S(1)} %collective-permute-done.21.refs_2_), channel_id=1, source_target_pairs={{1,0},{0,1},{3,2},{2,3},{5,4},{4,5},{7,6},{6,7},{9,8},{8,9},{11,10... | collective-permute-start | bytes 3145736 | tf_op jit(solution)/shard_map/n_q2x_1/ppermute | solution.py:30
  152.1 25.1 %collective-permute-start.38 = (f32[4,2,128,256]{3,2,1,0:T(8,128)S(1)}, f32[4,2,128,256]{3,2,1,0:T(8,128)S(1)}, u32[]{:S(2)}, u32[]{:S(2)}) collective-permute-start(f32[4,2,128,256]{3,2,1,0:T(8,128)S(1)} %get-tuple-element.49), channel_id=1, source_target_pairs={{6,0},{3,1},{0,2},{5,3},{2,4},{7,5},{4,6},{1,7},{14,8},{11,9},{8,1... | collective-permute-start | bytes 3145736 | tf_op jit(solution)/shard_map/n_sb_1/ppermute | solution.py:30
  153.6 24.4 %collective-permute-start.29 = (f32[4,2,128,256]{3,2,1,0:T(8,128)S(1)}, f32[4,2,128,256]{3,2,1,0:T(8,128)S(1)}, u32[]{:S(2)}, u32[]{:S(2)}) collective-permute-start(f32[4,2,128,256]{3,2,1,0:T(8,128)S(1)} %get-tuple-element.42), channel_id=1, source_target_pairs={{2,0},{7,1},{4,2},{1,3},{6,4},{3,5},{0,6},{5,7},{10,8},{15,9},{12,... | collective-permute-start | bytes 3145736 | tf_op jit(solution)/shard_map/n_sa_1/ppermute | solution.py:30
  156.0 25.6 %collective-permute-start.26 = (f32[4,2,128,256]{3,2,1,0:T(8,128)S(1)}, f32[4,2,128,256]{3,2,1,0:T(8,128)S(1)}, u32[]{:S(2)}, u32[]{:S(2)}) collective-permute-start(f32[4,2,128,256]{3,2,1,0:T(8,128)S(1)} %collective-permute-done.21.refs_2_), channel_id=1, source_target_pairs={{24,0},{25,1},{26,2},{27,3},{12,4},{13,5},{14,6},{15,7},{0,8},{1,9... | collective-permute-start | bytes 3145736 | tf_op jit(solution)/shard_map/n_x2_1/ppermute | solution.py:30
  (8 other events, 44.5 us)
